TPU v7x, 32 devices: a whole 2x2x4 slice. The times are simulated.
32 devices in a mesh: groups: 2 (over y), replica: 4 (over z), tensor: 4 (over x, core).
Axes of the slice: x: 2, y: 2, z: 4, core: 2. Of those that a mesh axis runs over, the one named last changes fastest.
Arguments:
- queries: bfloat16 [1024, 2, 4096], P(('groups', 'replica'), None, 'tensor'), parts along dimension 0, may hold values from -8 to 8
- recent_keys: bfloat16 [1024, 2, 1024], P(('groups', 'replica'), None, 'tensor'), parts along dimension 0, may hold values from -12 to 12
- recent_values: bfloat16 [1024, 2, 1024], P(('groups', 'replica'), None, 'tensor'), parts along dimension 0, may hold values from -24 to 24
- prefix_key_value: bfloat16 [8, 2, 4096, 1024], P(('groups', 'replica'), None, None, 'tensor'), parts along dimension 0, may hold values from -6 to 6
- prefix_length_each: int32 [1024], P(('groups', 'replica')), parts along dimension 0, may hold values from 512 to 4096, as said below
- batch_adapter_index: int32 [128], P(('groups', 'replica')), parts along dimension 0, may hold values from 0 to 63, as said below
- adapter_table_row: int32 [128], P('groups'), parts along dimension 0, may hold values from 0 to 63, as said below
- down_weight_table: bfloat16 [64, 16, 4096], P('replica', None, 'tensor'), may hold values from -2 to 2
- up_weight_table: bfloat16 [64, 16, 8192], P('replica', None, 'tensor'), may hold values from -1.5 to 1.5
- output_weight: bfloat16 [4096, 8192], P('tensor'), may hold values from -2 to 2
Outputs:
- block_out: bfloat16 [1024, 2, 8192], P(('groups', 'replica'), None, 'tensor'), parts along dimension 0
There are 2 independent parts, one for each index of `groups`. A program takes and returns all parts, laid end to end along the dimension named above; an argument that names none is the same for every part. Nothing has to cross between parts.
Inputs may be any that keep to these rules, and one draw needn't show every extreme that they name: `prefix_length_each`: the largest length equals 4096 in every draw. adapter_table_row is a permutation of 0 to 63; rows k * 16 to (k + 1) * 16 - 1 of the tables lie on replica k. `batch_adapter_index`: of the 16 fork batches of one replica, at most 8 name adapters whose table rows lie on one replica; every draw reaches 8. An adapter may serve several batches.
All inputs are finite; a program needn't handle non-finite values.
Results may differ from a plain program's by a relative error of at most 0.0095.
Values may be sent and summed in bfloat16 or wider, within the bound.
No kernel may reach another device: no remote copies, remote signals or barrier semaphores. Data moves between devices by JAX's collectives and lax.ppermute only.
A program may use at most 192 MiB of HBM per device.

v0:
```python
import functools
import math

import jax
import jax.numpy as jnp
from jax import lax
from jax.experimental import pallas as pl
from jax.experimental.pallas import tpu as pltpu
from jax.sharding import PartitionSpec as P

HD = 128
NEG = -1e30
LOG2_SCALE = math.log2(math.e) / math.sqrt(HD)
BF16, F32 = jnp.bfloat16, jnp.float32
VMEM = pl.BlockSpec(memory_space=pltpu.VMEM)
SMEM = pl.BlockSpec(memory_space=pltpu.SMEM)
SMALL_PARAMS = pltpu.CompilerParams(vmem_limit_bytes=20 * 1024 * 1024)
PARAMS = pltpu.CompilerParams(vmem_limit_bytes=58 * 1024 * 1024)


def attention_kernel(
    unit_heads, key_block, q_ref, rk_ref, rv_ref, kv_ref, lens_ref, o_ref,
    s_a, s_b, vaug, mx_a, mx_b, mb, acc, lensb, qs,
):
    steps, forks, width = q_ref.shape
    heads = width // HD
    heads_kv = rk_ref.shape[2] // HD
    group = heads // heads_kv
    head_rows = steps * forks
    rows = unit_heads * head_rows
    units = heads // unit_heads
    prefix = kv_ref.shape[2]
    longest = jnp.max(lens_ref[...])
    blocks = (longest + (key_block - 1)) // key_block
    lens = jnp.broadcast_to(lens_ref[...], (head_rows, HD))
    for i in range(unit_heads):
        lensb[i * head_rows : (i + 1) * head_rows, :] = lens
    for v in range(heads_kv):
        vaug[v, :, 0:HD] = kv_ref[0, 1, :, v * HD : (v + 1) * HD]
        vaug[v, :, HD : 2 * HD] = jnp.ones((prefix, HD), BF16)
    for h in range(heads):
        qs[h * head_rows : (h + 1) * head_rows, :] = q_ref[:, :, h * HD : (h + 1) * HD].reshape(head_rows, HD)
    score_refs, max_refs = (s_a, s_b), (mx_a, mx_b)

    def own_scores(u, t):
        parts = []
        for i in range(unit_heads):
            h = u * unit_heads + i
            v = h // group
            k = rk_ref[t, :, v * HD : (v + 1) * HD].astype(F32)
            for s in range(steps):
                if t <= s:
                    at = h * head_rows + s * forks
                    parts.append(jnp.sum(qs[at : at + forks, :].astype(F32) * k, axis=1, keepdims=True))
                else:
                    parts.append(jnp.full((forks, 1), NEG, F32))
        return jnp.concatenate(parts, axis=0)

    def score_block(u, j, s_ref, mx_ref):
        v = (u * unit_heads) // group
        keys = kv_ref[0, 0, pl.ds(pl.multiple_of(j * key_block, key_block), key_block), v * HD : (v + 1) * HD]
        s = lax.dot_general(
            qs[u * rows : (u + 1) * rows, :], keys, (((1,), (1,)), ((), ())), preferred_element_type=F32
        )
        top = mx_ref[...]
        left = lensb[...] - j * key_block
        lane = lax.broadcasted_iota(jnp.int32, (rows, HD), 1)
        for c in range(key_block // HD):
            part = jnp.where(lane + c * HD < left, s[:, c * HD : (c + 1) * HD], NEG)
            top = jnp.maximum(top, part)
            s_ref[j, :, c * HD : (c + 1) * HD] = part
        mx_ref[...] = top

    def value_block(u, j, s_ref):
        v = (u * unit_heads) // group
        top = mb[...]
        parts = [
            jnp.exp2((s_ref[j, :, c * HD : (c + 1) * HD] - top) * LOG2_SCALE).astype(BF16)
            for c in range(key_block // HD)
        ]
        values = vaug[v, pl.ds(pl.multiple_of(j * key_block, key_block), key_block), :]
        acc[...] += jnp.dot(jnp.concatenate(parts, axis=1), values, preferred_element_type=F32)

    for u in range(units + 1):
        done = u - 1
        if u < units:
            max_refs[u % 2][...] = jnp.full((rows, HD), NEG, F32)
        if u > 0:
            own = [own_scores(done, t) for t in range(steps)]
            top = jnp.max(max_refs[done % 2][...], axis=1, keepdims=True)
            for o in own:
                top = jnp.maximum(top, o)
            mb[...] = jnp.broadcast_to(top, (rows, HD))
            acc[...] = jnp.zeros_like(acc)

        @pl.loop(0, blocks)
        def _(j):
            if u < units:
                score_block(u, j, score_refs[u % 2], max_refs[u % 2])
            if u > 0:
                value_block(done, j, score_refs[done % 2])

        if u > 0:
            weights = [jnp.exp2((o - top) * LOG2_SCALE) for o in own]
            total = acc[:, HD : 2 * HD]
            for w in weights:
                total = total + w
            for i in range(unit_heads):
                h = done * unit_heads + i
                v = h // group
                at = slice(i * head_rows, (i + 1) * head_rows)
                mixed = acc[at, 0:HD]
                for t in range(steps):
                    value = rv_ref[t, :, v * HD : (v + 1) * HD].astype(F32)
                    value = jnp.concatenate([value] * steps, axis=0)
                    mixed = mixed + weights[t][at].astype(BF16).astype(F32) * value
                o_ref[:, h * HD : (h + 1) * HD] = (mixed / total[at]).astype(BF16)


def attention(q, rk, rv, kv, lens):
    steps, forks, width = q.shape
    prefix = kv.shape[2]
    heads_kv = rk.shape[2] // HD
    unit_heads = 2
    key_block = prefix
    rows = unit_heads * steps * forks
    return pl.pallas_call(
        functools.partial(attention_kernel, unit_heads, key_block),
        out_shape=jax.ShapeDtypeStruct((steps * forks, width), BF16),
        in_specs=[VMEM] * 5,
        out_specs=VMEM,
        scratch_shapes=[pltpu.VMEM((prefix // key_block, rows, key_block), F32)] * 2
        + [pltpu.VMEM((heads_kv, prefix, 2 * HD), BF16)]
        + [pltpu.VMEM((rows, HD), F32)] * 3
        + [
            pltpu.VMEM((rows, 2 * HD), F32),
            pltpu.VMEM((rows, HD), jnp.int32),
            pltpu.VMEM((width // HD * steps * forks, HD), BF16),
        ],
        compiler_params=PARAMS,
        cost_estimate=pl.CostEstimate(flops=2 * 10**10, bytes_accessed=6 * 2**20, transcendentals=0),
        name="attention",
    )(q, rk, rv, kv, lens)


def project(attended, weight, column_group, width, add, dtype):
    rows, depth = attended.shape
    tile = 1024 if width % 1024 == 0 else width
    tiles = width // tile

    def kernel(group_ref, a_ref, w_ref, *rest):
        o_ref = rest[-1]
        part = jnp.dot(a_ref[...], w_ref[...], preferred_element_type=F32)
        for r in rest[:-1]:
            part = part + r[...].astype(F32)
        o_ref[...] = part.astype(o_ref.dtype)

    in_specs = [
        pl.BlockSpec((rows, depth), lambda i, g: (0, 0)),
        pl.BlockSpec((depth, tile), lambda i, g: (0, g[0] * tiles + i)),
    ]
    operands = [attended, weight]
    in_specs += [pl.BlockSpec((rows, tile), lambda i, g: (0, i))] * len(add)
    operands += add
    return pl.pallas_call(
        kernel,
        out_shape=jax.ShapeDtypeStruct((rows, width), dtype),
        grid_spec=pltpu.PrefetchScalarGridSpec(
            num_scalar_prefetch=1,
            grid=(tiles,),
            in_specs=in_specs,
            out_specs=pl.BlockSpec((rows, tile), lambda i, g: (0, i)),
        ),
        compiler_params=PARAMS,
        cost_estimate=pl.CostEstimate(
            flops=2 * rows * depth * width, bytes_accessed=2 * depth * width, transcendentals=0
        ),
        name="project",
    )(column_group.reshape(1), *operands)


def pack(tables, rows_all, place, capacity):
    replicas, batches = rows_all.shape
    stored, rank, _ = tables[0].shape
    widths = [t.shape[2] for t in tables]

    def kernel(rows_ref, place_ref, *refs):
        out = refs[-1]
        to = pl.program_id(0)

        def step(b, count):
            row = rows_ref[to, b] - place_ref[0] * stored
            mine = (row >= 0) & (row < stored)

            @pl.when(mine)
            def _():
                at = 0
                for ref, width in zip(refs, widths):
                    out[0, count, :, at : at + width] = ref[row]
                    at += width

            return count + mine.astype(jnp.int32)

        lax.fori_loop(0, batches, step, jnp.int32(0))

    return pl.pallas_call(
        kernel,
        out_shape=jax.ShapeDtypeStruct((replicas, capacity, rank, sum(widths)), BF16),
        grid=(replicas,),
        in_specs=[SMEM, SMEM] + [whole(t.shape) for t in tables],
        out_specs=pl.BlockSpec((1, capacity, rank, sum(widths)), lambda i: (i, 0, 0, 0)),
        compiler_params=PARAMS,
        name="pack",
    )(rows_all, place, *tables)


def partner_rows(rows, place, received):
    nearest = received[0]
    batches = rows.shape[0]

    def kernel(rows_ref, place_ref, *refs):
        out = refs[-1]

        @pl.loop(0, batches)
        def _(b):
            pick(rows_ref[b], place_ref, refs[:-1], lambda value: out.__setitem__(b, value))

    return pl.pallas_call(
        kernel,
        out_shape=jax.ShapeDtypeStruct((batches,) + nearest.shape[1:], BF16),
        in_specs=[SMEM, SMEM] + [VMEM] * len(received),
        out_specs=VMEM,
        compiler_params=SMALL_PARAMS,
        name="partner_rows",
    )(rows, place, *received)


def pick(row, place_ref, refs, put):
    stored = refs[0].shape[0]
    me = place_ref[0]
    owner, at = row // stored, lax.rem(row, stored)
    apart = owner ^ me
    middle = (me == 1) | (me == 2)
    for ref, where in zip(
        refs,
        (
            apart == 1,
            middle & (apart == 3),
            middle & (apart == 2),
            jnp.logical_not(middle) & (apart == 2),
            jnp.logical_not(middle) & (apart == 3),
        ),
    ):

        @pl.when(where)
        def _():
            put(ref[at])


def low_rank_of_halves(attended, forks, own_rows, place, table, received, partner):
    rows, depth = attended.shape
    batches = own_rows.shape[0]
    stored, rank, _ = table.shape
    half = depth // 2

    def kernel(rows_ref, place_ref, a_ref, table_ref, *refs):
        partner_ref, o_ref, mine, other = refs[-4:]
        here = pl.multiple_of(place_ref[1] * half, half)
        there = pl.multiple_of((1 - place_ref[1]) * half, half)

        @pl.loop(0, batches)
        def _(b):
            row = rows_ref[b]
            own = row // stored == place_ref[0]
            at = lax.rem(row, stored)

            @pl.when(own)
            def _():
                mine[b] = table_ref[at, :, pl.ds(here, half)]
                other[b] = table_ref[at, :, pl.ds(there, half)]

            @pl.when(jnp.logical_not(own))
            def _():
                other[b] = partner_ref[b]

            pick(row, place_ref, refs[:-4], lambda value: mine.__setitem__(b, value))

        every = jnp.zeros((rows, batches * rank), F32)
        for at, selected in ((here, mine), (there, other)):
            every = every + lax.dot_general(
                a_ref[:, pl.ds(at, half)],
                selected[...].reshape(batches * rank, half),
                (((1,), (1,)), ((), ())),
                preferred_element_type=F32,
            )
        o_ref[...] = fold(every, rows, forks, batches, rank)

    return pl.pallas_call(
        kernel,
        out_shape=jax.ShapeDtypeStruct((rows, HD), F32),
        in_specs=[SMEM, SMEM] + [VMEM] * (3 + len(received)),
        out_specs=VMEM,
        scratch_shapes=[pltpu.VMEM((batches, rank, half), BF16)] * 2,
        compiler_params=SMALL_PARAMS,
        name="low_rank",
    )(own_rows, place, attended, table, *received, partner)


def collect(rows_ref, stored, arrived_ref, selected):
    batches = selected.shape[0]
    for owner in range(arrived_ref.shape[0]):

        def step(b, count):
            row = rows_ref[b] - owner * stored
            there = (row >= 0) & (row < stored)

            @pl.when(there)
            def _():
                selected[b] = arrived_ref[owner, count]

            return count + there.astype(jnp.int32)

        lax.fori_loop(0, batches, step, jnp.int32(0))


def whole(shape):
    return pl.BlockSpec(shape, lambda i: (0,) * len(shape))


def columns(packed, width, block):
    shape = packed.shape[:-1] + (width,)
    return pl.BlockSpec(shape, lambda i: (0,) * (len(shape) - 1) + (block,))


def batch_mask(rows, forks, batches, rank):
    batch_forks = forks // batches
    row = lax.broadcasted_iota(jnp.int32, (rows, batches * rank), 0)
    column = lax.broadcasted_iota(jnp.int32, (rows, batches * rank), 1)
    return lax.rem(row, forks) // batch_forks == column // rank


def fold(every, rows, forks, batches, rank):
    every = jnp.where(batch_mask(rows, forks, batches, rank), every, 0.0)
    total = every[:, 0:HD]
    for c in range(1, batches * rank // HD):
        total = total + every[:, c * HD : (c + 1) * HD]
    return total


def low_rank(attended, forks, own_rows, stored, arrived):
    rows, depth = attended.shape
    batches = own_rows.shape[0]
    rank = arrived.shape[2]

    def kernel(rows_ref, a_ref, arrived_ref, o_ref, selected):
        collect(rows_ref, stored, arrived_ref, selected)
        every = lax.dot_general(
            a_ref[...],
            selected[...].reshape(batches * rank, depth),
            (((1,), (1,)), ((), ())),
            preferred_element_type=F32,
        )
        o_ref[...] = fold(every, rows, forks, batches, rank)

    return pl.pallas_call(
        kernel,
        out_shape=jax.ShapeDtypeStruct((rows, HD), F32),
        grid=(1,),
        in_specs=[SMEM, whole(attended.shape), columns(arrived, depth, (arrived.shape[3] - depth) // depth)],
        out_specs=whole((rows, HD)),
        scratch_shapes=[pltpu.VMEM((batches, rank, depth), BF16)],
        compiler_params=SMALL_PARAMS,
        name="low_rank",
    )(own_rows, attended, arrived)


def finish(base, ranks, forks, own_rows, stored, arrived):
    rows, width = base.shape
    batches = own_rows.shape[0]
    rank = arrived.shape[2]
    tile = min(width, 1024)
    steps = rows // forks

    def kernel(rows_ref, base_ref, *rest):
        rank_refs = rest[:-3]
        arrived_ref, o_ref, selected = rest[-3:]
        collect(rows_ref, stored, arrived_ref, selected)
        total = rank_refs[0][...]
        for r in rank_refs[1:]:
            total = total + r[...]
        spread = jnp.concatenate([total] * (batches * rank // HD), axis=1)
        spread = jnp.where(batch_mask(rows, forks, batches, rank), spread, 0.0)
        high = spread.astype(BF16)
        low = (spread - high.astype(F32)).astype(BF16)
        up = selected[...].reshape(batches * rank, tile)
        out = jnp.dot(high, up, preferred_element_type=F32)
        out = out + jnp.dot(low, up, preferred_element_type=F32)
        out = out + base_ref[...]
        out = out.astype(BF16)
        for s in range(steps):
            o_ref[:, s, :] = out[s * forks : (s + 1) * forks, :]

    by_tile = pl.BlockSpec((rows, tile), lambda i: (0, i))
    return pl.pallas_call(
        kernel,
        out_shape=jax.ShapeDtypeStruct((forks, steps, width), BF16),
        grid=(width // tile,),
        in_specs=[SMEM, by_tile]
        + [whole(r.shape) for r in ranks]
        + [pl.BlockSpec(arrived.shape[:3] + (tile,), lambda i: (0, 0, 0, i))],
        out_specs=pl.BlockSpec((forks, steps, tile), lambda i: (0, 0, i)),
        scratch_shapes=[pltpu.VMEM((batches, rank, tile), BF16)],
        compiler_params=SMALL_PARAMS,
        name="finish",
    )(own_rows, base, *ranks, arrived)


def lookup(wanted, adapter_table_row):
    matches = wanted[..., None] == jnp.arange(adapter_table_row.shape[0], dtype=jnp.int32)
    return jnp.sum(jnp.where(matches, adapter_table_row, 0), axis=-1)


def body(
    groups,
    replicas,
    chips,
    queries,
    recent_keys,
    recent_values,
    prefix_key_value,
    prefix_length_each,
    batch_adapter_index,
    adapter_table_row,
    down_weight_table,
    up_weight_table,
    output_weight,
):
    forks, steps, _ = queries.shape
    batches = batch_adapter_index.shape[0]
    capacity = max(2, 2 * batches // replicas)
    model_width = output_weight.shape[1]
    width = model_width // (2 * chips)
    replica = lax.axis_index("replica").astype(jnp.int32)
    tensor = lax.axis_index("tensor").astype(jnp.int32)
    chip, core = tensor // 2, lax.rem(tensor, 2)
    place = replica.reshape(1)

    own_rows = lookup(batch_adapter_index, adapter_table_row)
    by_halves = replicas == 4 and groups == 2
    stored = down_weight_table.shape[0]
    if by_halves:
        group = lax.axis_index("groups").astype(jnp.int32)
        place = jnp.stack([replica, group])
        half = down_weight_table.shape[2] // 2
        mine = lax.dynamic_slice_in_dim(down_weight_table, group * half, half, axis=2)
        nearest = lax.ppermute(mine, "replica", [(0, 1), (1, 0), (2, 3), (3, 2)])
        middle = lax.ppermute(mine, "replica", [(1, 2), (2, 1)])
        far = lax.ppermute(mine, "replica", [(0, 2), (3, 1)])
        onward = [(1, 0), (2, 3)]
        received = [nearest, middle, far, lax.ppermute(middle, "replica", onward), lax.ppermute(far, "replica", onward)]
        rows_all = lax.all_gather(own_rows, ("groups", "replica"))
        partner_named = lax.dynamic_index_in_dim(rows_all, (1 - group) * replicas + replica, keepdims=False)
        rows_all = lax.dynamic_slice_in_dim(rows_all, group * replicas, replicas, axis=0)
        parts = pack([up_weight_table], rows_all, place, capacity)
    else:
        rows_all = lax.all_gather(own_rows, "replica")
        parts = pack([up_weight_table, down_weight_table], rows_all, place, capacity)
    queries = lax.optimization_barrier((queries, parts))[0]
    arrived = lax.all_to_all(parts, "replica", 0, 0)

    lens = jnp.concatenate([prefix_length_each] * steps)[:, None]
    attended = attention(
        queries.transpose(1, 0, 2),
        recent_keys.transpose(1, 0, 2),
        recent_values.transpose(1, 0, 2),
        prefix_key_value,
        lens,
    )

    if by_halves:
        attended, *received = lax.optimization_barrier((attended, *received))

    swap = [(t, t ^ 1) for t in range(2 * chips)]

    def along(e):
        return [(t, (t + 2 * e) % (2 * chips)) for t in range(2 * chips)]

    order = list(range(1, chips)) + [0]
    starts = [lax.rem(chip + e, chips) * 2 for e in order]
    halves = [
        lax.ppermute(project(attended, output_weight, g + 1 - core, width, [], BF16), "tensor", swap)
        for g in starts
    ]
    sums = []
    for e, g, half in zip(order, starts, halves):
        if e:
            part = project(attended, output_weight, g + core, width, [half], BF16)
            sums.append(lax.ppermute(part, "tensor", along(e)))
        else:
            base = project(attended, output_weight, g + core, width, [half] + sums, F32)

    if by_halves:
        partner = lax.ppermute(partner_rows(partner_named, place, received), "groups", [(0, 1), (1, 0)])
        rank_part = low_rank_of_halves(attended, forks, own_rows, place, down_weight_table, received, partner)
    else:
        rank_part = low_rank(attended, forks, own_rows, stored, arrived)
    ranks = [rank_part] + [
        lax.ppermute(rank_part, "tensor", [(t, t ^ e) for t in range(2 * chips)]) for e in range(1, 2 * chips)
    ]
    return finish(base, ranks, forks, own_rows, stored, arrived)


def solution(mesh):
    placed = (
        P(("groups", "replica"), None, "tensor"),
        P(("groups", "replica"), None, "tensor"),
        P(("groups", "replica"), None, "tensor"),
        P(("groups", "replica"), None, None, "tensor"),
        P(("groups", "replica")),
        P(("groups", "replica")),
        P("groups"),
        P("replica", None, "tensor"),
        P("replica", None, "tensor"),
        P("tensor", None),
    )
    return jax.shard_map(
        functools.partial(body, mesh.shape["groups"], mesh.shape["replica"], mesh.shape["tensor"] // 2),
        mesh=mesh,
        in_specs=placed,
        out_specs=P(("groups", "replica"), None, "tensor"),
        check_vma=False,
    )
```

profile of v0, /device:TPU:0, one launch (start us, length us, event | category | flops | bytes accessed | tf_op | source)
XLA Modules:
  0.0 119.8 jit_solution(11255223160946241981)
XLA Ops:
  0.0 1.7 %constant_dynamic-slice_fusion.1 = bf16[16,16,512]{2,1,0:T(8,128)(2,1)} fusion(bf16[16,16,1024]{2,1,0:T(8,128)(2,1)} %table_ref.1, s32[]{:T(128)S(6)} %select_n.22), kind=kLoop, calls=%fused_computation.7 | loop fusion | bytes 524292 | tf_op jit(solution)/shard_map/dynamic_slice | solution.py:455
  1.7 5.9 %collective-permute-start.2 = (bf16[16,16,512]{2,1,0:T(8,128)(2,1)}, bf16[16,16,512]{2,1,0:T(8,128)(2,1)S(1)}, u32[]{:S(2)}, u32[]{:S(2)}) collective-permute-start(bf16[16,16,512]{2,1,0:T(8,128)(2,1)} %constant_dynamic-slice_fusion.1), channel_id=1, source_target_pairs={{0,8},{12,4},{1,9},{13,5},{2,10},{14,6},{3,11},{15,7},{16,24},{28,... | collective-permute-start | bytes 786440 | tf_op jit(solution)/shard_map/ppermute | solution.py:458
  7.6 0.7 collective-permute-start.1
  8.3 1.2 %collective-permute-start = (bf16[16,16,512]{2,1,0:T(8,128)(2,1)}, bf16[16,16,512]{2,1,0:T(8,128)(2,1)S(1)}, u32[]{:S(2)}, u32[]{:S(2)}) collective-permute-start(bf16[16,16,512]{2,1,0:T(8,128)(2,1)} %constant_dynamic-slice_fusion.1), channel_id=1, source_target_pairs={{0,4},{4,0},{8,12},{12,8},{1,5},{5,1},{9,13},{13,9},{2,6},{6,2},{1... | collective-permute-start | bytes 786440 | tf_op jit(solution)/shard_map/ppermute | solution.py:456
  9.5 1.2 %dynamic-slice = u32[1]{0:T(128)} dynamic-slice(u32[32]{0:T(128)} %constant.49, u32[]{:T(128)S(6)} %add.38), dynamic_slice_sizes={1} | dynamic-slice | bytes 12
  11.4 0.9 select_reduce_fusion.rows_ref
  12.3 0.2 dynamic-update-slice
  12.5 13.7 %all-reduce = s32[128]{0:T(128)S(1)} all-reduce(s32[128]{0:T(128)S(1)} %dynamic-update-slice), channel_id=2, replica_groups=mesh['groups'=2,'replica'=4,'tensor'=4] {'groups','replica'}, use_global_device_ids=true, to_apply=%add | all-reduce | flops 128 | bytes 1024
  26.2 0.1 reshape.17
  26.3 0.6 pad_add_fusion.1.place_ref
  26.9 0.6 constant_dynamic-slice_fusion.2.rows_ref
  27.5 3.8 %pack.1 = bf16[4,8,16,2048]{3,2,1,0:T(8,128)(2,1)} custom-call(s32[4,16]{1,0:T(4,128)} %constant_dynamic-slice_fusion.2.rows_ref, s32[2]{0:T(128)} %pad_add_fusion.1.place_ref, bf16[16,16,2048]{2,1,0:T(8,128)(2,1)} %refs_0_.1), custom_call_target="tpu_custom_call" | custom-call | tf_op jit(solution)/shard_map/pack/pallas_call | solution.py:206
  31.3 3.9 %all-to-all-start = ((bf16[4,8,16,2048]{3,2,1,0:T(8,128)(2,1)}), bf16[4,8,16,2048]{3,2,1,0:T(8,128)(2,1)S(1)}, u32[]{:S(2)}, u32[]{:S(2)}) async-start(bf16[4,8,16,2048]{3,2,1,0:T(8,128)(2,1)} %pack.1), calls=%async_computation | async-start | bytes 4194304 | tf_op jit(solution)/shard_map/all_to_all | solution.py:469
  35.2 0.8 copy.21.lens_ref
  36.0 0.9 copy.25
  36.9 1.6 %copy_bitcast_fusion.1 = (bf16[2,128,256]{2,1,0:T(8,128)(2,1)}, bf16[2,128,256]{2,1,0:T(8,128)(2,1)}) fusion(bf16[128,2,256]{2,1,0:T(2,128)(2,1)S(1)} %copy-done.15, bf16[128,2,256]{2,1,0:T(2,128)(2,1)} %param.11), kind=kLoop, calls=%fused_computation.1 | loop fusion | bytes 524288 | tf_op jit(solution)/shard_map/transpose | solution.py:475
  38.5 0.0 collective-permute-done.2.refs_2_
  38.5 1.3 %collective-permute-start.4 = (bf16[16,16,512]{2,1,0:T(8,128)(2,1)S(1)}, bf16[16,16,512]{2,1,0:T(8,128)(2,1)S(1)}, u32[]{:S(2)}, u32[]{:S(2)}) collective-permute-start(bf16[16,16,512]{2,1,0:T(8,128)(2,1)S(1)} %collective-permute-done.2.refs_2_), channel_id=1, source_target_pairs={{4,0},{8,12},{5,1},{9,13},{6,2},{10,14},{7,3},{11,15},{20,16},{24,... | collective-permute-start | bytes 786440 | tf_op jit(solution)/shard_map/ppermute | solution.py:460
  39.8 0.0 collective-permute-done.1.refs_1_
  39.9 1.3 %collective-permute-start.3 = (bf16[16,16,512]{2,1,0:T(8,128)(2,1)S(1)}, bf16[16,16,512]{2,1,0:T(8,128)(2,1)S(1)}, u32[]{:S(2)}, u32[]{:S(2)}) collective-permute-start(bf16[16,16,512]{2,1,0:T(8,128)(2,1)S(1)} %collective-permute-done.1.refs_1_), channel_id=1, source_target_pairs={{4,0},{8,12},{5,1},{9,13},{6,2},{10,14},{7,3},{11,15},{20,16},{24,... | collective-permute-start | bytes 786440 | tf_op jit(solution)/shard_map/ppermute | solution.py:460
  41.2 17.5 %attention.1.a_ref = bf16[256,1024]{1,0:T(8,128)(2,1)} custom-call(bf16[2,128,1024]{2,1,0:T(8,128)(2,1)} %bitcast.17, bf16[2,128,256]{2,1,0:T(8,128)(2,1)} %get-tuple-element.20.rk_ref, bf16[2,128,256]{2,1,0:T(8,128)(2,1)} %get-tuple-element.19.rv_ref, bf16[1,2,4096,256]{3,2,1,0:T(8,128)(2,1)} %kv_ref.1, s32[256,1]{1,0:T(8,128)} %copy.21.lens_ref), custom_call_target="tpu_custom_call" | custom-call | flops 20000000000 | bytes 6291456 | tf_op jit(solution)/shard_map/attention/pallas_call | solution.py:127
  58.7 7.5 %collective-permute-done.4.refs_4_ = bf16[16,16,512]{2,1,0:T(8,128)(2,1)S(1)} collective-permute-done((bf16[16,16,512]{2,1,0:T(8,128)(2,1)S(1)}, bf16[16,16,512]{2,1,0:T(8,128)(2,1)S(1)}, u32[]{:S(2)}, u32[]{:S(2)}) %collective-permute-start.4) | collective-permute-done | bytes 262176 | tf_op jit(solution)/shard_map/ppermute | solution.py:460
  66.1 3.6 %collective-permute-done.3.refs_3_ = bf16[16,16,512]{2,1,0:T(8,128)(2,1)S(1)} collective-permute-done((bf16[16,16,512]{2,1,0:T(8,128)(2,1)S(1)}, bf16[16,16,512]{2,1,0:T(8,128)(2,1)S(1)}, u32[]{:S(2)}, u32[]{:S(2)}) %collective-permute-start.3) | collective-permute-done | bytes 262176 | tf_op jit(solution)/shard_map/ppermute | solution.py:460
  69.7 4.0 %project.5 = bf16[256,2048]{1,0:T(8,128)(2,1)} custom-call(s32[1]{0:T(128)} %bitcast.10.group_ref, bf16[256,1024]{1,0:T(8,128)(2,1)} %attention.1.a_ref, bf16[1024,8192]{1,0:T(8,128)(2,1)} %w_ref.7), custom_call_target="tpu_custom_call" | custom-call | flops 1073741824 | bytes 4194304 | tf_op jit(solution)/shard_map/project/pallas_call | solution.py:165
  73.8 0.1 collective-permute-start.6
  73.9 3.9 %project.4 = bf16[256,2048]{1,0:T(8,128)(2,1)} custom-call(s32[1]{0:T(128)} %bitcast.8.group_ref, bf16[256,1024]{1,0:T(8,128)(2,1)} %attention.1.a_ref, bf16[1024,8192]{1,0:T(8,128)(2,1)} %w_ref.7), custom_call_target="tpu_custom_call" | custom-call | flops 1073741824 | bytes 4194304 | tf_op jit(solution)/shard_map/project/pallas_call | solution.py:165
  77.8 0.5 collective-permute-start.5
  78.3 4.3 %project.6 = bf16[256,2048]{1,0:T(8,128)(2,1)} custom-call(s32[1]{0:T(128)} %bitcast.9.group_ref, bf16[256,1024]{1,0:T(8,128)(2,1)} %attention.1.a_ref, bf16[1024,8192]{1,0:T(8,128)(2,1)} %w_ref.7, bf16[256,2048]{1,0:T(8,128)(2,1)} %collective-permute-done.6.rest_0_), custom_call_target="tpu_custom_call" | custom-call | flops 1073741824 | bytes 4194304 | tf_op jit(solution)/shard_map/project/pallas_call | solution.py:165
  82.5 1.5 %collective-permute-start.7 = (bf16[256,2048]{1,0:T(8,128)(2,1)}, bf16[256,2048]{1,0:T(8,128)(2,1)}, u32[]{:S(2)}, u32[]{:S(2)}) collective-permute-start(bf16[256,2048]{1,0:T(8,128)(2,1)} %project.6), channel_id=1, source_target_pairs={{0,2},{1,3},{2,0},{3,1},{4,6},{5,7},{6,4},{7,5},{8,10},{9,11},{10,... | collective-permute-start | bytes 3145736 | tf_op jit(solution)/shard_map/ppermute | solution.py:498
  84.0 0.9 copy-done.4
  85.0 0.9 copy-done.7
  85.9 0.9 copy-done.10
  86.9 0.9 copy-done.12
  87.8 1.1 partner_rows.1
  89.0 0.6 collective-permute-start.8
  89.6 7.5 %collective-permute-done.8.refs_5_ = bf16[16,16,512]{2,1,0:T(8,128)(2,1)S(1)} collective-permute-done((bf16[16,16,512]{2,1,0:T(8,128)(2,1)S(1)}, bf16[16,16,512]{2,1,0:T(8,128)(2,1)S(1)}, u32[]{:S(2)}, u32[]{:S(2)}) %collective-permute-start.8) | collective-permute-done | bytes 262176 | tf_op jit(solution)/shard_map/ppermute | solution.py:503
  97.0 0.9 copy-done.5
  98.0 0.9 copy-done.8
  98.9 1.7 %low_rank.1.rest_0_ = f32[256,128]{1,0:T(8,128)S(1)} custom-call(s32[16]{0:T(128)S(1)} %select_reduce_fusion.rows_ref, s32[2]{0:T(128)S(1)} %copy-done.13, bf16[256,1024]{1,0:T(8,128)(2,1)S(1)} %copy-done, bf16[16,16,1024]{2,1,0:T(8,128)(2,1)S(1)} %copy-done.2, bf16[16,16,512]{2,1,0:T(8,128)(2,1)S(1)} %copy-done.8, bf16[16,16,512]{2,1,0:T(8,128)(2,1)S(1)} %copy-done.5, ...), custom_call_target="tpu_custom_call" | custom-call | tf_op jit(solution)/shard_map/low_rank/pallas_call | solution.py:298
  100.6 0.1 collective-permute-start.11
  100.7 0.6 collective-permute-start.10
  101.3 1.2 %collective-permute-start.9 = (f32[256,128]{1,0:T(8,128)S(1)}, f32[256,128]{1,0:T(8,128)S(1)}, u32[]{:S(2)}, u32[]{:S(2)}) collective-permute-start(f32[256,128]{1,0:T(8,128)S(1)} %low_rank.1.rest_0_), channel_id=1, source_target_pairs={{0,1},{1,0},{2,3},{3,2},{4,5},{5,4},{6,7},{7,6},{8,9},{9,8},{10,11... | collective-permute-start | bytes 393224 | tf_op jit(solution)/shard_map/ppermute | solution.py:508
  102.5 6.3 %collective-permute-done.7.rest_1_ = bf16[256,2048]{1,0:T(8,128)(2,1)} collective-permute-done((bf16[256,2048]{1,0:T(8,128)(2,1)}, bf16[256,2048]{1,0:T(8,128)(2,1)}, u32[]{:S(2)}, u32[]{:S(2)}) %collective-permute-start.7) | collective-permute-done | bytes 1048608 | tf_op jit(solution)/shard_map/ppermute | solution.py:498
  108.9 4.7 %project.7.base_ref = f32[256,2048]{1,0:T(8,128)} custom-call(s32[1]{0:T(128)} %bitcast.group_ref, bf16[256,1024]{1,0:T(8,128)(2,1)} %attention.1.a_ref, bf16[1024,8192]{1,0:T(8,128)(2,1)} %w_ref.7, bf16[256,2048]{1,0:T(8,128)(2,1)} %collective-permute-done.5.rest_0_, bf16[256,2048]{1,0:T(8,128)(2,1)} %collective-permute-done.7.rest_1_), custom_call_target="tpu_custom_call" | custom-call | flops 1073741824 | bytes 4194304 | tf_op jit(solution)/shard_map/project/pallas_call | solution.py:165
  113.6 0.0 collective-permute-done.9.rest_1_
  113.6 0.0 all-to-all-done.rest_4_
  113.6 1.6 %copy-done.1 = f32[256,2048]{1,0:T(8,128)S(1)} copy-done((f32[256,2048]{1,0:T(8,128)S(1)}, f32[256,2048]{1,0:T(8,128)}, u32[]{:S(2)}) %copy-start.1) | copy-done | bytes 2097176
  115.2 4.6 %finish.1 = bf16[128,2,2048]{2,1,0:T(2,128)(2,1)} custom-call(s32[16]{0:T(128)S(1)} %select_reduce_fusion.rows_ref, f32[256,2048]{1,0:T(8,128)S(1)} %copy-done.1, f32[256,128]{1,0:T(8,128)S(1)} %low_rank.1.rest_0_, f32[256,128]{1,0:T(8,128)S(1)} %collective-permute-done.9.rest_1_, f32[256,128]{1,0:T(8,128)S(1)} %collective-permute-done.10.rest_2_, ...), custom_call_target="tpu_custom_call" | custom-call | tf_op jit(solution)/shard_map/finish/pallas_call | solution.py:404
  (35 shorter events, 0.1 us)
Async XLA Ops:
  1.7 36.9 %collective-permute-start.2 = (bf16[16,16,512]{2,1,0:T(8,128)(2,1)}, bf16[16,16,512]{2,1,0:T(8,128)(2,1)S(1)}, u32[]{:S(2)}, u32[]{:S(2)}) collective-permute-start(bf16[16,16,512]{2,1,0:T(8,128)(2,1)} %constant_dynamic-slice_fusion.1), channel_id=1, source_target_pairs={{0,8},{12,4},{1,9},{13,5},{2,10},{14,6},{3,11},{15,7},{16,24},{28,... | collective-permute-start | bytes 786440 | tf_op jit(solution)/shard_map/ppermute | solution.py:458
  7.6 32.2 %collective-permute-start.1 = (bf16[16,16,512]{2,1,0:T(8,128)(2,1)}, bf16[16,16,512]{2,1,0:T(8,128)(2,1)S(1)}, u32[]{:S(2)}, u32[]{:S(2)}) collective-permute-start(bf16[16,16,512]{2,1,0:T(8,128)(2,1)} %constant_dynamic-slice_fusion.1), channel_id=1, source_target_pairs={{4,8},{8,4},{5,9},{9,5},{6,10},{10,6},{7,11},{11,7},{20,24},{24,20... | collective-permute-start | bytes 786440 | tf_op jit(solution)/shard_map/ppermute | solution.py:457
  8.3 50.4 %collective-permute-start = (bf16[16,16,512]{2,1,0:T(8,128)(2,1)}, bf16[16,16,512]{2,1,0:T(8,128)(2,1)S(1)}, u32[]{:S(2)}, u32[]{:S(2)}) collective-permute-start(bf16[16,16,512]{2,1,0:T(8,128)(2,1)} %constant_dynamic-slice_fusion.1), channel_id=1, source_target_pairs={{0,4},{4,0},{8,12},{12,8},{1,5},{5,1},{9,13},{13,9},{2,6},{6,2},{1... | collective-permute-start | bytes 786440 | tf_op jit(solution)/shard_map/ppermute | solution.py:456
  31.3 3.9 %copy-start.16 = (s32[128]{0:T(128)S(1)}, s32[128]{0:T(128)}, u32[]{:S(2)}) copy-start(s32[128]{0:T(128)} %param.14) | copy-start | bytes 1540
  31.3 4.7 %copy-start.14 = (bf16[128,2,1024]{2,1,0:T(2,128)(2,1)S(1)}, bf16[128,2,1024]{2,1,0:T(2,128)(2,1)}, u32[]{:S(2)}) copy-start(bf16[128,2,1024]{2,1,0:T(2,128)(2,1)} %param.10) | copy-start | bytes 1572868
  31.3 5.6 %copy-start.15 = (bf16[128,2,256]{2,1,0:T(2,128)(2,1)S(1)}, bf16[128,2,256]{2,1,0:T(2,128)(2,1)}, u32[]{:S(2)}) copy-start(bf16[128,2,256]{2,1,0:T(2,128)(2,1)} %param.12) | copy-start | bytes 393220
  31.3 82.3 %all-to-all-start = ((bf16[4,8,16,2048]{3,2,1,0:T(8,128)(2,1)}), bf16[4,8,16,2048]{3,2,1,0:T(8,128)(2,1)S(1)}, u32[]{:S(2)}, u32[]{:S(2)}) async-start(bf16[4,8,16,2048]{3,2,1,0:T(8,128)(2,1)} %pack.1), calls=%async_computation | async-start | bytes 4194304 | tf_op jit(solution)/shard_map/all_to_all | solution.py:469
  38.5 27.6 %collective-permute-start.4 = (bf16[16,16,512]{2,1,0:T(8,128)(2,1)S(1)}, bf16[16,16,512]{2,1,0:T(8,128)(2,1)S(1)}, u32[]{:S(2)}, u32[]{:S(2)}) collective-permute-start(bf16[16,16,512]{2,1,0:T(8,128)(2,1)S(1)} %collective-permute-done.2.refs_2_), channel_id=1, source_target_pairs={{4,0},{8,12},{5,1},{9,13},{6,2},{10,14},{7,3},{11,15},{20,16},{24,... | collective-permute-start | bytes 786440 | tf_op jit(solution)/shard_map/ppermute | solution.py:460
  39.8 18.8 %copy-start.3 = (bf16[16,16,512]{2,1,0:T(8,128)(2,1)}, bf16[16,16,512]{2,1,0:T(8,128)(2,1)S(1)}, u32[]{:S(2)}) copy-start(bf16[16,16,512]{2,1,0:T(8,128)(2,1)S(1)} %collective-permute-done.1.refs_1_) | copy-start | bytes 786436
  39.9 29.9 %collective-permute-start.3 = (bf16[16,16,512]{2,1,0:T(8,128)(2,1)S(1)}, bf16[16,16,512]{2,1,0:T(8,128)(2,1)S(1)}, u32[]{:S(2)}, u32[]{:S(2)}) collective-permute-start(bf16[16,16,512]{2,1,0:T(8,128)(2,1)S(1)} %collective-permute-done.1.refs_1_), channel_id=1, source_target_pairs={{4,0},{8,12},{5,1},{9,13},{6,2},{10,14},{7,3},{11,15},{20,16},{24,... | collective-permute-start | bytes 786440 | tf_op jit(solution)/shard_map/ppermute | solution.py:460
  58.7 15.1 %copy-start.6 = (bf16[16,16,512]{2,1,0:T(8,128)(2,1)}, bf16[16,16,512]{2,1,0:T(8,128)(2,1)S(1)}, u32[]{:S(2)}) copy-start(bf16[16,16,512]{2,1,0:T(8,128)(2,1)S(1)} %collective-permute-done.refs_0_) | copy-start | bytes 786436
  66.1 7.6 %copy-start.9 = (bf16[16,16,512]{2,1,0:T(8,128)(2,1)}, bf16[16,16,512]{2,1,0:T(8,128)(2,1)S(1)}, u32[]{:S(2)}) copy-start(bf16[16,16,512]{2,1,0:T(8,128)(2,1)S(1)} %collective-permute-done.4.refs_4_) | copy-start | bytes 786436
  69.7 4.0 %copy-start.11 = (bf16[16,16,512]{2,1,0:T(8,128)(2,1)}, bf16[16,16,512]{2,1,0:T(8,128)(2,1)S(1)}, u32[]{:S(2)}) copy-start(bf16[16,16,512]{2,1,0:T(8,128)(2,1)S(1)} %collective-permute-done.3.refs_3_) | copy-start | bytes 786436
  73.8 4.5 %collective-permute-start.6 = (bf16[256,2048]{1,0:T(8,128)(2,1)}, bf16[256,2048]{1,0:T(8,128)(2,1)}, u32[]{:S(2)}, u32[]{:S(2)}) collective-permute-start(bf16[256,2048]{1,0:T(8,128)(2,1)} %project.5), channel_id=1, source_target_pairs={{0,1},{1,0},{2,3},{3,2},{4,5},{5,4},{6,7},{7,6},{8,9},{9,8},{10,11... | collective-permute-start | bytes 3145736 | tf_op jit(solution)/shard_map/ppermute | solution.py:491
  77.8 24.7 %collective-permute-start.5 = (bf16[256,2048]{1,0:T(8,128)(2,1)}, bf16[256,2048]{1,0:T(8,128)(2,1)}, u32[]{:S(2)}, u32[]{:S(2)}) collective-permute-start(bf16[256,2048]{1,0:T(8,128)(2,1)} %project.4), channel_id=1, source_target_pairs={{0,1},{1,0},{2,3},{3,2},{4,5},{5,4},{6,7},{7,6},{8,9},{9,8},{10,11... | collective-permute-start | bytes 3145736 | tf_op jit(solution)/shard_map/ppermute | solution.py:491
  78.3 5.8 %copy-start.13 = (s32[2]{0:T(128)S(1)}, s32[2]{0:T(128)}, u32[]{:S(2)}) copy-start(s32[2]{0:T(128)} %pad_add_fusion.1.place_ref) | copy-start | bytes 28
  78.3 18.7 %copy-start = (bf16[256,1024]{1,0:T(8,128)(2,1)S(1)}, bf16[256,1024]{1,0:T(8,128)(2,1)}, u32[]{:S(2)}) copy-start(bf16[256,1024]{1,0:T(8,128)(2,1)} %attention.1.a_ref) | copy-start | bytes 1572868
  78.3 18.7 %copy-start.2 = (bf16[16,16,1024]{2,1,0:T(8,128)(2,1)S(1)}, bf16[16,16,1024]{2,1,0:T(8,128)(2,1)}, u32[]{:S(2)}) copy-start(bf16[16,16,1024]{2,1,0:T(8,128)(2,1)} %table_ref.1) | copy-start | bytes 1572868
  82.5 26.3 %collective-permute-start.7 = (bf16[256,2048]{1,0:T(8,128)(2,1)}, bf16[256,2048]{1,0:T(8,128)(2,1)}, u32[]{:S(2)}, u32[]{:S(2)}) collective-permute-start(bf16[256,2048]{1,0:T(8,128)(2,1)} %project.6), channel_id=1, source_target_pairs={{0,2},{1,3},{2,0},{3,1},{4,6},{5,7},{6,4},{7,5},{8,10},{9,11},{10,... | collective-permute-start | bytes 3145736 | tf_op jit(solution)/shard_map/ppermute | solution.py:498
  84.0 1.0 copy-start.4
  85.0 0.9 copy-start.7
  85.9 0.9 copy-start.10
  86.9 0.9 copy-start.12
  89.0 8.1 %collective-permute-start.8 = (bf16[16,16,512]{2,1,0:T(8,128)(2,1)S(1)}, bf16[16,16,512]{2,1,0:T(8,128)(2,1)S(1)}, u32[]{:S(2)}, u32[]{:S(2)}) collective-permute-start(bf16[16,16,512]{2,1,0:T(8,128)(2,1)S(1)} %partner_rows.1), channel_id=1, source_target_pairs={{0,16},{16,0},{1,17},{17,1},{2,18},{18,2},{3,19},{19,3},{4,20},{20... | collective-permute-start | bytes 786440 | tf_op jit(solution)/shard_map/ppermute | solution.py:503
  97.0 1.0 copy-start.5
  98.0 0.9 copy-start.8
  100.6 13.0 %collective-permute-start.11 = (f32[256,128]{1,0:T(8,128)S(1)}, f32[256,128]{1,0:T(8,128)S(1)}, u32[]{:S(2)}, u32[]{:S(2)}) collective-permute-start(f32[256,128]{1,0:T(8,128)S(1)} %low_rank.1.rest_0_), channel_id=1, source_target_pairs={{0,3},{1,2},{2,1},{3,0},{4,7},{5,6},{6,5},{7,4},{8,11},{9,10},{10,... | collective-permute-start | bytes 393224 | tf_op jit(solution)/shard_map/ppermute | solution.py:508
  100.7 12.9 %collective-permute-start.10 = (f32[256,128]{1,0:T(8,128)S(1)}, f32[256,128]{1,0:T(8,128)S(1)}, u32[]{:S(2)}, u32[]{:S(2)}) collective-permute-start(f32[256,128]{1,0:T(8,128)S(1)} %low_rank.1.rest_0_), channel_id=1, source_target_pairs={{0,2},{1,3},{2,0},{3,1},{4,6},{5,7},{6,4},{7,5},{8,10},{9,11},{10,... | collective-permute-start | bytes 393224 | tf_op jit(solution)/shard_map/ppermute | solution.py:508
  101.3 12.3 %collective-permute-start.9 = (f32[256,128]{1,0:T(8,128)S(1)}, f32[256,128]{1,0:T(8,128)S(1)}, u32[]{:S(2)}, u32[]{:S(2)}) collective-permute-start(f32[256,128]{1,0:T(8,128)S(1)} %low_rank.1.rest_0_), channel_id=1, source_target_pairs={{0,1},{1,0},{2,3},{3,2},{4,5},{5,4},{6,7},{7,6},{8,9},{9,8},{10,11... | collective-permute-start | bytes 393224 | tf_op jit(solution)/shard_map/ppermute | solution.py:508
  113.6 1.6 %copy-start.1 = (f32[256,2048]{1,0:T(8,128)S(1)}, f32[256,2048]{1,0:T(8,128)}, u32[]{:S(2)}) copy-start(f32[256,2048]{1,0:T(8,128)} %project.7.base_ref) | copy-start | bytes 6291460
where the time goes:
time: 121 us; the launch traced here: 120 us
  Pallas kernels  45.6 us (38%)
  waiting for transfers between devices  24.9 us (21%)
  starting transfers between devices  18.8 us (16%)
  local copies, waits for them, and re-layouts  14.5 us (12%)
  blocking collectives  13.7 us (11%)
  other arithmetic  1.48 us (1%)
    pallas_call x1, Pallas kernels, attention(): pl.pallas_call(functools.partial(attention_kernel, unit_heads, key_block)...  17.5 us
    pallas_call x4, Pallas kernels, project(): pl.pallas_call(kernel, out_shape=jax.ShapeDtypeStruct((rows, width), dtyp...  16.9 us
    unnamed x1, blocking collectives  13.7 us
    unnamed x37, local copies, waits for them, and re-layouts  8.8 us
    ppermute x1, waiting for transfers between devices, body(): lax.ppermute(far, 'replica', onward)  7.47 us
    ppermute x1, waiting for transfers between devices, body(): lax.ppermute(partner_rows(partner_named, place, received), 'groups', [(0,...  7.46 us
    ppermute x1, waiting for transfers between devices, body(): sums.append(lax.ppermute(part, 'tensor', along(e)))  6.33 us
    ppermute x1, starting transfers between devices, body(): far = lax.ppermute(mine, 'replica', [(0, 2), (3, 1)])  5.94 us
  transfers between devices with their start and end apart: 13, of which 4 were waited for; matrix products, arithmetic and copies ran while one was open for 6% of the time, Pallas kernels for 34%

commit v1 on v0

--- a/solution.py
+++ b/solution.py
@@ -14,7 +14,6 @@
 BF16, F32 = jnp.bfloat16, jnp.float32
 VMEM = pl.BlockSpec(memory_space=pltpu.VMEM)
 SMEM = pl.BlockSpec(memory_space=pltpu.SMEM)
-SMALL_PARAMS = pltpu.CompilerParams(vmem_limit_bytes=20 * 1024 * 1024)
 PARAMS = pltpu.CompilerParams(vmem_limit_bytes=58 * 1024 * 1024)
 
 
@@ -145,7 +144,7 @@
 
 def project(attended, weight, column_group, width, add, dtype):
     rows, depth = attended.shape
-    tile = 1024 if width % 1024 == 0 else width
+    tile = 512 if width % 512 == 0 else width
     tiles = width // tile
 
     def kernel(group_ref, a_ref, w_ref, *rest):
@@ -179,7 +178,25 @@
     )(column_group.reshape(1), *operands)
 
 
-def pack(tables, rows_all, place, capacity):
+def add(a, b):
+    rows, width = a.shape
+    spec = pl.BlockSpec((rows // 4, width), lambda i: (i, 0))
+
+    def kernel(a_ref, b_ref, o_ref):
+        o_ref[...] = (a_ref[...].astype(F32) + b_ref[...].astype(F32)).astype(o_ref.dtype)
+
+    return pl.pallas_call(
+        kernel,
+        out_shape=jax.ShapeDtypeStruct((rows, width), BF16),
+        grid=(4,),
+        in_specs=[spec, spec],
+        out_specs=spec,
+        compiler_params=PARAMS,
+        name="add",
+    )(a, b)
+
+
+def pack(tables, rows_all, place, capacity, relative):
     replicas, batches = rows_all.shape
     stored, rank, _ = tables[0].shape
     widths = [t.shape[2] for t in tables]
@@ -189,7 +206,7 @@
         to = pl.program_id(0)
 
         def step(b, count):
-            row = rows_ref[to, b] - place_ref[0] * stored
+            row = rows_ref[to ^ place_ref[0] if relative else to, b] - place_ref[0] * stored
             mine = (row >= 0) & (row < stored)
 
             @pl.when(mine)
@@ -230,7 +247,7 @@
         out_shape=jax.ShapeDtypeStruct((batches,) + nearest.shape[1:], BF16),
         in_specs=[SMEM, SMEM] + [VMEM] * len(received),
         out_specs=VMEM,
-        compiler_params=SMALL_PARAMS,
+        compiler_params=PARAMS,
         name="partner_rows",
     )(rows, place, *received)
 
@@ -301,7 +318,7 @@
         in_specs=[SMEM, SMEM] + [VMEM] * (3 + len(received)),
         out_specs=VMEM,
         scratch_shapes=[pltpu.VMEM((batches, rank, half), BF16)] * 2,
-        compiler_params=SMALL_PARAMS,
+        compiler_params=PARAMS,
         name="low_rank",
     )(own_rows, place, attended, table, *received, partner)
 
@@ -369,7 +386,7 @@
         in_specs=[SMEM, whole(attended.shape), columns(arrived, depth, (arrived.shape[3] - depth) // depth)],
         out_specs=whole((rows, HD)),
         scratch_shapes=[pltpu.VMEM((batches, rank, depth), BF16)],
-        compiler_params=SMALL_PARAMS,
+        compiler_params=PARAMS,
         name="low_rank",
     )(own_rows, attended, arrived)
 
@@ -410,7 +427,7 @@
         + [pl.BlockSpec(arrived.shape[:3] + (tile,), lambda i: (0, 0, 0, i))],
         out_specs=pl.BlockSpec((forks, steps, tile), lambda i: (0, 0, i)),
         scratch_shapes=[pltpu.VMEM((batches, rank, tile), BF16)],
-        compiler_params=SMALL_PARAMS,
+        compiler_params=PARAMS,
         name="finish",
     )(own_rows, base, *ranks, arrived)
 
@@ -458,13 +475,15 @@
         far = lax.ppermute(mine, "replica", [(0, 2), (3, 1)])
         onward = [(1, 0), (2, 3)]
         received = [nearest, middle, far, lax.ppermute(middle, "replica", onward), lax.ppermute(far, "replica", onward)]
-        rows_all = lax.all_gather(own_rows, ("groups", "replica"))
-        partner_named = lax.dynamic_index_in_dim(rows_all, (1 - group) * replicas + replica, keepdims=False)
-        rows_all = lax.dynamic_slice_in_dim(rows_all, group * replicas, replicas, axis=0)
-        parts = pack([up_weight_table], rows_all, place, capacity)
+        partner_named = lax.ppermute(own_rows, "groups", [(0, 1), (1, 0)])
+        rows_all = jnp.stack(
+            [own_rows]
+            + [lax.ppermute(own_rows, "replica", [(z, z ^ d) for z in range(replicas)]) for d in range(1, replicas)]
+        )
+        parts = pack([up_weight_table], rows_all, place, capacity, True)
     else:
         rows_all = lax.all_gather(own_rows, "replica")
-        parts = pack([up_weight_table, down_weight_table], rows_all, place, capacity)
+        parts = pack([up_weight_table, down_weight_table], rows_all, place, capacity, False)
     queries = lax.optimization_barrier((queries, parts))[0]
     arrived = lax.all_to_all(parts, "replica", 0, 0)
 
@@ -478,7 +497,7 @@
     )
 
     if by_halves:
-        attended, *received = lax.optimization_barrier((attended, *received))
+        attended, *received[:3] = lax.optimization_barrier((attended, *received[:3]))
 
     swap = [(t, t ^ 1) for t in range(2 * chips)]
 
@@ -487,17 +506,16 @@
 
     order = list(range(1, chips)) + [0]
     starts = [lax.rem(chip + e, chips) * 2 for e in order]
-    halves = [
-        lax.ppermute(project(attended, output_weight, g + 1 - core, width, [], BF16), "tensor", swap)
-        for g in starts
-    ]
     sums = []
-    for e, g, half in zip(order, starts, halves):
-        if e:
-            part = project(attended, output_weight, g + core, width, [half], BF16)
-            sums.append(lax.ppermute(part, "tensor", along(e)))
-        else:
-            base = project(attended, output_weight, g + core, width, [half] + sums, F32)
+    own_start = starts[-1]
+    for e, g in zip(order[:-1], starts[:-1]):
+        half = lax.ppermute(project(attended, output_weight, g + 1 - core, width, [], BF16), "tensor", swap)
+        part = project(attended, output_weight, g + core, width, [], BF16)
+        part = add(part, half)
+        sums.append(lax.ppermute(part, "tensor", along(e)))
+    own_attended = lax.optimization_barrier((attended, part))[0] if sums else attended
+    half = lax.ppermute(project(own_attended, output_weight, own_start + 1 - core, width, [], BF16), "tensor", swap)
+    base = project(own_attended, output_weight, own_start + core, width, [half] + sums, F32)
 
     if by_halves:
         partner = lax.ppermute(partner_rows(partner_named, place, received), "groups", [(0, 1), (1, 0)])

time: 121 us -> 118 us (0.975)
  blocking collectives: 13.7 us -> 0 us
  Pallas kernels: 45.6 us -> 56.5 us
  starting transfers between devices: 18.8 us -> 25.1 us
  local copies, waits for them, and re-layouts: 14.5 us -> 10.4 us
  waiting for transfers between devices: 24.9 us -> 22.8 us
  other arithmetic: 1.48 us -> 2.82 us
    unnamed x1 -> x0, blocking collectives: 13.7 us -> none
    ppermute x0 -> x5, starting transfers between devices: none -> 7.84 us  [the longest x3 5.76 us: body(): lax.ppermute(own_rows, 'replica', [(z, z ^ d) for z in range(replicas)])]
    ppermute x1, waiting for transfers between devices: 6.33 us -> 0.01 us  [body(): sums.append(lax.ppermute(part, 'tensor', along(e)))]
    pallas_call x4, Pallas kernels: 16.9 us -> 20.7 us  [project(): pl.pallas_call(kernel, out_shape=jax.ShapeDtypeStruct((rows, width), dtyp...]
    pallas_call x0 -> x1, Pallas kernels: none -> 3.64 us  [add(): pl.pallas_call(kernel, out_shape=jax.ShapeDtypeStruct((rows, width), BF16...]
    unnamed x37 -> x32, local copies, waits for them, and re-layouts: 8.8 us -> 5.28 us
    ppermute x0 -> x5, waiting for transfers between devices: none -> 2.03 us  [the longest x1 2.02 us: body(): partner_named = lax.ppermute(own_rows, 'groups', [(0, 1), (1, 0)])]
    ppermute x1, waiting for transfers between devices: 3.6 us -> 5.52 us  [body(): lax.ppermute(middle, 'replica', onward)]
  transfers between devices with their start and end apart: 13 -> 17, of which waited for: 4 -> 5; matrix products, arithmetic and copies ran while one was open for 6% -> 6% of each run, Pallas kernels for 34% -> 43%
where the time goes in v1:
time: 118 us
  Pallas kernels  56.5 us (48%)
  starting transfers between devices  25.1 us (21%)
  waiting for transfers between devices  22.8 us (19%)
  local copies, waits for them, and re-layouts  10.4 us (9%)
  other arithmetic  2.82 us (2%)
    pallas_call x4, Pallas kernels, project(): pl.pallas_call(kernel, out_shape=jax.ShapeDtypeStruct((rows, width), dtyp...  20.7 us
    pallas_call x1, Pallas kernels, attention(): pl.pallas_call(functools.partial(attention_kernel, unit_heads, key_block)...  16.5 us
    ppermute x1, waiting for transfers between devices, body(): lax.ppermute(partner_rows(partner_named, place, received), 'groups', [(0,...  7.02 us
    ppermute x1, waiting for transfers between devices, body(): lax.ppermute(far, 'replica', onward)  6.92 us
    ppermute x3, starting transfers between devices, body(): lax.ppermute(own_rows, 'replica', [(z, z ^ d) for z in range(replicas)])  5.76 us
    pallas_call x1, Pallas kernels, finish(): pl.pallas_call(kernel, out_shape=jax.ShapeDtypeStruct((forks, steps, widt...  5.64 us
    ppermute x1, waiting for transfers between devices, body(): lax.ppermute(middle, 'replica', onward)  5.52 us
    unnamed x32, local copies, waits for them, and re-layouts  5.28 us
  transfers between devices with their start and end apart: 17, of which 5 were waited for; matrix products, arithmetic and copies ran while one was open for 6% of the time, Pallas kernels for 43%

profile of v1, /device:TPU:0, one launch (start us, length us, event | category | flops | bytes accessed | tf_op | source)
XLA Modules:
  0.0 117.7 jit_solution(15750835673281108571)
XLA Ops:
  0.0 0.9 select_reduce_fusion.rows_ref
  0.9 5.1 %collective-permute-start.2 = (s32[16]{0:T(128)S(1)}, s32[16]{0:T(128)S(1)}, u32[]{:S(2)}, u32[]{:S(2)}) collective-permute-start(s32[16]{0:T(128)S(1)} %select_reduce_fusion.rows_ref), channel_id=1, source_target_pairs={{0,12},{4,8},{8,4},{12,0},{1,13},{5,9},{9,5},{13,1},{2,14},{6,10},... | collective-permute-start | bytes 200 | tf_op jit(solution)/shard_map/ppermute | solution.py:481
  6.0 0.0 collective-permute-start.1
  6.0 0.6 collective-permute-start
  6.6 1.7 %constant_dynamic-slice_fusion = bf16[16,16,512]{2,1,0:T(8,128)(2,1)} fusion(bf16[16,16,1024]{2,1,0:T(8,128)(2,1)} %table_ref.1, s32[]{:T(128)S(6)} %select_n.14), kind=kLoop, calls=%fused_computation.8 | loop fusion | bytes 524292 | tf_op jit(solution)/shard_map/dynamic_slice | solution.py:472
  8.3 4.2 %collective-permute-start.5 = (bf16[16,16,512]{2,1,0:T(8,128)(2,1)}, bf16[16,16,512]{2,1,0:T(8,128)(2,1)S(1)}, u32[]{:S(2)}, u32[]{:S(2)}) collective-permute-start(bf16[16,16,512]{2,1,0:T(8,128)(2,1)} %constant_dynamic-slice_fusion), channel_id=1, source_target_pairs={{0,8},{12,4},{1,9},{13,5},{2,10},{14,6},{3,11},{15,7},{16,24},{28,... | collective-permute-start | bytes 786440 | tf_op jit(solution)/shard_map/ppermute | solution.py:475
  12.5 0.7 collective-permute-start.4
  13.2 0.7 pad_add_fusion.1
  13.9 0.6 pad_add_fusion.2.place_ref
  14.6 1.7 %copy_bitcast_fusion.1 = (bf16[2,128,256]{2,1,0:T(8,128)(2,1)}, bf16[2,128,256]{2,1,0:T(8,128)(2,1)}) fusion(bf16[128,2,256]{2,1,0:T(2,128)(2,1)} %param.12, bf16[128,2,256]{2,1,0:T(2,128)(2,1)} %param.11), kind=kLoop, calls=%fused_computation.1 | loop fusion | bytes 524288 | tf_op jit(solution)/shard_map/transpose | solution.py:494
  16.3 0.8 copy.21.lens_ref
  17.1 1.2 collective-permute-start.3
  18.3 0.0 collective-permute-done.1
  18.3 0.6 pad_add_fusion.rows_ref
  18.9 3.9 %pack.1 = bf16[4,8,16,2048]{3,2,1,0:T(8,128)(2,1)} custom-call(s32[4,16]{1,0:T(4,128)} %pad_add_fusion.rows_ref, s32[2]{0:T(128)} %pad_add_fusion.2.place_ref, bf16[16,16,2048]{2,1,0:T(8,128)(2,1)} %refs_0_.1), custom_call_target="tpu_custom_call" | custom-call | tf_op jit(solution)/shard_map/pack/pallas_call | solution.py:223
  22.8 3.7 %all-to-all-start = ((bf16[4,8,16,2048]{3,2,1,0:T(8,128)(2,1)}), bf16[4,8,16,2048]{3,2,1,0:T(8,128)(2,1)S(1)}, u32[]{:S(2)}, u32[]{:S(2)}) async-start(bf16[4,8,16,2048]{3,2,1,0:T(8,128)(2,1)} %pack.1), calls=%async_computation | async-start | bytes 4194304 | tf_op jit(solution)/shard_map/all_to_all | solution.py:488
  26.6 0.9 copy.25
  27.5 16.5 %attention.1.a_ref = bf16[256,1024]{1,0:T(8,128)(2,1)} custom-call(bf16[2,128,1024]{2,1,0:T(8,128)(2,1)} %bitcast.18, bf16[2,128,256]{2,1,0:T(8,128)(2,1)} %get-tuple-element.18.rk_ref, bf16[2,128,256]{2,1,0:T(8,128)(2,1)} %get-tuple-element.17.rv_ref, bf16[1,2,4096,256]{3,2,1,0:T(8,128)(2,1)} %kv_ref.1, s32[256,1]{1,0:T(8,128)} %copy.21.lens_ref), custom_call_target="tpu_custom_call" | custom-call | flops 20000000000 | bytes 6291456 | tf_op jit(solution)/shard_map/attention/pallas_call | solution.py:126
  44.0 0.7 copy-done.4
  44.7 0.1 copy-done.6
  44.8 5.0 %project.5 = bf16[256,2048]{1,0:T(8,128)(2,1)} custom-call(s32[1]{0:T(128)} %bitcast.12.group_ref, bf16[256,1024]{1,0:T(8,128)(2,1)} %attention.1.a_ref, bf16[1024,8192]{1,0:T(8,128)(2,1)} %w_ref.7), custom_call_target="tpu_custom_call" | custom-call | flops 1073741824 | bytes 4194304 | tf_op jit(solution)/shard_map/project/pallas_call | solution.py:164
  49.8 5.0 %project.4.a_ref = bf16[256,2048]{1,0:T(8,128)(2,1)} custom-call(s32[1]{0:T(128)} %bitcast.11.group_ref, bf16[256,1024]{1,0:T(8,128)(2,1)} %attention.1.a_ref, bf16[1024,8192]{1,0:T(8,128)(2,1)} %w_ref.7), custom_call_target="tpu_custom_call" | custom-call | flops 1073741824 | bytes 4194304 | tf_op jit(solution)/shard_map/project/pallas_call | solution.py:164
  54.8 1.0 copy-done.2
  55.7 3.6 %add.36 = bf16[256,2048]{1,0:T(8,128)(2,1)} custom-call(bf16[256,2048]{1,0:T(8,128)(2,1)} %project.4.a_ref, bf16[256,2048]{1,0:T(8,128)(2,1)} %copy-done.2), custom_call_target="tpu_custom_call" | custom-call | tf_op jit(solution)/shard_map/add/pallas_call | solution.py:188
  59.4 5.1 %project.6 = bf16[256,2048]{1,0:T(8,128)(2,1)} custom-call(s32[1]{0:T(128)} %bitcast.13.group_ref, bf16[256,1024]{1,0:T(8,128)(2,1)} %attention.1.a_ref, bf16[1024,8192]{1,0:T(8,128)(2,1)} %w_ref.7), custom_call_target="tpu_custom_call" | custom-call | flops 1073741824 | bytes 4194304 | tf_op jit(solution)/shard_map/project/pallas_call | solution.py:164
  64.4 0.5 collective-permute-start.7
  64.9 1.5 %collective-permute-start.8 = (bf16[256,2048]{1,0:T(8,128)(2,1)S(1)}, bf16[256,2048]{1,0:T(8,128)(2,1)}, u32[]{:S(2)}, u32[]{:S(2)}) collective-permute-start(bf16[256,2048]{1,0:T(8,128)(2,1)S(1)} %copy-done.1), channel_id=1, source_target_pairs={{0,2},{1,3},{2,0},{3,1},{4,6},{5,7},{6,4},{7,5},{8,10},{9,11},{10,... | collective-permute-start | bytes 3145736 | tf_op jit(solution)/shard_map/ppermute | solution.py:515
  66.4 1.3 %collective-permute-start.10 = (bf16[16,16,512]{2,1,0:T(8,128)(2,1)S(1)}, bf16[16,16,512]{2,1,0:T(8,128)(2,1)S(1)}, u32[]{:S(2)}, u32[]{:S(2)}) collective-permute-start(bf16[16,16,512]{2,1,0:T(8,128)(2,1)S(1)} %collective-permute-done.5.refs_2_), channel_id=1, source_target_pairs={{4,0},{8,12},{5,1},{9,13},{6,2},{10,14},{7,3},{11,15},{20,16},{24,... | collective-permute-start | bytes 786440 | tf_op jit(solution)/shard_map/ppermute | solution.py:477
  67.7 1.3 %collective-permute-start.9 = (bf16[16,16,512]{2,1,0:T(8,128)(2,1)S(1)}, bf16[16,16,512]{2,1,0:T(8,128)(2,1)S(1)}, u32[]{:S(2)}, u32[]{:S(2)}) collective-permute-start(bf16[16,16,512]{2,1,0:T(8,128)(2,1)S(1)} %copy-done.5), channel_id=1, source_target_pairs={{4,0},{8,12},{5,1},{9,13},{6,2},{10,14},{7,3},{11,15},{20,16},{24,... | collective-permute-start | bytes 786440 | tf_op jit(solution)/shard_map/ppermute | solution.py:477
  69.1 1.6 %collective-permute-start.11 = (s32[16]{0:T(128)S(1)}, s32[16]{0:T(128)S(1)}, u32[]{:S(2)}, u32[]{:S(2)}) collective-permute-start(s32[16]{0:T(128)S(1)} %select_reduce_fusion.rows_ref), channel_id=1, source_target_pairs={{0,16},{16,0},{1,17},{17,1},{2,18},{18,2},{3,19},{19,3},{4,20},{20... | collective-permute-start | bytes 200 | tf_op jit(solution)/shard_map/ppermute | solution.py:478
  70.6 2.0 %collective-permute-done.11.rows_ref = s32[16]{0:T(128)S(1)} collective-permute-done((s32[16]{0:T(128)S(1)}, s32[16]{0:T(128)S(1)}, u32[]{:S(2)}, u32[]{:S(2)}) %collective-permute-start.11) | collective-permute-done | bytes 96 | tf_op jit(solution)/shard_map/ppermute | solution.py:478
  72.7 6.9 %collective-permute-done.10.refs_4_ = bf16[16,16,512]{2,1,0:T(8,128)(2,1)S(1)} collective-permute-done((bf16[16,16,512]{2,1,0:T(8,128)(2,1)S(1)}, bf16[16,16,512]{2,1,0:T(8,128)(2,1)S(1)}, u32[]{:S(2)}, u32[]{:S(2)}) %collective-permute-start.10) | collective-permute-done | bytes 262176 | tf_op jit(solution)/shard_map/ppermute | solution.py:477
  79.6 5.5 %collective-permute-done.9.refs_3_ = bf16[16,16,512]{2,1,0:T(8,128)(2,1)S(1)} collective-permute-done((bf16[16,16,512]{2,1,0:T(8,128)(2,1)S(1)}, bf16[16,16,512]{2,1,0:T(8,128)(2,1)S(1)}, u32[]{:S(2)}, u32[]{:S(2)}) %collective-permute-start.9) | collective-permute-done | bytes 262176 | tf_op jit(solution)/shard_map/ppermute | solution.py:477
  85.1 0.7 copy-done.8
  85.8 2.6 %partner_rows.1 = bf16[16,16,512]{2,1,0:T(8,128)(2,1)} custom-call(s32[16]{0:T(128)} %copy-done.15, s32[2]{0:T(128)} %pad_add_fusion.2.place_ref, bf16[16,16,512]{2,1,0:T(8,128)(2,1)} %copy-done.6, bf16[16,16,512]{2,1,0:T(8,128)(2,1)} %copy-done.4, bf16[16,16,512]{2,1,0:T(8,128)(2,1)} %copy-done.3, bf16[16,16,512]{2,1,0:T(8,128)(2,1)} %copy-done.8, ...), custom_call_target="tpu_custom_call" | custom-call | tf_op jit(solution)/shard_map/partner_rows/pallas_call | solution.py:245
  88.4 1.5 %collective-permute-start.12 = (bf16[16,16,512]{2,1,0:T(8,128)(2,1)}, bf16[16,16,512]{2,1,0:T(8,128)(2,1)S(1)}, u32[]{:S(2)}, u32[]{:S(2)}) collective-permute-start(bf16[16,16,512]{2,1,0:T(8,128)(2,1)} %partner_rows.1), channel_id=1, source_target_pairs={{0,16},{16,0},{1,17},{17,1},{2,18},{18,2},{3,19},{19,3},{4,20},{20... | collective-permute-start | bytes 786440 | tf_op jit(solution)/shard_map/ppermute | solution.py:521
  89.9 7.0 %collective-permute-done.12.refs_5_ = bf16[16,16,512]{2,1,0:T(8,128)(2,1)S(1)} collective-permute-done((bf16[16,16,512]{2,1,0:T(8,128)(2,1)}, bf16[16,16,512]{2,1,0:T(8,128)(2,1)S(1)}, u32[]{:S(2)}, u32[]{:S(2)}) %collective-permute-start.12) | collective-permute-done | bytes 262176 | tf_op jit(solution)/shard_map/ppermute | solution.py:521
  97.0 0.7 copy-done.10
  97.7 3.5 %low_rank.1.rest_0_ = f32[256,128]{1,0:T(8,128)} custom-call(s32[16]{0:T(128)} %copy-done.14, s32[2]{0:T(128)} %pad_add_fusion.2.place_ref, bf16[256,1024]{1,0:T(8,128)(2,1)} %attention.1.a_ref, bf16[16,16,1024]{2,1,0:T(8,128)(2,1)} %table_ref.1, bf16[16,16,512]{2,1,0:T(8,128)(2,1)} %copy-done.6, bf16[16,16,512]{2,1,0:T(8,128)(2,1)} %copy-done.4, ...), custom_call_target="tpu_custom_call" | custom-call | tf_op jit(solution)/shard_map/low_rank/pallas_call | solution.py:315
  101.1 0.4 collective-permute-start.15
  101.5 1.1 collective-permute-start.14
  102.6 0.3 collective-permute-start.13
  103.0 5.7 %project.7.base_ref = f32[256,2048]{1,0:T(8,128)} custom-call(s32[1]{0:T(128)} %bitcast.group_ref, bf16[256,1024]{1,0:T(8,128)(2,1)} %attention.1.a_ref, bf16[1024,8192]{1,0:T(8,128)(2,1)} %w_ref.7, bf16[256,2048]{1,0:T(8,128)(2,1)} %collective-permute-done.7.rest_0_, bf16[256,2048]{1,0:T(8,128)(2,1)} %collective-permute-done.8.rest_1_), custom_call_target="tpu_custom_call" | custom-call | flops 1073741824 | bytes 4194304 | tf_op jit(solution)/shard_map/project/pallas_call | solution.py:164
  108.7 1.2 %collective-permute-done.14.rest_2_ = f32[256,128]{1,0:T(8,128)S(1)} collective-permute-done((f32[256,128]{1,0:T(8,128)}, f32[256,128]{1,0:T(8,128)S(1)}, u32[]{:S(2)}, u32[]{:S(2)}) %collective-permute-start.14) | collective-permute-done | bytes 131104 | tf_op jit(solution)/shard_map/ppermute | solution.py:526
  110.0 0.6 copy-done.12
  110.6 0.1 copy-done.13
  110.7 1.4 %copy-done = bf16[4,8,16,2048]{3,2,1,0:T(8,128)(2,1)} copy-done((bf16[4,8,16,2048]{3,2,1,0:T(8,128)(2,1)}, bf16[4,8,16,2048]{3,2,1,0:T(8,128)(2,1)S(1)}, u32[]{:S(2)}) %copy-start) | copy-done | bytes 2097176
  112.0 5.6 %finish.1 = bf16[128,2,2048]{2,1,0:T(2,128)(2,1)} custom-call(s32[16]{0:T(128)} %copy-done.14, f32[256,2048]{1,0:T(8,128)} %project.7.base_ref, f32[256,128]{1,0:T(8,128)} %low_rank.1.rest_0_, f32[256,128]{1,0:T(8,128)} %copy-done.13, f32[256,128]{1,0:T(8,128)} %copy-done.12, f32[256,128]{1,0:T(8,128)} %copy-done.11, bf16[4,8,16,2048]{3,2,1,0:T(8,128)(2,1)} %copy-done), custom_call_target="tpu_custom_call" | custom-call | tf_op jit(solution)/shard_map/finish/pallas_call | solution.py:421
  (36 shorter events, 0.1 us)
Async XLA Ops:
  0.9 68.2 %copy-start.14 = (s32[16]{0:T(128)}, s32[16]{0:T(128)S(1)}, u32[]{:S(2)}) copy-start(s32[16]{0:T(128)S(1)} %select_reduce_fusion.rows_ref) | copy-start | bytes 196
  0.9 16.3 %collective-permute-start.2 = (s32[16]{0:T(128)S(1)}, s32[16]{0:T(128)S(1)}, u32[]{:S(2)}, u32[]{:S(2)}) collective-permute-start(s32[16]{0:T(128)S(1)} %select_reduce_fusion.rows_ref), channel_id=1, source_target_pairs={{0,12},{4,8},{8,4},{12,0},{1,13},{5,9},{9,5},{13,1},{2,14},{6,10},... | collective-permute-start | bytes 200 | tf_op jit(solution)/shard_map/ppermute | solution.py:481
  6.0 12.3 %collective-permute-start.1 = (s32[16]{0:T(128)S(1)}, s32[16]{0:T(128)S(1)}, u32[]{:S(2)}, u32[]{:S(2)}) collective-permute-start(s32[16]{0:T(128)S(1)} %select_reduce_fusion.rows_ref), channel_id=1, source_target_pairs={{0,8},{4,12},{8,0},{12,4},{1,9},{5,13},{9,1},{13,5},{2,10},{6,14},... | collective-permute-start | bytes 200 | tf_op jit(solution)/shard_map/ppermute | solution.py:481
  6.0 12.3 %collective-permute-start = (s32[16]{0:T(128)S(1)}, s32[16]{0:T(128)S(1)}, u32[]{:S(2)}, u32[]{:S(2)}) collective-permute-start(s32[16]{0:T(128)S(1)} %select_reduce_fusion.rows_ref), channel_id=1, source_target_pairs={{0,4},{4,0},{8,12},{12,8},{1,5},{5,1},{9,13},{13,9},{2,6},{6,2},{1... | collective-permute-start | bytes 200 | tf_op jit(solution)/shard_map/ppermute | solution.py:481
  8.3 35.7 %collective-permute-start.5 = (bf16[16,16,512]{2,1,0:T(8,128)(2,1)}, bf16[16,16,512]{2,1,0:T(8,128)(2,1)S(1)}, u32[]{:S(2)}, u32[]{:S(2)}) collective-permute-start(bf16[16,16,512]{2,1,0:T(8,128)(2,1)} %constant_dynamic-slice_fusion), channel_id=1, source_target_pairs={{0,8},{12,4},{1,9},{13,5},{2,10},{14,6},{3,11},{15,7},{16,24},{28,... | collective-permute-start | bytes 786440 | tf_op jit(solution)/shard_map/ppermute | solution.py:475
  12.5 31.5 %collective-permute-start.4 = (bf16[16,16,512]{2,1,0:T(8,128)(2,1)}, bf16[16,16,512]{2,1,0:T(8,128)(2,1)S(1)}, u32[]{:S(2)}, u32[]{:S(2)}) collective-permute-start(bf16[16,16,512]{2,1,0:T(8,128)(2,1)} %constant_dynamic-slice_fusion), channel_id=1, source_target_pairs={{4,8},{8,4},{5,9},{9,5},{6,10},{10,6},{7,11},{11,7},{20,24},{24,20... | collective-permute-start | bytes 786440 | tf_op jit(solution)/shard_map/ppermute | solution.py:474
  17.1 26.9 %collective-permute-start.3 = (bf16[16,16,512]{2,1,0:T(8,128)(2,1)}, bf16[16,16,512]{2,1,0:T(8,128)(2,1)S(1)}, u32[]{:S(2)}, u32[]{:S(2)}) collective-permute-start(bf16[16,16,512]{2,1,0:T(8,128)(2,1)} %constant_dynamic-slice_fusion), channel_id=1, source_target_pairs={{0,4},{4,0},{8,12},{12,8},{1,5},{5,1},{9,13},{13,9},{2,6},{6,2},{1... | collective-permute-start | bytes 786440 | tf_op jit(solution)/shard_map/ppermute | solution.py:473
  22.8 3.8 %copy-start.9 = (bf16[128,2,1024]{2,1,0:T(2,128)(2,1)S(1)}, bf16[128,2,1024]{2,1,0:T(2,128)(2,1)}, u32[]{:S(2)}) copy-start(bf16[128,2,1024]{2,1,0:T(2,128)(2,1)} %param.10) | copy-start | bytes 1572868
  22.8 87.1 %all-to-all-start = ((bf16[4,8,16,2048]{3,2,1,0:T(8,128)(2,1)}), bf16[4,8,16,2048]{3,2,1,0:T(8,128)(2,1)S(1)}, u32[]{:S(2)}, u32[]{:S(2)}) async-start(bf16[4,8,16,2048]{3,2,1,0:T(8,128)(2,1)} %pack.1), calls=%async_computation | async-start | bytes 4194304 | tf_op jit(solution)/shard_map/all_to_all | solution.py:488
  44.0 22.4 %copy-start.3 = (bf16[16,16,512]{2,1,0:T(8,128)(2,1)}, bf16[16,16,512]{2,1,0:T(8,128)(2,1)S(1)}, u32[]{:S(2)}) copy-start(bf16[16,16,512]{2,1,0:T(8,128)(2,1)S(1)} %collective-permute-done.5.refs_2_) | copy-start | bytes 786436
  44.0 0.7 copy-start.4
  44.0 0.8 copy-start.6
  49.8 5.0 %collective-permute-start.6 = (bf16[256,2048]{1,0:T(8,128)(2,1)}, bf16[256,2048]{1,0:T(8,128)(2,1)S(1)}, u32[]{:S(2)}, u32[]{:S(2)}) collective-permute-start(bf16[256,2048]{1,0:T(8,128)(2,1)} %project.5), channel_id=1, source_target_pairs={{0,1},{1,0},{2,3},{3,2},{4,5},{5,4},{6,7},{7,6},{8,9},{9,8},{10,11... | collective-permute-start | bytes 3145736 | tf_op jit(solution)/shard_map/ppermute | solution.py:512
  54.8 1.0 copy-start.2
  59.4 5.6 %copy-start.1 = (bf16[256,2048]{1,0:T(8,128)(2,1)S(1)}, bf16[256,2048]{1,0:T(8,128)(2,1)}, u32[]{:S(2)}) copy-start(bf16[256,2048]{1,0:T(8,128)(2,1)} %add.36) | copy-start | bytes 3145732
  59.4 8.4 %copy-start.5 = (bf16[16,16,512]{2,1,0:T(8,128)(2,1)S(1)}, bf16[16,16,512]{2,1,0:T(8,128)(2,1)}, u32[]{:S(2)}) copy-start(bf16[16,16,512]{2,1,0:T(8,128)(2,1)} %copy-done.4) | copy-start | bytes 786436
  64.4 38.5 %collective-permute-start.7 = (bf16[256,2048]{1,0:T(8,128)(2,1)}, bf16[256,2048]{1,0:T(8,128)(2,1)}, u32[]{:S(2)}, u32[]{:S(2)}) collective-permute-start(bf16[256,2048]{1,0:T(8,128)(2,1)} %project.6), channel_id=1, source_target_pairs={{0,1},{1,0},{2,3},{3,2},{4,5},{5,4},{6,7},{7,6},{8,9},{9,8},{10,11... | collective-permute-start | bytes 3145736 | tf_op jit(solution)/shard_map/ppermute | solution.py:517
  64.9 38.0 %collective-permute-start.8 = (bf16[256,2048]{1,0:T(8,128)(2,1)S(1)}, bf16[256,2048]{1,0:T(8,128)(2,1)}, u32[]{:S(2)}, u32[]{:S(2)}) collective-permute-start(bf16[256,2048]{1,0:T(8,128)(2,1)S(1)} %copy-done.1), channel_id=1, source_target_pairs={{0,2},{1,3},{2,0},{3,1},{4,6},{5,7},{6,4},{7,5},{8,10},{9,11},{10,... | collective-permute-start | bytes 3145736 | tf_op jit(solution)/shard_map/ppermute | solution.py:515
  66.4 13.1 %collective-permute-start.10 = (bf16[16,16,512]{2,1,0:T(8,128)(2,1)S(1)}, bf16[16,16,512]{2,1,0:T(8,128)(2,1)S(1)}, u32[]{:S(2)}, u32[]{:S(2)}) collective-permute-start(bf16[16,16,512]{2,1,0:T(8,128)(2,1)S(1)} %collective-permute-done.5.refs_2_), channel_id=1, source_target_pairs={{4,0},{8,12},{5,1},{9,13},{6,2},{10,14},{7,3},{11,15},{20,16},{24,... | collective-permute-start | bytes 786440 | tf_op jit(solution)/shard_map/ppermute | solution.py:477
  67.7 17.4 %collective-permute-start.9 = (bf16[16,16,512]{2,1,0:T(8,128)(2,1)S(1)}, bf16[16,16,512]{2,1,0:T(8,128)(2,1)S(1)}, u32[]{:S(2)}, u32[]{:S(2)}) collective-permute-start(bf16[16,16,512]{2,1,0:T(8,128)(2,1)S(1)} %copy-done.5), channel_id=1, source_target_pairs={{4,0},{8,12},{5,1},{9,13},{6,2},{10,14},{7,3},{11,15},{20,16},{24,... | collective-permute-start | bytes 786440 | tf_op jit(solution)/shard_map/ppermute | solution.py:477
  69.1 3.6 %collective-permute-start.11 = (s32[16]{0:T(128)S(1)}, s32[16]{0:T(128)S(1)}, u32[]{:S(2)}, u32[]{:S(2)}) collective-permute-start(s32[16]{0:T(128)S(1)} %select_reduce_fusion.rows_ref), channel_id=1, source_target_pairs={{0,16},{16,0},{1,17},{17,1},{2,18},{18,2},{3,19},{19,3},{4,20},{20... | collective-permute-start | bytes 200 | tf_op jit(solution)/shard_map/ppermute | solution.py:478
  72.7 12.5 %copy-start.15 = (s32[16]{0:T(128)}, s32[16]{0:T(128)S(1)}, u32[]{:S(2)}) copy-start(s32[16]{0:T(128)S(1)} %collective-permute-done.11.rows_ref) | copy-start | bytes 196
  79.6 5.5 %copy-start.7 = (bf16[16,16,512]{2,1,0:T(8,128)(2,1)}, bf16[16,16,512]{2,1,0:T(8,128)(2,1)S(1)}, u32[]{:S(2)}) copy-start(bf16[16,16,512]{2,1,0:T(8,128)(2,1)S(1)} %collective-permute-done.10.refs_4_) | copy-start | bytes 786436
  85.1 0.7 copy-start.8
  88.4 8.5 %collective-permute-start.12 = (bf16[16,16,512]{2,1,0:T(8,128)(2,1)}, bf16[16,16,512]{2,1,0:T(8,128)(2,1)S(1)}, u32[]{:S(2)}, u32[]{:S(2)}) collective-permute-start(bf16[16,16,512]{2,1,0:T(8,128)(2,1)} %partner_rows.1), channel_id=1, source_target_pairs={{0,16},{16,0},{1,17},{17,1},{2,18},{18,2},{3,19},{19,3},{4,20},{20... | collective-permute-start | bytes 786440 | tf_op jit(solution)/shard_map/ppermute | solution.py:521
  96.9 0.7 copy-start.10
  101.1 7.6 %collective-permute-start.15 = (f32[256,128]{1,0:T(8,128)}, f32[256,128]{1,0:T(8,128)S(1)}, u32[]{:S(2)}, u32[]{:S(2)}) collective-permute-start(f32[256,128]{1,0:T(8,128)} %low_rank.1.rest_0_), channel_id=1, source_target_pairs={{0,3},{1,2},{2,1},{3,0},{4,7},{5,6},{6,5},{7,4},{8,11},{9,10},{10,... | collective-permute-start | bytes 393224 | tf_op jit(solution)/shard_map/ppermute | solution.py:526
  101.5 8.4 %collective-permute-start.14 = (f32[256,128]{1,0:T(8,128)}, f32[256,128]{1,0:T(8,128)S(1)}, u32[]{:S(2)}, u32[]{:S(2)}) collective-permute-start(f32[256,128]{1,0:T(8,128)} %low_rank.1.rest_0_), channel_id=1, source_target_pairs={{0,2},{1,3},{2,0},{3,1},{4,6},{5,7},{6,4},{7,5},{8,10},{9,11},{10,... | collective-permute-start | bytes 393224 | tf_op jit(solution)/shard_map/ppermute | solution.py:526
  102.6 7.3 %collective-permute-start.13 = (f32[256,128]{1,0:T(8,128)}, f32[256,128]{1,0:T(8,128)S(1)}, u32[]{:S(2)}, u32[]{:S(2)}) collective-permute-start(f32[256,128]{1,0:T(8,128)} %low_rank.1.rest_0_), channel_id=1, source_target_pairs={{0,1},{1,0},{2,3},{3,2},{4,5},{5,4},{6,7},{7,6},{8,9},{9,8},{10,11... | collective-permute-start | bytes 393224 | tf_op jit(solution)/shard_map/ppermute | solution.py:526
  108.7 1.3 %copy-start.11 = (f32[256,128]{1,0:T(8,128)}, f32[256,128]{1,0:T(8,128)S(1)}, u32[]{:S(2)}) copy-start(f32[256,128]{1,0:T(8,128)S(1)} %collective-permute-done.15.rest_3_) | copy-start | bytes 393220
  109.9 0.7 copy-start.12
  109.9 0.7 copy-start.13
  110.7 1.4 %copy-start = (bf16[4,8,16,2048]{3,2,1,0:T(8,128)(2,1)}, bf16[4,8,16,2048]{3,2,1,0:T(8,128)(2,1)S(1)}, u32[]{:S(2)}) copy-start(bf16[4,8,16,2048]{3,2,1,0:T(8,128)(2,1)S(1)} %all-to-all-done.rest_4_) | copy-start | bytes 6291460

commit v2 on v1

--- a/solution.py
+++ b/solution.py
@@ -14,13 +14,26 @@
 BF16, F32 = jnp.bfloat16, jnp.float32
 VMEM = pl.BlockSpec(memory_space=pltpu.VMEM)
 SMEM = pl.BlockSpec(memory_space=pltpu.SMEM)
+SMALL_PARAMS = pltpu.CompilerParams(vmem_limit_bytes=20 * 1024 * 1024)
 PARAMS = pltpu.CompilerParams(vmem_limit_bytes=58 * 1024 * 1024)
 
 
 def attention_kernel(
-    unit_heads, key_block, q_ref, rk_ref, rv_ref, kv_ref, lens_ref, o_ref,
-    s_a, s_b, vaug, mx_a, mx_b, mb, acc, lensb, qs,
+    unit_heads, key_block, groups_ref, q_ref, rk_ref, rv_ref, kv_ref, lens_ref, w_ref, o_ref, *rest
 ):
+    s_a, s_b, vaug, mx_a, mx_b, mb, acc, lensb, qs, w_buf, sems = rest[-11:]
+    part_refs = rest[:-11]
+    width_out = w_buf.shape[2]
+    loads = [
+        pltpu.make_async_copy(
+            w_ref.at[:, pl.ds(pl.multiple_of(groups_ref[i] * width_out, width_out), width_out)],
+            w_buf.at[i],
+            sems.at[i],
+        )
+        for i in range(len(part_refs))
+    ]
+    for load in loads:
+        load.start()
     steps, forks, width = q_ref.shape
     heads = width // HD
     heads_kv = rk_ref.shape[2] // HD
@@ -115,19 +128,28 @@
                     mixed = mixed + weights[t][at].astype(BF16).astype(F32) * value
                 o_ref[:, h * HD : (h + 1) * HD] = (mixed / total[at]).astype(BF16)
 
-
-def attention(q, rk, rv, kv, lens):
+    tile = 512
+    for i, (load, part_ref) in enumerate(zip(loads, part_refs)):
+        load.wait()
+        for c in range(width_out // tile):
+            at = slice(c * tile, (c + 1) * tile)
+            part_ref[:, at] = jnp.dot(o_ref[...], w_buf[i, :, at], preferred_element_type=F32).astype(BF16)
+
+
+def attention(q, rk, rv, kv, lens, weight, column_groups, out_width):
     steps, forks, width = q.shape
     prefix = kv.shape[2]
     heads_kv = rk.shape[2] // HD
+    parts = column_groups.shape[0]
     unit_heads = 2
     key_block = prefix
     rows = unit_heads * steps * forks
     return pl.pallas_call(
         functools.partial(attention_kernel, unit_heads, key_block),
-        out_shape=jax.ShapeDtypeStruct((steps * forks, width), BF16),
-        in_specs=[VMEM] * 5,
-        out_specs=VMEM,
+        out_shape=[jax.ShapeDtypeStruct((steps * forks, width), BF16)]
+        + [jax.ShapeDtypeStruct((steps * forks, out_width), BF16)] * parts,
+        in_specs=[SMEM] + [VMEM] * 5 + [pl.BlockSpec(memory_space=pl.ANY)],
+        out_specs=[VMEM] * (1 + parts),
         scratch_shapes=[pltpu.VMEM((prefix // key_block, rows, key_block), F32)] * 2
         + [pltpu.VMEM((heads_kv, prefix, 2 * HD), BF16)]
         + [pltpu.VMEM((rows, HD), F32)] * 3
@@ -135,16 +157,18 @@
             pltpu.VMEM((rows, 2 * HD), F32),
             pltpu.VMEM((rows, HD), jnp.int32),
             pltpu.VMEM((width // HD * steps * forks, HD), BF16),
+            pltpu.VMEM((parts, weight.shape[0], out_width), BF16),
+            pltpu.SemaphoreType.DMA((parts,)),
         ],
         compiler_params=PARAMS,
         cost_estimate=pl.CostEstimate(flops=2 * 10**10, bytes_accessed=6 * 2**20, transcendentals=0),
         name="attention",
-    )(q, rk, rv, kv, lens)
+    )(column_groups, q, rk, rv, kv, lens, weight)
 
 
 def project(attended, weight, column_group, width, add, dtype):
     rows, depth = attended.shape
-    tile = 512 if width % 512 == 0 else width
+    tile = 1024 if width % 1024 == 0 else width
     tiles = width // tile
 
     def kernel(group_ref, a_ref, w_ref, *rest):
@@ -176,24 +200,6 @@
         ),
         name="project",
     )(column_group.reshape(1), *operands)
-
-
-def add(a, b):
-    rows, width = a.shape
-    spec = pl.BlockSpec((rows // 4, width), lambda i: (i, 0))
-
-    def kernel(a_ref, b_ref, o_ref):
-        o_ref[...] = (a_ref[...].astype(F32) + b_ref[...].astype(F32)).astype(o_ref.dtype)
-
-    return pl.pallas_call(
-        kernel,
-        out_shape=jax.ShapeDtypeStruct((rows, width), BF16),
-        grid=(4,),
-        in_specs=[spec, spec],
-        out_specs=spec,
-        compiler_params=PARAMS,
-        name="add",
-    )(a, b)
 
 
 def pack(tables, rows_all, place, capacity, relative):
@@ -391,15 +397,16 @@
     )(own_rows, attended, arrived)
 
 
-def finish(base, ranks, forks, own_rows, stored, arrived):
-    rows, width = base.shape
+def finish(bases, ranks, forks, own_rows, stored, arrived):
+    rows, width = bases[0].shape
+    n_bases = len(bases)
     batches = own_rows.shape[0]
     rank = arrived.shape[2]
     tile = min(width, 1024)
     steps = rows // forks
 
-    def kernel(rows_ref, base_ref, *rest):
-        rank_refs = rest[:-3]
+    def kernel(rows_ref, *rest):
+        base_refs, rank_refs = rest[:n_bases], rest[n_bases:-3]
         arrived_ref, o_ref, selected = rest[-3:]
         collect(rows_ref, stored, arrived_ref, selected)
         total = rank_refs[0][...]
@@ -412,7 +419,8 @@
         up = selected[...].reshape(batches * rank, tile)
         out = jnp.dot(high, up, preferred_element_type=F32)
         out = out + jnp.dot(low, up, preferred_element_type=F32)
-        out = out + base_ref[...]
+        for r in base_refs:
+            out = out + r[...].astype(F32)
         out = out.astype(BF16)
         for s in range(steps):
             o_ref[:, s, :] = out[s * forks : (s + 1) * forks, :]
@@ -422,14 +430,15 @@
         kernel,
         out_shape=jax.ShapeDtypeStruct((forks, steps, width), BF16),
         grid=(width // tile,),
-        in_specs=[SMEM, by_tile]
+        in_specs=[SMEM]
+        + [by_tile] * n_bases
         + [whole(r.shape) for r in ranks]
         + [pl.BlockSpec(arrived.shape[:3] + (tile,), lambda i: (0, 0, 0, i))],
         out_specs=pl.BlockSpec((forks, steps, tile), lambda i: (0, 0, i)),
         scratch_shapes=[pltpu.VMEM((batches, rank, tile), BF16)],
-        compiler_params=PARAMS,
+        compiler_params=SMALL_PARAMS,
         name="finish",
-    )(own_rows, base, *ranks, arrived)
+    )(own_rows, *bases, *ranks, arrived)
 
 
 def lookup(wanted, adapter_table_row):
@@ -488,34 +497,40 @@
     arrived = lax.all_to_all(parts, "replica", 0, 0)
 
     lens = jnp.concatenate([prefix_length_each] * steps)[:, None]
-    attended = attention(
+    order = list(range(1, chips)) + [0]
+    starts = [lax.rem(chip + e, chips) * 2 for e in order]
+    first = [starts[0] + 1 - core, starts[0] + core, starts[-1] + 1 - core]
+    attended, *parts = attention(
         queries.transpose(1, 0, 2),
         recent_keys.transpose(1, 0, 2),
         recent_values.transpose(1, 0, 2),
         prefix_key_value,
         lens,
+        output_weight,
+        jnp.stack(first),
+        width,
     )
-
     if by_halves:
-        attended, *received[:3] = lax.optimization_barrier((attended, *received[:3]))
+        attended, *rest = lax.optimization_barrier((attended, *parts, *received[:3]))
+        parts, received[:3] = rest[: len(parts)], rest[len(parts) :]
 
     swap = [(t, t ^ 1) for t in range(2 * chips)]
 
     def along(e):
         return [(t, (t + 2 * e) % (2 * chips)) for t in range(2 * chips)]
 
-    order = list(range(1, chips)) + [0]
-    starts = [lax.rem(chip + e, chips) * 2 for e in order]
+    swapped = [lax.ppermute(p, "tensor", swap) for p in (parts[0], parts[2])]
     sums = []
-    own_start = starts[-1]
-    for e, g in zip(order[:-1], starts[:-1]):
-        half = lax.ppermute(project(attended, output_weight, g + 1 - core, width, [], BF16), "tensor", swap)
-        part = project(attended, output_weight, g + core, width, [], BF16)
-        part = add(part, half)
+    for i, (e, g) in enumerate(zip(order[:-1], starts[:-1])):
+        if i == 0:
+            half, part = swapped[0], parts[1]
+        else:
+            half = lax.ppermute(project(attended, output_weight, g + 1 - core, width, [], BF16), "tensor", swap)
+            part = project(attended, output_weight, g + core, width, [], BF16)
+        part = (part.astype(F32) + half.astype(F32)).astype(BF16)
         sums.append(lax.ppermute(part, "tensor", along(e)))
-    own_attended = lax.optimization_barrier((attended, part))[0] if sums else attended
-    half = lax.ppermute(project(own_attended, output_weight, own_start + 1 - core, width, [], BF16), "tensor", swap)
-    base = project(own_attended, output_weight, own_start + core, width, [half] + sums, F32)
+    last = lax.optimization_barrier((attended, part))[0]
+    base = project(last, output_weight, starts[-1] + core, width, [swapped[1]], BF16)
 
     if by_halves:
         partner = lax.ppermute(partner_rows(partner_named, place, received), "groups", [(0, 1), (1, 0)])
@@ -525,7 +540,7 @@
     ranks = [rank_part] + [
         lax.ppermute(rank_part, "tensor", [(t, t ^ e) for t in range(2 * chips)]) for e in range(1, 2 * chips)
     ]
-    return finish(base, ranks, forks, own_rows, stored, arrived)
+    return finish([base] + sums, ranks, forks, own_rows, stored, arrived)
 
 
 def solution(mesh):

time: 118 us -> 116 us (0.983)
  Pallas kernels: 56.5 us -> 40.6 us
  waiting for transfers between devices: 22.8 us -> 33.3 us
  starting transfers between devices: 25.1 us -> 28.6 us
  local copies, waits for them, and re-layouts: 10.4 us -> 7.05 us
  other arithmetic: 2.82 us -> 5.89 us
    pallas_call x4 -> x1, Pallas kernels: 20.7 us -> 4.18 us  [project(): pl.pallas_call(kernel, out_shape=jax.ShapeDtypeStruct((rows, width), dtyp...]
    ppermute x1, waiting for transfers between devices: 5.52 us -> 15.3 us  [body(): lax.ppermute(middle, 'replica', onward)]
    pallas_call x1, Pallas kernels: 16.5 us -> 21.3 us  [attention(): pl.pallas_call(functools.partial(attention_kernel, unit_heads, key_block)...]
    pallas_call x1 -> x0, Pallas kernels: 3.64 us -> none  [add(): pl.pallas_call(kernel, out_shape=jax.ShapeDtypeStruct((rows, width), BF16...]
    ppermute x2, waiting for transfers between devices: 0.01 us -> 3.08 us  [body(): swapped = [lax.ppermute(p, 'tensor', swap) for p in (parts[0], parts[2])]]
    unnamed x32 -> x22, local copies, waits for them, and re-layouts: 5.28 us -> 2.68 us
    ppermute x1, starting transfers between devices: 4.19 us -> 6.78 us  [body(): far = lax.ppermute(mine, 'replica', [(0, 2), (3, 1)])]
    convert_element_type x0 -> x1, other arithmetic: none -> 2.48 us  [body(): part = (part.astype(F32) + half.astype(F32)).astype(BF16)]
  transfers between devices with their start and end apart: 17 -> 17, of which waited for: 5 -> 7; matrix products, arithmetic and copies ran while one was open for 6% -> 8% of each run, Pallas kernels for 43% -> 31%
where the time goes in v2:
time: 116 us
  Pallas kernels  40.6 us (35%)
  waiting for transfers between devices  33.3 us (29%)
  starting transfers between devices  28.6 us (25%)
  local copies, waits for them, and re-layouts  7.05 us (6%)
  other arithmetic  5.89 us (5%)
    pallas_call x1, Pallas kernels, attention(): pl.pallas_call(functools.partial(attention_kernel, unit_heads, key_block)...  21.3 us
    ppermute x1, waiting for transfers between devices, body(): lax.ppermute(middle, 'replica', onward)  15.3 us
    ppermute x1, starting transfers between devices, body(): far = lax.ppermute(mine, 'replica', [(0, 2), (3, 1)])  6.78 us
    ppermute x1, waiting for transfers between devices, body(): lax.ppermute(partner_rows(partner_named, place, received), 'groups', [(0,...  5.86 us
    ppermute x3, starting transfers between devices, body(): lax.ppermute(own_rows, 'replica', [(z, z ^ d) for z in range(replicas)])  5.76 us
    pallas_call x1, Pallas kernels, finish(): pl.pallas_call(kernel, out_shape=jax.ShapeDtypeStruct((forks, steps, widt...  5.16 us
    ppermute x1, waiting for transfers between devices, body(): lax.ppermute(far, 'replica', onward)  4.49 us
    all_to_all x1, starting transfers between devices, body(): arrived = lax.all_to_all(parts, 'replica', 0, 0)  4.31 us
  transfers between devices with their start and end apart: 17, of which 7 were waited for; matrix products, arithmetic and copies ran while one was open for 8% of the time, Pallas kernels for 31%

profile of v2, /device:TPU:0, one launch (start us, length us, event | category | flops | bytes accessed | tf_op | source)
XLA Modules:
  0.0 115.6 jit_solution(11528006085632642985)
XLA Ops:
  0.0 0.9 select_reduce_fusion.rows_ref
  0.9 5.1 %collective-permute-start.2 = (s32[16]{0:T(128)S(1)}, s32[16]{0:T(128)S(1)}, u32[]{:S(2)}, u32[]{:S(2)}) collective-permute-start(s32[16]{0:T(128)S(1)} %select_reduce_fusion.rows_ref), channel_id=1, source_target_pairs={{0,12},{4,8},{8,4},{12,0},{1,13},{5,9},{9,5},{13,1},{2,14},{6,10},... | collective-permute-start | bytes 200 | tf_op jit(solution)/shard_map/ppermute | solution.py:490
  6.0 0.0 collective-permute-start.1
  6.0 0.6 collective-permute-start
  6.6 1.0 constant_dynamic-slice_fusion
  7.6 1.5 %collective-permute-start.3 = (bf16[16,16,512]{2,1,0:T(8,128)(2,1)S(1)}, bf16[16,16,512]{2,1,0:T(8,128)(2,1)S(1)}, u32[]{:S(2)}, u32[]{:S(2)}) collective-permute-start(bf16[16,16,512]{2,1,0:T(8,128)(2,1)S(1)} %constant_dynamic-slice_fusion), channel_id=1, source_target_pairs={{0,4},{4,0},{8,12},{12,8},{1,5},{5,1},{9,13},{13,9},{2,6},{6,2},{1... | collective-permute-start | bytes 786440 | tf_op jit(solution)/shard_map/ppermute | solution.py:482
  9.0 0.7 collective-permute-start.4
  9.7 0.7 pad_add_fusion.1
  10.5 0.6 pad_add_fusion.3.place_ref
  11.1 1.7 %copy_bitcast_fusion.1 = (bf16[2,128,256]{2,1,0:T(8,128)(2,1)}, bf16[2,128,256]{2,1,0:T(8,128)(2,1)}) fusion(bf16[128,2,256]{2,1,0:T(2,128)(2,1)} %param.12, bf16[128,2,256]{2,1,0:T(2,128)(2,1)} %param.11), kind=kLoop, calls=%fused_computation.2 | loop fusion | bytes 524288 | tf_op jit(solution)/shard_map/transpose | solution.py:506
  12.8 0.6 pad_add_fusion.2.groups_ref
  13.4 0.8 copy.21.lens_ref
  14.2 6.8 %collective-permute-start.5 = (bf16[16,16,512]{2,1,0:T(8,128)(2,1)S(1)}, bf16[16,16,512]{2,1,0:T(8,128)(2,1)}, u32[]{:S(2)}, u32[]{:S(2)}) collective-permute-start(bf16[16,16,512]{2,1,0:T(8,128)(2,1)S(1)} %constant_dynamic-slice_fusion), channel_id=1, source_target_pairs={{0,8},{12,4},{1,9},{13,5},{2,10},{14,6},{3,11},{15,7},{16,24},{28,... | collective-permute-start | bytes 786440 | tf_op jit(solution)/shard_map/ppermute | solution.py:484
  21.0 0.0 collective-permute-done
  21.0 0.6 pad_add_fusion.rows_ref
  21.6 3.9 %pack.1 = bf16[4,8,16,2048]{3,2,1,0:T(8,128)(2,1)} custom-call(s32[4,16]{1,0:T(4,128)} %pad_add_fusion.rows_ref, s32[2]{0:T(128)} %pad_add_fusion.3.place_ref, bf16[16,16,2048]{2,1,0:T(8,128)(2,1)} %refs_0_.1), custom_call_target="tpu_custom_call" | custom-call | tf_op jit(solution)/shard_map/pack/pallas_call | solution.py:229
  25.5 4.3 %all-to-all-start = ((bf16[4,8,16,2048]{3,2,1,0:T(8,128)(2,1)}), bf16[4,8,16,2048]{3,2,1,0:T(8,128)(2,1)S(1)}, u32[]{:S(2)}, u32[]{:S(2)}) async-start(bf16[4,8,16,2048]{3,2,1,0:T(8,128)(2,1)} %pack.1), calls=%async_computation | async-start | bytes 4194304 | tf_op jit(solution)/shard_map/all_to_all | solution.py:497
  29.8 0.9 copy.25
  30.7 21.3 %attention.1 = (bf16[256,1024]{1,0:T(8,128)(2,1)}, bf16[256,2048]{1,0:T(8,128)(2,1)}, bf16[256,2048]{1,0:T(8,128)(2,1)}, bf16[256,2048]{1,0:T(8,128)(2,1)}) custom-call(s32[3]{0:T(128)} %pad_add_fusion.2.groups_ref, bf16[2,128,1024]{2,1,0:T(8,128)(2,1)} %bitcast.19, bf16[2,128,256]{2,1,0:T(8,128)(2,1)} %get-tuple-element.32.rk_ref, ...), custom_call_target="tpu_custom_call" | custom-call | flops 20000000000 | bytes 6291456 | tf_op jit(solution)/shard_map/attention/pallas_call | solution.py:147
  52.1 0.0 collective-permute-done.3.refs_0_
  52.1 0.0 collective-permute-done.4.refs_1_
  52.1 0.1 collective-permute-start.6
  52.2 0.5 collective-permute-start.7
  52.7 3.1 %collective-permute-done.6 = bf16[256,2048]{1,0:T(8,128)(2,1)S(1)} collective-permute-done((bf16[256,2048]{1,0:T(8,128)(2,1)}, bf16[256,2048]{1,0:T(8,128)(2,1)S(1)}, u32[]{:S(2)}, u32[]{:S(2)}) %collective-permute-start.6) | collective-permute-done | bytes 1048608 | tf_op jit(solution)/shard_map/ppermute | solution.py:522
  55.8 2.5 %add_convert_fusion = bf16[256,2048]{1,0:T(8,128)(2,1)} fusion(bf16[256,2048]{1,0:T(8,128)(2,1)S(1)} %collective-permute-done.6, bf16[256,2048]{1,0:T(8,128)(2,1)} %get-tuple-element.24), kind=kLoop, calls=%fused_computation | loop fusion | flops 2097152 | bytes 3145728 | tf_op jit(solution)/shard_map/convert_element_type | solution.py:530
  58.3 1.5 %collective-permute-start.8 = (bf16[256,2048]{1,0:T(8,128)(2,1)}, bf16[256,2048]{1,0:T(8,128)(2,1)S(1)}, u32[]{:S(2)}, u32[]{:S(2)}) collective-permute-start(bf16[256,2048]{1,0:T(8,128)(2,1)} %add_convert_fusion), channel_id=1, source_target_pairs={{0,2},{1,3},{2,0},{3,1},{4,6},{5,7},{6,4},{7,5},{8,10},{9,11},{10,... | collective-permute-start | bytes 3145736 | tf_op jit(solution)/shard_map/ppermute | solution.py:531
  59.7 1.3 %collective-permute-start.9 = (bf16[16,16,512]{2,1,0:T(8,128)(2,1)}, bf16[16,16,512]{2,1,0:T(8,128)(2,1)S(1)}, u32[]{:S(2)}, u32[]{:S(2)}) collective-permute-start(bf16[16,16,512]{2,1,0:T(8,128)(2,1)} %copy-done.5), channel_id=1, source_target_pairs={{4,0},{8,12},{5,1},{9,13},{6,2},{10,14},{7,3},{11,15},{20,16},{24,... | collective-permute-start | bytes 786440 | tf_op jit(solution)/shard_map/ppermute | solution.py:486
  61.0 1.3 %collective-permute-start.10 = (bf16[16,16,512]{2,1,0:T(8,128)(2,1)}, bf16[16,16,512]{2,1,0:T(8,128)(2,1)S(1)}, u32[]{:S(2)}, u32[]{:S(2)}) collective-permute-start(bf16[16,16,512]{2,1,0:T(8,128)(2,1)} %collective-permute-done.5.refs_2_), channel_id=1, source_target_pairs={{4,0},{8,12},{5,1},{9,13},{6,2},{10,14},{7,3},{11,15},{20,16},{24,... | collective-permute-start | bytes 786440 | tf_op jit(solution)/shard_map/ppermute | solution.py:486
  62.3 1.6 %collective-permute-start.11 = (s32[16]{0:T(128)S(1)}, s32[16]{0:T(128)S(1)}, u32[]{:S(2)}, u32[]{:S(2)}) collective-permute-start(s32[16]{0:T(128)S(1)} %select_reduce_fusion.rows_ref), channel_id=1, source_target_pairs={{0,16},{16,0},{1,17},{17,1},{2,18},{18,2},{3,19},{19,3},{4,20},{20... | collective-permute-start | bytes 200 | tf_op jit(solution)/shard_map/ppermute | solution.py:487
  63.9 2.0 %collective-permute-done.11.rows_ref = s32[16]{0:T(128)S(1)} collective-permute-done((s32[16]{0:T(128)S(1)}, s32[16]{0:T(128)S(1)}, u32[]{:S(2)}, u32[]{:S(2)}) %collective-permute-start.11) | collective-permute-done | bytes 96 | tf_op jit(solution)/shard_map/ppermute | solution.py:487
  65.9 15.3 %collective-permute-done.9.refs_3_ = bf16[16,16,512]{2,1,0:T(8,128)(2,1)S(1)} collective-permute-done((bf16[16,16,512]{2,1,0:T(8,128)(2,1)}, bf16[16,16,512]{2,1,0:T(8,128)(2,1)S(1)}, u32[]{:S(2)}, u32[]{:S(2)}) %collective-permute-start.9) | collective-permute-done | bytes 262176 | tf_op jit(solution)/shard_map/ppermute | solution.py:486
  81.2 4.5 %collective-permute-done.10.refs_4_ = bf16[16,16,512]{2,1,0:T(8,128)(2,1)S(1)} collective-permute-done((bf16[16,16,512]{2,1,0:T(8,128)(2,1)}, bf16[16,16,512]{2,1,0:T(8,128)(2,1)S(1)}, u32[]{:S(2)}, u32[]{:S(2)}) %collective-permute-start.10) | collective-permute-done | bytes 262176 | tf_op jit(solution)/shard_map/ppermute | solution.py:486
  85.7 0.7 copy-done.7
  86.4 2.6 %partner_rows.1 = bf16[16,16,512]{2,1,0:T(8,128)(2,1)} custom-call(s32[16]{0:T(128)} %copy-done.10, s32[2]{0:T(128)} %pad_add_fusion.3.place_ref, bf16[16,16,512]{2,1,0:T(8,128)(2,1)} %copy-done.4, bf16[16,16,512]{2,1,0:T(8,128)(2,1)} %copy-done.5, bf16[16,16,512]{2,1,0:T(8,128)(2,1)} %collective-permute-done.5.refs_2_, bf16[16,16,512]{2,1,0:T(8,128)(2,1)} %copy-done.6, ...), custom_call_target="tpu_custom_call" | custom-call | tf_op jit(solution)/shard_map/partner_rows/pallas_call | solution.py:251
  89.0 1.5 %collective-permute-start.12 = (bf16[16,16,512]{2,1,0:T(8,128)(2,1)}, bf16[16,16,512]{2,1,0:T(8,128)(2,1)S(1)}, u32[]{:S(2)}, u32[]{:S(2)}) collective-permute-start(bf16[16,16,512]{2,1,0:T(8,128)(2,1)} %partner_rows.1), channel_id=1, source_target_pairs={{0,16},{16,0},{1,17},{17,1},{2,18},{18,2},{3,19},{19,3},{4,20},{20... | collective-permute-start | bytes 786440 | tf_op jit(solution)/shard_map/ppermute | solution.py:536
  90.5 5.9 %collective-permute-done.12.refs_5_ = bf16[16,16,512]{2,1,0:T(8,128)(2,1)S(1)} collective-permute-done((bf16[16,16,512]{2,1,0:T(8,128)(2,1)}, bf16[16,16,512]{2,1,0:T(8,128)(2,1)S(1)}, u32[]{:S(2)}, u32[]{:S(2)}) %collective-permute-start.12) | collective-permute-done | bytes 262176 | tf_op jit(solution)/shard_map/ppermute | solution.py:536
  96.4 0.7 copy-done.9
  97.1 3.5 %low_rank.1.rest_2_ = f32[256,128]{1,0:T(8,128)} custom-call(s32[16]{0:T(128)} %copy-done.2, s32[2]{0:T(128)} %pad_add_fusion.3.place_ref, bf16[256,1024]{1,0:T(8,128)(2,1)} %get-tuple-element.26.a_ref, bf16[16,16,1024]{2,1,0:T(8,128)(2,1)} %table_ref.1, bf16[16,16,512]{2,1,0:T(8,128)(2,1)} %copy-done.4, bf16[16,16,512]{2,1,0:T(8,128)(2,1)} %copy-done.5, ...), custom_call_target="tpu_custom_call" | custom-call | tf_op jit(solution)/shard_map/low_rank/pallas_call | solution.py:321
  100.6 0.5 collective-permute-start.14
  101.1 1.3 %collective-permute-start.15 = (f32[256,128]{1,0:T(8,128)}, f32[256,128]{1,0:T(8,128)}, u32[]{:S(2)}, u32[]{:S(2)}) collective-permute-start(f32[256,128]{1,0:T(8,128)} %low_rank.1.rest_2_), channel_id=1, source_target_pairs={{0,3},{1,2},{2,1},{3,0},{4,7},{5,6},{6,5},{7,4},{8,11},{9,10},{10,... | collective-permute-start | bytes 393224 | tf_op jit(solution)/shard_map/ppermute | solution.py:541
  102.4 0.0 collective-permute-done.7.rest_0_
  102.5 4.2 %project.1.rest_0_ = bf16[256,2048]{1,0:T(8,128)(2,1)} custom-call(s32[1]{0:T(128)} %bitcast.group_ref, bf16[256,1024]{1,0:T(8,128)(2,1)} %get-tuple-element.26.a_ref, bf16[1024,8192]{1,0:T(8,128)(2,1)} %w_ref.3, bf16[256,2048]{1,0:T(8,128)(2,1)} %collective-permute-done.7.rest_0_), custom_call_target="tpu_custom_call" | custom-call | flops 1073741824 | bytes 4194304 | tf_op jit(solution)/shard_map/project/pallas_call | solution.py:188
  106.6 0.0 collective-permute-done.13.rest_3_
  106.6 0.5 collective-permute-done.14.rest_4_
  107.1 2.1 %collective-permute-done.15.rest_5_ = f32[256,128]{1,0:T(8,128)} collective-permute-done((f32[256,128]{1,0:T(8,128)}, f32[256,128]{1,0:T(8,128)}, u32[]{:S(2)}, u32[]{:S(2)}) %collective-permute-start.15) | collective-permute-done | bytes 131104 | tf_op jit(solution)/shard_map/ppermute | solution.py:541
  109.3 0.0 copy-start
  109.3 1.2 %copy-done = bf16[256,2048]{1,0:T(8,128)(2,1)S(1)} copy-done((bf16[256,2048]{1,0:T(8,128)(2,1)S(1)}, bf16[256,2048]{1,0:T(8,128)(2,1)}, u32[]{:S(2)}) %copy-start) | copy-done | bytes 1048600
  110.5 5.2 %finish.1 = bf16[128,2,2048]{2,1,0:T(2,128)(2,1)} custom-call(s32[16]{0:T(128)S(1)} %copy-done.3, bf16[256,2048]{1,0:T(8,128)(2,1)S(1)} %copy-done, bf16[256,2048]{1,0:T(8,128)(2,1)S(1)} %collective-permute-done.8.rest_1_, f32[256,128]{1,0:T(8,128)S(1)} %copy-done.1, f32[256,128]{1,0:T(8,128)S(1)} %collective-permute-done.13.rest_3_, ...), custom_call_target="tpu_custom_call" | custom-call | tf_op jit(solution)/shard_map/finish/pallas_call | solution.py:429
  (24 shorter events, 0.0 us)
Async XLA Ops:
  0.9 61.5 %copy-start.2 = (s32[16]{0:T(128)}, s32[16]{0:T(128)S(1)}, u32[]{:S(2)}) copy-start(s32[16]{0:T(128)S(1)} %select_reduce_fusion.rows_ref) | copy-start | bytes 196
  0.9 13.4 %collective-permute-start.2 = (s32[16]{0:T(128)S(1)}, s32[16]{0:T(128)S(1)}, u32[]{:S(2)}, u32[]{:S(2)}) collective-permute-start(s32[16]{0:T(128)S(1)} %select_reduce_fusion.rows_ref), channel_id=1, source_target_pairs={{0,12},{4,8},{8,4},{12,0},{1,13},{5,9},{9,5},{13,1},{2,14},{6,10},... | collective-permute-start | bytes 200 | tf_op jit(solution)/shard_map/ppermute | solution.py:490
  6.0 15.0 %collective-permute-start.1 = (s32[16]{0:T(128)S(1)}, s32[16]{0:T(128)S(1)}, u32[]{:S(2)}, u32[]{:S(2)}) collective-permute-start(s32[16]{0:T(128)S(1)} %select_reduce_fusion.rows_ref), channel_id=1, source_target_pairs={{0,8},{4,12},{8,0},{12,4},{1,9},{5,13},{9,1},{13,5},{2,10},{6,14},... | collective-permute-start | bytes 200 | tf_op jit(solution)/shard_map/ppermute | solution.py:490
  6.0 15.0 %collective-permute-start = (s32[16]{0:T(128)S(1)}, s32[16]{0:T(128)S(1)}, u32[]{:S(2)}, u32[]{:S(2)}) collective-permute-start(s32[16]{0:T(128)S(1)} %select_reduce_fusion.rows_ref), channel_id=1, source_target_pairs={{0,4},{4,0},{8,12},{12,8},{1,5},{5,1},{9,13},{13,9},{2,6},{6,2},{1... | collective-permute-start | bytes 200 | tf_op jit(solution)/shard_map/ppermute | solution.py:490
  7.6 44.5 %collective-permute-start.3 = (bf16[16,16,512]{2,1,0:T(8,128)(2,1)S(1)}, bf16[16,16,512]{2,1,0:T(8,128)(2,1)S(1)}, u32[]{:S(2)}, u32[]{:S(2)}) collective-permute-start(bf16[16,16,512]{2,1,0:T(8,128)(2,1)S(1)} %constant_dynamic-slice_fusion), channel_id=1, source_target_pairs={{0,4},{4,0},{8,12},{12,8},{1,5},{5,1},{9,13},{13,9},{2,6},{6,2},{1... | collective-permute-start | bytes 786440 | tf_op jit(solution)/shard_map/ppermute | solution.py:482
  9.0 43.1 %collective-permute-start.4 = (bf16[16,16,512]{2,1,0:T(8,128)(2,1)S(1)}, bf16[16,16,512]{2,1,0:T(8,128)(2,1)S(1)}, u32[]{:S(2)}, u32[]{:S(2)}) collective-permute-start(bf16[16,16,512]{2,1,0:T(8,128)(2,1)S(1)} %constant_dynamic-slice_fusion), channel_id=1, source_target_pairs={{4,8},{8,4},{5,9},{9,5},{6,10},{10,6},{7,11},{11,7},{20,24},{24,20... | collective-permute-start | bytes 786440 | tf_op jit(solution)/shard_map/ppermute | solution.py:483
  14.2 37.9 %collective-permute-start.5 = (bf16[16,16,512]{2,1,0:T(8,128)(2,1)S(1)}, bf16[16,16,512]{2,1,0:T(8,128)(2,1)}, u32[]{:S(2)}, u32[]{:S(2)}) collective-permute-start(bf16[16,16,512]{2,1,0:T(8,128)(2,1)S(1)} %constant_dynamic-slice_fusion), channel_id=1, source_target_pairs={{0,8},{12,4},{1,9},{13,5},{2,10},{14,6},{3,11},{15,7},{16,24},{28,... | collective-permute-start | bytes 786440 | tf_op jit(solution)/shard_map/ppermute | solution.py:484
  25.5 4.3 %copy-start.8 = (bf16[128,2,1024]{2,1,0:T(2,128)(2,1)S(1)}, bf16[128,2,1024]{2,1,0:T(2,128)(2,1)}, u32[]{:S(2)}) copy-start(bf16[128,2,1024]{2,1,0:T(2,128)(2,1)} %param.10) | copy-start | bytes 1572868
  25.5 83.7 %all-to-all-start = ((bf16[4,8,16,2048]{3,2,1,0:T(8,128)(2,1)}), bf16[4,8,16,2048]{3,2,1,0:T(8,128)(2,1)S(1)}, u32[]{:S(2)}, u32[]{:S(2)}) async-start(bf16[4,8,16,2048]{3,2,1,0:T(8,128)(2,1)} %pack.1), calls=%async_computation | async-start | bytes 4194304 | tf_op jit(solution)/shard_map/all_to_all | solution.py:497
  52.1 33.6 %copy-start.4 = (bf16[16,16,512]{2,1,0:T(8,128)(2,1)}, bf16[16,16,512]{2,1,0:T(8,128)(2,1)S(1)}, u32[]{:S(2)}) copy-start(bf16[16,16,512]{2,1,0:T(8,128)(2,1)S(1)} %collective-permute-done.3.refs_0_) | copy-start | bytes 786436
  52.1 3.7 %copy-start.5 = (bf16[16,16,512]{2,1,0:T(8,128)(2,1)}, bf16[16,16,512]{2,1,0:T(8,128)(2,1)S(1)}, u32[]{:S(2)}) copy-start(bf16[16,16,512]{2,1,0:T(8,128)(2,1)S(1)} %collective-permute-done.4.refs_1_) | copy-start | bytes 786436
  52.1 3.7 %collective-permute-start.6 = (bf16[256,2048]{1,0:T(8,128)(2,1)}, bf16[256,2048]{1,0:T(8,128)(2,1)S(1)}, u32[]{:S(2)}, u32[]{:S(2)}) collective-permute-start(bf16[256,2048]{1,0:T(8,128)(2,1)} %get-tuple-element.25), channel_id=1, source_target_pairs={{0,1},{1,0},{2,3},{3,2},{4,5},{5,4},{6,7},{7,6},{8,9},{9,8},{10,11... | collective-permute-start | bytes 3145736 | tf_op jit(solution)/shard_map/ppermute | solution.py:522
  52.2 50.2 %collective-permute-start.7 = (bf16[256,2048]{1,0:T(8,128)(2,1)}, bf16[256,2048]{1,0:T(8,128)(2,1)}, u32[]{:S(2)}, u32[]{:S(2)}) collective-permute-start(bf16[256,2048]{1,0:T(8,128)(2,1)} %get-tuple-element.27), channel_id=1, source_target_pairs={{0,1},{1,0},{2,3},{3,2},{4,5},{5,4},{6,7},{7,6},{8,9},{9,8},{10,11... | collective-permute-start | bytes 3145736 | tf_op jit(solution)/shard_map/ppermute | solution.py:522
  58.3 51.0 %collective-permute-start.8 = (bf16[256,2048]{1,0:T(8,128)(2,1)}, bf16[256,2048]{1,0:T(8,128)(2,1)S(1)}, u32[]{:S(2)}, u32[]{:S(2)}) collective-permute-start(bf16[256,2048]{1,0:T(8,128)(2,1)} %add_convert_fusion), channel_id=1, source_target_pairs={{0,2},{1,3},{2,0},{3,1},{4,6},{5,7},{6,4},{7,5},{8,10},{9,11},{10,... | collective-permute-start | bytes 3145736 | tf_op jit(solution)/shard_map/ppermute | solution.py:531
  59.7 21.5 %collective-permute-start.9 = (bf16[16,16,512]{2,1,0:T(8,128)(2,1)}, bf16[16,16,512]{2,1,0:T(8,128)(2,1)S(1)}, u32[]{:S(2)}, u32[]{:S(2)}) collective-permute-start(bf16[16,16,512]{2,1,0:T(8,128)(2,1)} %copy-done.5), channel_id=1, source_target_pairs={{4,0},{8,12},{5,1},{9,13},{6,2},{10,14},{7,3},{11,15},{20,16},{24,... | collective-permute-start | bytes 786440 | tf_op jit(solution)/shard_map/ppermute | solution.py:486
  61.0 24.7 %collective-permute-start.10 = (bf16[16,16,512]{2,1,0:T(8,128)(2,1)}, bf16[16,16,512]{2,1,0:T(8,128)(2,1)S(1)}, u32[]{:S(2)}, u32[]{:S(2)}) collective-permute-start(bf16[16,16,512]{2,1,0:T(8,128)(2,1)} %collective-permute-done.5.refs_2_), channel_id=1, source_target_pairs={{4,0},{8,12},{5,1},{9,13},{6,2},{10,14},{7,3},{11,15},{20,16},{24,... | collective-permute-start | bytes 786440 | tf_op jit(solution)/shard_map/ppermute | solution.py:486
  62.3 3.6 %collective-permute-start.11 = (s32[16]{0:T(128)S(1)}, s32[16]{0:T(128)S(1)}, u32[]{:S(2)}, u32[]{:S(2)}) collective-permute-start(s32[16]{0:T(128)S(1)} %select_reduce_fusion.rows_ref), channel_id=1, source_target_pairs={{0,16},{16,0},{1,17},{17,1},{2,18},{18,2},{3,19},{19,3},{4,20},{20... | collective-permute-start | bytes 200 | tf_op jit(solution)/shard_map/ppermute | solution.py:487
  65.9 19.8 %copy-start.10 = (s32[16]{0:T(128)}, s32[16]{0:T(128)S(1)}, u32[]{:S(2)}) copy-start(s32[16]{0:T(128)S(1)} %collective-permute-done.11.rows_ref) | copy-start | bytes 196
  81.2 4.5 %copy-start.6 = (bf16[16,16,512]{2,1,0:T(8,128)(2,1)}, bf16[16,16,512]{2,1,0:T(8,128)(2,1)S(1)}, u32[]{:S(2)}) copy-start(bf16[16,16,512]{2,1,0:T(8,128)(2,1)S(1)} %collective-permute-done.9.refs_3_) | copy-start | bytes 786436
  85.7 0.7 copy-start.7
  89.0 7.4 %collective-permute-start.12 = (bf16[16,16,512]{2,1,0:T(8,128)(2,1)}, bf16[16,16,512]{2,1,0:T(8,128)(2,1)S(1)}, u32[]{:S(2)}, u32[]{:S(2)}) collective-permute-start(bf16[16,16,512]{2,1,0:T(8,128)(2,1)} %partner_rows.1), channel_id=1, source_target_pairs={{0,16},{16,0},{1,17},{17,1},{2,18},{18,2},{3,19},{19,3},{4,20},{20... | collective-permute-start | bytes 786440 | tf_op jit(solution)/shard_map/ppermute | solution.py:536
  96.4 0.7 copy-start.9
  100.6 6.1 %collective-permute-start.13 = (f32[256,128]{1,0:T(8,128)}, f32[256,128]{1,0:T(8,128)S(1)}, u32[]{:S(2)}, u32[]{:S(2)}) collective-permute-start(f32[256,128]{1,0:T(8,128)} %low_rank.1.rest_2_), channel_id=1, source_target_pairs={{0,1},{1,0},{2,3},{3,2},{4,5},{5,4},{6,7},{7,6},{8,9},{9,8},{10,11... | collective-permute-start | bytes 393224 | tf_op jit(solution)/shard_map/ppermute | solution.py:541
  100.6 6.5 %collective-permute-start.14 = (f32[256,128]{1,0:T(8,128)}, f32[256,128]{1,0:T(8,128)S(1)}, u32[]{:S(2)}, u32[]{:S(2)}) collective-permute-start(f32[256,128]{1,0:T(8,128)} %low_rank.1.rest_2_), channel_id=1, source_target_pairs={{0,2},{1,3},{2,0},{3,1},{4,6},{5,7},{6,4},{7,5},{8,10},{9,11},{10,... | collective-permute-start | bytes 393224 | tf_op jit(solution)/shard_map/ppermute | solution.py:541
  101.1 8.1 %collective-permute-start.15 = (f32[256,128]{1,0:T(8,128)}, f32[256,128]{1,0:T(8,128)}, u32[]{:S(2)}, u32[]{:S(2)}) collective-permute-start(f32[256,128]{1,0:T(8,128)} %low_rank.1.rest_2_), channel_id=1, source_target_pairs={{0,3},{1,2},{2,1},{3,0},{4,7},{5,6},{6,5},{7,4},{8,11},{9,10},{10,... | collective-permute-start | bytes 393224 | tf_op jit(solution)/shard_map/ppermute | solution.py:541
  102.4 6.8 %copy-start.1 = (f32[256,128]{1,0:T(8,128)S(1)}, f32[256,128]{1,0:T(8,128)}, u32[]{:S(2)}) copy-start(f32[256,128]{1,0:T(8,128)} %low_rank.1.rest_2_) | copy-start | bytes 393220
  102.4 6.8 %copy-start.3 = (s32[16]{0:T(128)S(1)}, s32[16]{0:T(128)}, u32[]{:S(2)}) copy-start(s32[16]{0:T(128)} %copy-done.2) | copy-start | bytes 196
  109.3 1.2 %copy-start = (bf16[256,2048]{1,0:T(8,128)(2,1)S(1)}, bf16[256,2048]{1,0:T(8,128)(2,1)}, u32[]{:S(2)}) copy-start(bf16[256,2048]{1,0:T(8,128)(2,1)} %project.1.rest_0_) | copy-start | bytes 3145732

commit v3 on v2

--- a/solution.py
+++ b/solution.py
@@ -237,98 +237,6 @@
     )(rows_all, place, *tables)
 
 
-def partner_rows(rows, place, received):
-    nearest = received[0]
-    batches = rows.shape[0]
-
-    def kernel(rows_ref, place_ref, *refs):
-        out = refs[-1]
-
-        @pl.loop(0, batches)
-        def _(b):
-            pick(rows_ref[b], place_ref, refs[:-1], lambda value: out.__setitem__(b, value))
-
-    return pl.pallas_call(
-        kernel,
-        out_shape=jax.ShapeDtypeStruct((batches,) + nearest.shape[1:], BF16),
-        in_specs=[SMEM, SMEM] + [VMEM] * len(received),
-        out_specs=VMEM,
-        compiler_params=PARAMS,
-        name="partner_rows",
-    )(rows, place, *received)
-
-
-def pick(row, place_ref, refs, put):
-    stored = refs[0].shape[0]
-    me = place_ref[0]
-    owner, at = row // stored, lax.rem(row, stored)
-    apart = owner ^ me
-    middle = (me == 1) | (me == 2)
-    for ref, where in zip(
-        refs,
-        (
-            apart == 1,
-            middle & (apart == 3),
-            middle & (apart == 2),
-            jnp.logical_not(middle) & (apart == 2),
-            jnp.logical_not(middle) & (apart == 3),
-        ),
-    ):
-
-        @pl.when(where)
-        def _():
-            put(ref[at])
-
-
-def low_rank_of_halves(attended, forks, own_rows, place, table, received, partner):
-    rows, depth = attended.shape
-    batches = own_rows.shape[0]
-    stored, rank, _ = table.shape
-    half = depth // 2
-
-    def kernel(rows_ref, place_ref, a_ref, table_ref, *refs):
-        partner_ref, o_ref, mine, other = refs[-4:]
-        here = pl.multiple_of(place_ref[1] * half, half)
-        there = pl.multiple_of((1 - place_ref[1]) * half, half)
-
-        @pl.loop(0, batches)
-        def _(b):
-            row = rows_ref[b]
-            own = row // stored == place_ref[0]
-            at = lax.rem(row, stored)
-
-            @pl.when(own)
-            def _():
-                mine[b] = table_ref[at, :, pl.ds(here, half)]
-                other[b] = table_ref[at, :, pl.ds(there, half)]
-
-            @pl.when(jnp.logical_not(own))
-            def _():
-                other[b] = partner_ref[b]
-
-            pick(row, place_ref, refs[:-4], lambda value: mine.__setitem__(b, value))
-
-        every = jnp.zeros((rows, batches * rank), F32)
-        for at, selected in ((here, mine), (there, other)):
-            every = every + lax.dot_general(
-                a_ref[:, pl.ds(at, half)],
-                selected[...].reshape(batches * rank, half),
-                (((1,), (1,)), ((), ())),
-                preferred_element_type=F32,
-            )
-        o_ref[...] = fold(every, rows, forks, batches, rank)
-
-    return pl.pallas_call(
-        kernel,
-        out_shape=jax.ShapeDtypeStruct((rows, HD), F32),
-        in_specs=[SMEM, SMEM] + [VMEM] * (3 + len(received)),
-        out_specs=VMEM,
-        scratch_shapes=[pltpu.VMEM((batches, rank, half), BF16)] * 2,
-        compiler_params=PARAMS,
-        name="low_rank",
-    )(own_rows, place, attended, table, *received, partner)
-
-
 def collect(rows_ref, stored, arrived_ref, selected):
     batches = selected.shape[0]
     for owner in range(arrived_ref.shape[0]):
@@ -348,6 +256,11 @@
 
 def whole(shape):
     return pl.BlockSpec(shape, lambda i: (0,) * len(shape))
+
+
+def columns(packed, width, block):
+    shape = packed.shape[:-1] + (width,)
+    return pl.BlockSpec(shape, lambda i: (0,) * (len(shape) - 1) + (block,))
 
 
 def columns(packed, width, block):
@@ -397,18 +310,32 @@
     )(own_rows, attended, arrived)
 
 
-def finish(bases, ranks, forks, own_rows, stored, arrived):
-    rows, width = bases[0].shape
-    n_bases = len(bases)
+def chosen(own_rows, stored, arrived, width):
     batches = own_rows.shape[0]
     rank = arrived.shape[2]
+
+    def kernel(rows_ref, arrived_ref, o_ref):
+        collect(rows_ref, stored, arrived_ref, o_ref)
+
+    return pl.pallas_call(
+        kernel,
+        out_shape=jax.ShapeDtypeStruct((batches, rank, width), BF16),
+        grid=(1,),
+        in_specs=[SMEM, columns(arrived, width, 0)],
+        out_specs=whole((batches, rank, width)),
+        compiler_params=PARAMS,
+        name="chosen",
+    )(own_rows, arrived)
+
+
+def finish(base, ranks, forks, up):
+    rows, width = base.shape
+    batches, rank, _ = up.shape
     tile = min(width, 1024)
     steps = rows // forks
 
-    def kernel(rows_ref, *rest):
-        base_refs, rank_refs = rest[:n_bases], rest[n_bases:-3]
-        arrived_ref, o_ref, selected = rest[-3:]
-        collect(rows_ref, stored, arrived_ref, selected)
+    def kernel(base_ref, up_ref, *rest):
+        rank_refs, o_ref = rest[:-1], rest[-1]
         total = rank_refs[0][...]
         for r in rank_refs[1:]:
             total = total + r[...]
@@ -416,29 +343,26 @@
         spread = jnp.where(batch_mask(rows, forks, batches, rank), spread, 0.0)
         high = spread.astype(BF16)
         low = (spread - high.astype(F32)).astype(BF16)
-        up = selected[...].reshape(batches * rank, tile)
-        out = jnp.dot(high, up, preferred_element_type=F32)
-        out = out + jnp.dot(low, up, preferred_element_type=F32)
-        for r in base_refs:
-            out = out + r[...].astype(F32)
-        out = out.astype(BF16)
+        columns = up_ref[...].reshape(batches * rank, tile)
+        out = jnp.dot(high, columns, preferred_element_type=F32)
+        out = out + jnp.dot(low, columns, preferred_element_type=F32)
+        out = (out + base_ref[...].astype(F32)).astype(BF16)
         for s in range(steps):
             o_ref[:, s, :] = out[s * forks : (s + 1) * forks, :]
 
-    by_tile = pl.BlockSpec((rows, tile), lambda i: (0, i))
     return pl.pallas_call(
         kernel,
         out_shape=jax.ShapeDtypeStruct((forks, steps, width), BF16),
         grid=(width // tile,),
-        in_specs=[SMEM]
-        + [by_tile] * n_bases
-        + [whole(r.shape) for r in ranks]
-        + [pl.BlockSpec(arrived.shape[:3] + (tile,), lambda i: (0, 0, 0, i))],
+        in_specs=[
+            pl.BlockSpec((rows, tile), lambda i: (0, i)),
+            pl.BlockSpec((batches, rank, tile), lambda i: (0, 0, i)),
+        ]
+        + [whole(r.shape) for r in ranks],
         out_specs=pl.BlockSpec((forks, steps, tile), lambda i: (0, 0, i)),
-        scratch_shapes=[pltpu.VMEM((batches, rank, tile), BF16)],
         compiler_params=SMALL_PARAMS,
         name="finish",
-    )(own_rows, *bases, *ranks, arrived)
+    )(base, up, *ranks)
 
 
 def lookup(wanted, adapter_table_row):
@@ -447,7 +371,6 @@
 
 
 def body(
-    groups,
     replicas,
     chips,
     queries,
@@ -472,34 +395,23 @@
     place = replica.reshape(1)
 
     own_rows = lookup(batch_adapter_index, adapter_table_row)
-    by_halves = replicas == 4 and groups == 2
     stored = down_weight_table.shape[0]
-    if by_halves:
-        group = lax.axis_index("groups").astype(jnp.int32)
-        place = jnp.stack([replica, group])
-        half = down_weight_table.shape[2] // 2
-        mine = lax.dynamic_slice_in_dim(down_weight_table, group * half, half, axis=2)
-        nearest = lax.ppermute(mine, "replica", [(0, 1), (1, 0), (2, 3), (3, 2)])
-        middle = lax.ppermute(mine, "replica", [(1, 2), (2, 1)])
-        far = lax.ppermute(mine, "replica", [(0, 2), (3, 1)])
-        onward = [(1, 0), (2, 3)]
-        received = [nearest, middle, far, lax.ppermute(middle, "replica", onward), lax.ppermute(far, "replica", onward)]
-        partner_named = lax.ppermute(own_rows, "groups", [(0, 1), (1, 0)])
+    by_xor = replicas == 4
+    if by_xor:
         rows_all = jnp.stack(
             [own_rows]
             + [lax.ppermute(own_rows, "replica", [(z, z ^ d) for z in range(replicas)]) for d in range(1, replicas)]
         )
-        parts = pack([up_weight_table], rows_all, place, capacity, True)
     else:
         rows_all = lax.all_gather(own_rows, "replica")
-        parts = pack([up_weight_table, down_weight_table], rows_all, place, capacity, False)
-    queries = lax.optimization_barrier((queries, parts))[0]
-    arrived = lax.all_to_all(parts, "replica", 0, 0)
+    packed = pack([up_weight_table, down_weight_table], rows_all, place, capacity, by_xor)
+    arrived = lax.all_to_all(packed, "replica", 0, 0)
 
     lens = jnp.concatenate([prefix_length_each] * steps)[:, None]
     order = list(range(1, chips)) + [0]
     starts = [lax.rem(chip + e, chips) * 2 for e in order]
     first = [starts[0] + 1 - core, starts[0] + core, starts[-1] + 1 - core]
+    first = lax.optimization_barrier((jnp.stack(first), packed))[0]
     attended, *parts = attention(
         queries.transpose(1, 0, 2),
         recent_keys.transpose(1, 0, 2),
@@ -507,13 +419,9 @@
         prefix_key_value,
         lens,
         output_weight,
-        jnp.stack(first),
+        first,
         width,
     )
-    if by_halves:
-        attended, *rest = lax.optimization_barrier((attended, *parts, *received[:3]))
-        parts, received[:3] = rest[: len(parts)], rest[len(parts) :]
-
     swap = [(t, t ^ 1) for t in range(2 * chips)]
 
     def along(e):
@@ -530,17 +438,15 @@
         part = (part.astype(F32) + half.astype(F32)).astype(BF16)
         sums.append(lax.ppermute(part, "tensor", along(e)))
     last = lax.optimization_barrier((attended, part))[0]
-    base = project(last, output_weight, starts[-1] + core, width, [swapped[1]], BF16)
-
-    if by_halves:
-        partner = lax.ppermute(partner_rows(partner_named, place, received), "groups", [(0, 1), (1, 0)])
-        rank_part = low_rank_of_halves(attended, forks, own_rows, place, down_weight_table, received, partner)
-    else:
-        rank_part = low_rank(attended, forks, own_rows, stored, arrived)
+    base = project(last, output_weight, starts[-1] + core, width, [swapped[1]] + sums, BF16)
+
+    ready = lax.optimization_barrier((attended, base))[0]
+    rank_part = low_rank(ready, forks, own_rows, stored, arrived)
     ranks = [rank_part] + [
         lax.ppermute(rank_part, "tensor", [(t, t ^ e) for t in range(2 * chips)]) for e in range(1, 2 * chips)
     ]
-    return finish([base] + sums, ranks, forks, own_rows, stored, arrived)
+    up = chosen(own_rows, stored, arrived, width)
+    return finish(base, ranks, forks, up)
 
 
 def solution(mesh):
@@ -557,7 +463,7 @@
         P("tensor", None),
     )
     return jax.shard_map(
-        functools.partial(body, mesh.shape["groups"], mesh.shape["replica"], mesh.shape["tensor"] // 2),
+        functools.partial(body, mesh.shape["replica"], mesh.shape["tensor"] // 2),
         mesh=mesh,
         in_specs=placed,
         out_specs=P(("groups", "replica"), None, "tensor"),

time: 116 us -> 105 us (0.905)
  starting transfers between devices: 28.6 us -> 14.5 us
  waiting for transfers between devices: 33.3 us -> 42.7 us
  Pallas kernels: 40.6 us -> 38.2 us
  other arithmetic: 5.89 us -> 3.69 us
  local copies, waits for them, and re-layouts: 7.05 us -> 5.71 us
    ppermute x7 -> x0, waiting for transfers between devices: 27.6 us -> none  [the longest x1 15.3 us: body(): lax.ppermute(middle, 'replica', onward)]
    ppermute x1, waiting for transfers between devices: 0.01 us -> 23.7 us  [body(): sums.append(lax.ppermute(part, 'tensor', along(e)))]
    ppermute x7 -> x0, starting transfers between devices: 14.6 us -> none  [the longest x1 6.78 us: body(): far = lax.ppermute(mine, 'replica', [(0, 2), (3, 1)])]
    all_to_all x1, waiting for transfers between devices: 0.01 us -> 11.5 us  [body(): arrived = lax.all_to_all(packed, 'replica', 0, 0)]
    pallas_call x1, Pallas kernels: 5.16 us -> 2.1 us  [finish(): pl.pallas_call(kernel, out_shape=jax.ShapeDtypeStruct((forks, steps, widt...]
    ppermute x3, waiting for transfers between devices: 0.01 us -> 2.1 us  [body(): lax.ppermute(own_rows, 'replica', [(z, z ^ d) for z in range(replicas)])]
    unnamed x22 -> x17, local copies, waits for them, and re-layouts: 2.68 us -> 3.21 us
  transfers between devices with their start and end apart: 17 -> 10, of which waited for: 7 -> 6; matrix products, arithmetic and copies ran while one was open for 8% -> 5% of each run, Pallas kernels for 31% -> 27%
where the time goes in v3:
time: 105 us
  waiting for transfers between devices  42.7 us (41%)
  Pallas kernels  38.2 us (36%)
  starting transfers between devices  14.5 us (14%)
  local copies, waits for them, and re-layouts  5.71 us (5%)
  other arithmetic  3.69 us (4%)
    ppermute x1, waiting for transfers between devices, body(): sums.append(lax.ppermute(part, 'tensor', along(e)))  23.7 us
    pallas_call x1, Pallas kernels, attention(): pl.pallas_call(functools.partial(attention_kernel, unit_heads, key_block)...  20.3 us
    all_to_all x1, waiting for transfers between devices, body(): arrived = lax.all_to_all(packed, 'replica', 0, 0)  11.5 us
    ppermute x3, starting transfers between devices, body(): lax.ppermute(own_rows, 'replica', [(z, z ^ d) for z in range(replicas)])  5.76 us
    all_to_all x1, starting transfers between devices, body(): arrived = lax.all_to_all(packed, 'replica', 0, 0)  4.8 us
    pallas_call x1, Pallas kernels, project(): pl.pallas_call(kernel, out_shape=jax.ShapeDtypeStruct((rows, width), dtyp...  4.53 us
    pallas_call x1, Pallas kernels, pack(): pl.pallas_call(kernel, out_shape=jax.ShapeDtypeStruct((replicas, capacity...  4.27 us
    pallas_call x1, Pallas kernels, chosen(): pl.pallas_call(kernel, out_shape=jax.ShapeDtypeStruct((batches, rank, wid...  3.59 us
  transfers between devices with their start and end apart: 10, of which 6 were waited for; matrix products, arithmetic and copies ran while one was open for 5% of the time, Pallas kernels for 27%

profile of v3, /device:TPU:0, one launch (start us, length us, event | category | flops | bytes accessed | tf_op | source)
XLA Modules:
  0.0 104.9 jit_solution(17112932188545638515)
XLA Ops:
  0.0 0.9 select_reduce_fusion.rows_ref
  0.9 0.0 copy-start.6
  0.9 5.1 %collective-permute-start.2 = (s32[16]{0:T(128)S(1)}, s32[16]{0:T(128)S(1)}, u32[]{:S(2)}, u32[]{:S(2)}) collective-permute-start(s32[16]{0:T(128)S(1)} %select_reduce_fusion.rows_ref), channel_id=1, source_target_pairs={{0,12},{4,8},{8,4},{12,0},{1,13},{5,9},{9,5},{13,1},{2,14},{6,10},... | collective-permute-start | bytes 200 | tf_op jit(solution)/shard_map/ppermute | solution.py:403
  6.0 0.0 collective-permute-start.1
  6.0 0.6 collective-permute-start
  6.6 1.7 %copy_bitcast_fusion.1 = (bf16[2,128,256]{2,1,0:T(8,128)(2,1)}, bf16[2,128,256]{2,1,0:T(8,128)(2,1)}) fusion(bf16[128,2,256]{2,1,0:T(2,128)(2,1)} %param.12, bf16[128,2,256]{2,1,0:T(2,128)(2,1)} %param.11), kind=kLoop, calls=%fused_computation.2 | loop fusion | bytes 524288 | tf_op jit(solution)/shard_map/transpose | solution.py:418
  8.3 0.0 collective-permute-done.2
  8.3 2.1 %collective-permute-done.1 = s32[16]{0:T(128)S(1)} collective-permute-done((s32[16]{0:T(128)S(1)}, s32[16]{0:T(128)S(1)}, u32[]{:S(2)}, u32[]{:S(2)}) %collective-permute-start.1) | collective-permute-done | bytes 96 | tf_op jit(solution)/shard_map/ppermute | solution.py:403
  10.4 0.0 collective-permute-done
  10.4 0.6 pad_add_fusion.rows_ref
  11.0 4.3 %pack.1 = bf16[4,8,16,3072]{3,2,1,0:T(8,128)(2,1)} custom-call(s32[4,16]{1,0:T(4,128)} %pad_add_fusion.rows_ref, s32[1]{0:T(128)} %bitcast.8.place_ref, bf16[16,16,2048]{2,1,0:T(8,128)(2,1)} %refs_0_.1, bf16[16,16,1024]{2,1,0:T(8,128)(2,1)} %refs_1_.1), custom_call_target="tpu_custom_call" | custom-call | tf_op jit(solution)/shard_map/pack/pallas_call | solution.py:229
  15.3 0.0 copy-start.7
  15.3 0.0 copy-done.6
  15.3 4.8 %all-to-all-start = ((bf16[4,8,16,3072]{3,2,1,0:T(8,128)(2,1)}), bf16[4,8,16,3072]{3,2,1,0:T(8,128)(2,1)}, u32[]{:S(2)}, u32[]{:S(2)}) async-start(bf16[4,8,16,3072]{3,2,1,0:T(8,128)(2,1)} %pack.1), calls=%async_computation | async-start | bytes 6291456 | tf_op jit(solution)/shard_map/all_to_all | solution.py:408
  20.1 0.0 copy-done.7
  20.2 0.0 copy-done.5
  20.2 0.9 copy.25
  21.1 0.8 copy.21.lens_ref
  21.9 0.6 pad_add_fusion.2.groups_ref
  22.5 20.3 %attention.1 = (bf16[256,1024]{1,0:T(8,128)(2,1)}, bf16[256,2048]{1,0:T(8,128)(2,1)}, bf16[256,2048]{1,0:T(8,128)(2,1)}, bf16[256,2048]{1,0:T(8,128)(2,1)}) custom-call(s32[3]{0:T(128)} %pad_add_fusion.2.groups_ref, bf16[2,128,1024]{2,1,0:T(8,128)(2,1)} %bitcast.17, bf16[2,128,256]{2,1,0:T(8,128)(2,1)} %get-tuple-element.20.rk_ref, ...), custom_call_target="tpu_custom_call" | custom-call | flops 20000000000 | bytes 6291456 | tf_op jit(solution)/shard_map/attention/pallas_call | solution.py:147
  42.8 0.1 collective-permute-start.3
  42.9 0.5 collective-permute-start.4
  43.4 2.4 %collective-permute-done.3 = bf16[256,2048]{1,0:T(8,128)(2,1)S(1)} collective-permute-done((bf16[256,2048]{1,0:T(8,128)(2,1)}, bf16[256,2048]{1,0:T(8,128)(2,1)S(1)}, u32[]{:S(2)}, u32[]{:S(2)}) %collective-permute-start.3) | collective-permute-done | bytes 1048608 | tf_op jit(solution)/shard_map/ppermute | solution.py:430
  45.7 1.6 %add_convert_fusion = bf16[256,2048]{1,0:T(8,128)(2,1)S(1)} fusion(bf16[256,2048]{1,0:T(8,128)(2,1)S(1)} %collective-permute-done.3, bf16[256,2048]{1,0:T(8,128)(2,1)} %get-tuple-element.14), kind=kLoop, calls=%fused_computation | loop fusion | flops 2097152 | bytes 3145728 | tf_op jit(solution)/shard_map/convert_element_type | solution.py:438
  47.4 1.6 %collective-permute-start.5 = (bf16[256,2048]{1,0:T(8,128)(2,1)S(1)}, bf16[256,2048]{1,0:T(8,128)(2,1)S(1)}, u32[]{:S(2)}, u32[]{:S(2)}) collective-permute-start(bf16[256,2048]{1,0:T(8,128)(2,1)S(1)} %add_convert_fusion), channel_id=1, source_target_pairs={{0,2},{1,3},{2,0},{3,1},{4,6},{5,7},{6,4},{7,5},{8,10},{9,11},{10,... | collective-permute-start | bytes 3145736 | tf_op jit(solution)/shard_map/ppermute | solution.py:439
  48.9 0.0 collective-permute-done.4.rest_0_
  49.0 0.0 copy-start.3
  49.0 23.7 %collective-permute-done.5.rest_1_ = bf16[256,2048]{1,0:T(8,128)(2,1)S(1)} collective-permute-done((bf16[256,2048]{1,0:T(8,128)(2,1)S(1)}, bf16[256,2048]{1,0:T(8,128)(2,1)S(1)}, u32[]{:S(2)}, u32[]{:S(2)}) %collective-permute-start.5) | collective-permute-done | bytes 1048608 | tf_op jit(solution)/shard_map/ppermute | solution.py:439
  72.7 0.0 copy-start.4
  72.7 0.0 copy-done.3
  72.7 1.0 copy-done.4
  73.7 4.5 %project.1.base_ref = bf16[256,2048]{1,0:T(8,128)(2,1)} custom-call(s32[1]{0:T(128)} %bitcast.group_ref, bf16[256,1024]{1,0:T(8,128)(2,1)} %get-tuple-element.18.a_ref, bf16[1024,8192]{1,0:T(8,128)(2,1)} %w_ref.3, bf16[256,2048]{1,0:T(8,128)(2,1)} %copy-done.3, bf16[256,2048]{1,0:T(8,128)(2,1)} %copy-done.4), custom_call_target="tpu_custom_call" | custom-call | flops 1073741824 | bytes 4194304 | tf_op jit(solution)/shard_map/project/pallas_call | solution.py:188
  78.2 0.0 copy-start
  78.2 11.5 %all-to-all-done.arrived_ref = bf16[4,8,16,3072]{3,2,1,0:T(8,128)(2,1)} async-done(((bf16[4,8,16,3072]{3,2,1,0:T(8,128)(2,1)}), bf16[4,8,16,3072]{3,2,1,0:T(8,128)(2,1)}, u32[]{:S(2)}, u32[]{:S(2)}) %all-to-all-start) | async-done | bytes 3145760 | tf_op jit(solution)/shard_map/all_to_all | solution.py:408
  89.7 3.4 %low_rank.1.rest_0_ = f32[256,128]{1,0:T(8,128)} custom-call(s32[16]{0:T(128)} %copy-done.6, bf16[256,1024]{1,0:T(8,128)(2,1)} %get-tuple-element.18.a_ref, bf16[4,8,16,3072]{3,2,1,0:T(8,128)(2,1)} %all-to-all-done.arrived_ref), custom_call_target="tpu_custom_call" | custom-call | tf_op jit(solution)/shard_map/low_rank/pallas_call | solution.py:301
  93.0 0.0 copy-start.2
  93.0 0.0 collective-permute-start.6
  93.0 1.5 %collective-permute-start.7 = (f32[256,128]{1,0:T(8,128)}, f32[256,128]{1,0:T(8,128)S(1)}, u32[]{:S(2)}, u32[]{:S(2)}) collective-permute-start(f32[256,128]{1,0:T(8,128)} %low_rank.1.rest_0_), channel_id=1, source_target_pairs={{0,2},{1,3},{2,0},{3,1},{4,6},{5,7},{6,4},{7,5},{8,10},{9,11},{10,... | collective-permute-start | bytes 393224 | tf_op jit(solution)/shard_map/ppermute | solution.py:446
  94.5 0.4 collective-permute-start.8
  94.9 3.6 %chosen.1.up_ref = bf16[16,16,2048]{2,1,0:T(8,128)(2,1)} custom-call(s32[16]{0:T(128)} %copy-done.6, bf16[4,8,16,3072]{3,2,1,0:T(8,128)(2,1)} %all-to-all-done.arrived_ref), custom_call_target="tpu_custom_call" | custom-call | tf_op jit(solution)/shard_map/chosen/pallas_call | solution.py:320
  98.5 0.0 collective-permute-done.6.rest_1_
  98.5 1.1 %collective-permute-done.7.rest_2_ = f32[256,128]{1,0:T(8,128)S(1)} collective-permute-done((f32[256,128]{1,0:T(8,128)}, f32[256,128]{1,0:T(8,128)S(1)}, u32[]{:S(2)}, u32[]{:S(2)}) %collective-permute-start.7) | collective-permute-done | bytes 131104 | tf_op jit(solution)/shard_map/ppermute | solution.py:446
  99.5 2.0 %collective-permute-done.8.rest_3_ = f32[256,128]{1,0:T(8,128)S(1)} collective-permute-done((f32[256,128]{1,0:T(8,128)}, f32[256,128]{1,0:T(8,128)S(1)}, u32[]{:S(2)}, u32[]{:S(2)}) %collective-permute-start.8) | collective-permute-done | bytes 131104 | tf_op jit(solution)/shard_map/ppermute | solution.py:446
  101.6 0.0 copy-done
  101.6 0.0 copy-done.2
  101.6 0.0 copy-start.1
  101.6 1.2 %copy-done.1 = bf16[16,16,2048]{2,1,0:T(8,128)(2,1)S(1)} copy-done((bf16[16,16,2048]{2,1,0:T(8,128)(2,1)S(1)}, bf16[16,16,2048]{2,1,0:T(8,128)(2,1)}, u32[]{:S(2)}) %copy-start.1) | copy-done | bytes 1048600
  102.8 2.1 %finish.1 = bf16[128,2,2048]{2,1,0:T(2,128)(2,1)} custom-call(bf16[256,2048]{1,0:T(8,128)(2,1)S(1)} %copy-done, bf16[16,16,2048]{2,1,0:T(8,128)(2,1)S(1)} %copy-done.1, f32[256,128]{1,0:T(8,128)S(1)} %copy-done.2, f32[256,128]{1,0:T(8,128)S(1)} %collective-permute-done.6.rest_1_, f32[256,128]{1,0:T(8,128)S(1)} %collective-permute-done.7.rest_2_, ...), custom_call_target="tpu_custom_call" | custom-call | tf_op jit(solution)/shard_map/finish/pallas_call | solution.py:353
  (2 shorter events, 0.0 us)
Async XLA Ops:
  0.9 14.4 %copy-start.6 = (s32[16]{0:T(128)}, s32[16]{0:T(128)S(1)}, u32[]{:S(2)}) copy-start(s32[16]{0:T(128)S(1)} %select_reduce_fusion.rows_ref) | copy-start | bytes 196
  0.9 7.5 %collective-permute-start.2 = (s32[16]{0:T(128)S(1)}, s32[16]{0:T(128)S(1)}, u32[]{:S(2)}, u32[]{:S(2)}) collective-permute-start(s32[16]{0:T(128)S(1)} %select_reduce_fusion.rows_ref), channel_id=1, source_target_pairs={{0,12},{4,8},{8,4},{12,0},{1,13},{5,9},{9,5},{13,1},{2,14},{6,10},... | collective-permute-start | bytes 200 | tf_op jit(solution)/shard_map/ppermute | solution.py:403
  6.0 4.4 %collective-permute-start.1 = (s32[16]{0:T(128)S(1)}, s32[16]{0:T(128)S(1)}, u32[]{:S(2)}, u32[]{:S(2)}) collective-permute-start(s32[16]{0:T(128)S(1)} %select_reduce_fusion.rows_ref), channel_id=1, source_target_pairs={{0,8},{4,12},{8,0},{12,4},{1,9},{5,13},{9,1},{13,5},{2,10},{6,14},... | collective-permute-start | bytes 200 | tf_op jit(solution)/shard_map/ppermute | solution.py:403
  6.0 4.4 %collective-permute-start = (s32[16]{0:T(128)S(1)}, s32[16]{0:T(128)S(1)}, u32[]{:S(2)}, u32[]{:S(2)}) collective-permute-start(s32[16]{0:T(128)S(1)} %select_reduce_fusion.rows_ref), channel_id=1, source_target_pairs={{0,4},{4,0},{8,12},{12,8},{1,5},{5,1},{9,13},{13,9},{2,6},{6,2},{1... | collective-permute-start | bytes 200 | tf_op jit(solution)/shard_map/ppermute | solution.py:403
  15.3 4.8 %copy-start.7 = (s32[128]{0:T(128)S(1)}, s32[128]{0:T(128)}, u32[]{:S(2)}) copy-start(s32[128]{0:T(128)} %param.14) | copy-start | bytes 1540
  15.3 4.9 %copy-start.5 = (bf16[128,2,1024]{2,1,0:T(2,128)(2,1)S(1)}, bf16[128,2,1024]{2,1,0:T(2,128)(2,1)}, u32[]{:S(2)}) copy-start(bf16[128,2,1024]{2,1,0:T(2,128)(2,1)} %param.10) | copy-start | bytes 1572868
  15.3 74.4 %all-to-all-start = ((bf16[4,8,16,3072]{3,2,1,0:T(8,128)(2,1)}), bf16[4,8,16,3072]{3,2,1,0:T(8,128)(2,1)}, u32[]{:S(2)}, u32[]{:S(2)}) async-start(bf16[4,8,16,3072]{3,2,1,0:T(8,128)(2,1)} %pack.1), calls=%async_computation | async-start | bytes 6291456 | tf_op jit(solution)/shard_map/all_to_all | solution.py:408
  42.8 2.9 %collective-permute-start.3 = (bf16[256,2048]{1,0:T(8,128)(2,1)}, bf16[256,2048]{1,0:T(8,128)(2,1)S(1)}, u32[]{:S(2)}, u32[]{:S(2)}) collective-permute-start(bf16[256,2048]{1,0:T(8,128)(2,1)} %get-tuple-element.15), channel_id=1, source_target_pairs={{0,1},{1,0},{2,3},{3,2},{4,5},{5,4},{6,7},{7,6},{8,9},{9,8},{10,11... | collective-permute-start | bytes 3145736 | tf_op jit(solution)/shard_map/ppermute | solution.py:430
  42.9 6.1 %collective-permute-start.4 = (bf16[256,2048]{1,0:T(8,128)(2,1)}, bf16[256,2048]{1,0:T(8,128)(2,1)S(1)}, u32[]{:S(2)}, u32[]{:S(2)}) collective-permute-start(bf16[256,2048]{1,0:T(8,128)(2,1)} %get-tuple-element.17), channel_id=1, source_target_pairs={{0,1},{1,0},{2,3},{3,2},{4,5},{5,4},{6,7},{7,6},{8,9},{9,8},{10,11... | collective-permute-start | bytes 3145736 | tf_op jit(solution)/shard_map/ppermute | solution.py:430
  47.4 25.3 %collective-permute-start.5 = (bf16[256,2048]{1,0:T(8,128)(2,1)S(1)}, bf16[256,2048]{1,0:T(8,128)(2,1)S(1)}, u32[]{:S(2)}, u32[]{:S(2)}) collective-permute-start(bf16[256,2048]{1,0:T(8,128)(2,1)S(1)} %add_convert_fusion), channel_id=1, source_target_pairs={{0,2},{1,3},{2,0},{3,1},{4,6},{5,7},{6,4},{7,5},{8,10},{9,11},{10,... | collective-permute-start | bytes 3145736 | tf_op jit(solution)/shard_map/ppermute | solution.py:439
  49.0 23.7 %copy-start.3 = (bf16[256,2048]{1,0:T(8,128)(2,1)}, bf16[256,2048]{1,0:T(8,128)(2,1)S(1)}, u32[]{:S(2)}) copy-start(bf16[256,2048]{1,0:T(8,128)(2,1)S(1)} %collective-permute-done.4.rest_0_) | copy-start | bytes 3145732
  72.7 1.0 copy-start.4
  78.2 23.4 %copy-start = (bf16[256,2048]{1,0:T(8,128)(2,1)S(1)}, bf16[256,2048]{1,0:T(8,128)(2,1)}, u32[]{:S(2)}) copy-start(bf16[256,2048]{1,0:T(8,128)(2,1)} %project.1.base_ref) | copy-start | bytes 3145732
  93.0 8.6 %copy-start.2 = (f32[256,128]{1,0:T(8,128)S(1)}, f32[256,128]{1,0:T(8,128)}, u32[]{:S(2)}) copy-start(f32[256,128]{1,0:T(8,128)} %low_rank.1.rest_0_) | copy-start | bytes 393220
  93.0 5.5 %collective-permute-start.6 = (f32[256,128]{1,0:T(8,128)}, f32[256,128]{1,0:T(8,128)S(1)}, u32[]{:S(2)}, u32[]{:S(2)}) collective-permute-start(f32[256,128]{1,0:T(8,128)} %low_rank.1.rest_0_), channel_id=1, source_target_pairs={{0,1},{1,0},{2,3},{3,2},{4,5},{5,4},{6,7},{7,6},{8,9},{9,8},{10,11... | collective-permute-start | bytes 393224 | tf_op jit(solution)/shard_map/ppermute | solution.py:446
  93.0 6.5 %collective-permute-start.7 = (f32[256,128]{1,0:T(8,128)}, f32[256,128]{1,0:T(8,128)S(1)}, u32[]{:S(2)}, u32[]{:S(2)}) collective-permute-start(f32[256,128]{1,0:T(8,128)} %low_rank.1.rest_0_), channel_id=1, source_target_pairs={{0,2},{1,3},{2,0},{3,1},{4,6},{5,7},{6,4},{7,5},{8,10},{9,11},{10,... | collective-permute-start | bytes 393224 | tf_op jit(solution)/shard_map/ppermute | solution.py:446
  94.5 7.0 %collective-permute-start.8 = (f32[256,128]{1,0:T(8,128)}, f32[256,128]{1,0:T(8,128)S(1)}, u32[]{:S(2)}, u32[]{:S(2)}) collective-permute-start(f32[256,128]{1,0:T(8,128)} %low_rank.1.rest_0_), channel_id=1, source_target_pairs={{0,3},{1,2},{2,1},{3,0},{4,7},{5,6},{6,5},{7,4},{8,11},{9,10},{10,... | collective-permute-start | bytes 393224 | tf_op jit(solution)/shard_map/ppermute | solution.py:446
  101.6 1.2 %copy-start.1 = (bf16[16,16,2048]{2,1,0:T(8,128)(2,1)S(1)}, bf16[16,16,2048]{2,1,0:T(8,128)(2,1)}, u32[]{:S(2)}) copy-start(bf16[16,16,2048]{2,1,0:T(8,128)(2,1)} %chosen.1.up_ref) | copy-start | bytes 3145732

commit v4 on v3

--- a/solution.py
+++ b/solution.py
@@ -275,12 +275,21 @@
     return lax.rem(row, forks) // batch_forks == column // rank
 
 
+def each_rank(batches, rank):
+    k = lax.broadcasted_iota(jnp.int32, (rank, batches * rank), 0)
+    column = lax.broadcasted_iota(jnp.int32, (rank, batches * rank), 1)
+    return lax.rem(column, rank) == k
+
+
 def fold(every, rows, forks, batches, rank):
     every = jnp.where(batch_mask(rows, forks, batches, rank), every, 0.0)
-    total = every[:, 0:HD]
-    for c in range(1, batches * rank // HD):
-        total = total + every[:, c * HD : (c + 1) * HD]
-    return total
+    return lax.dot_general(
+        each_rank(batches, rank).astype(F32),
+        every,
+        (((1,), (1,)), ((), ())),
+        precision=lax.Precision.HIGHEST,
+        preferred_element_type=F32,
+    )
 
 
 def low_rank(attended, forks, own_rows, stored, arrived):
@@ -300,10 +309,10 @@
 
     return pl.pallas_call(
         kernel,
-        out_shape=jax.ShapeDtypeStruct((rows, HD), F32),
+        out_shape=jax.ShapeDtypeStruct((rank, rows), F32),
         grid=(1,),
         in_specs=[SMEM, whole(attended.shape), columns(arrived, depth, (arrived.shape[3] - depth) // depth)],
-        out_specs=whole((rows, HD)),
+        out_specs=whole((rank, rows)),
         scratch_shapes=[pltpu.VMEM((batches, rank, depth), BF16)],
         compiler_params=PARAMS,
         name="low_rank",
@@ -313,6 +322,7 @@
 def chosen(own_rows, stored, arrived, width):
     batches = own_rows.shape[0]
     rank = arrived.shape[2]
+    tile = min(width, 1024)
 
     def kernel(rows_ref, arrived_ref, o_ref):
         collect(rows_ref, stored, arrived_ref, o_ref)
@@ -320,9 +330,9 @@
     return pl.pallas_call(
         kernel,
         out_shape=jax.ShapeDtypeStruct((batches, rank, width), BF16),
-        grid=(1,),
-        in_specs=[SMEM, columns(arrived, width, 0)],
-        out_specs=whole((batches, rank, width)),
+        grid=(width // tile,),
+        in_specs=[SMEM, pl.BlockSpec(arrived.shape[:3] + (tile,), lambda i: (0, 0, 0, i))],
+        out_specs=pl.BlockSpec((batches, rank, tile), lambda i: (0, 0, i)),
         compiler_params=PARAMS,
         name="chosen",
     )(own_rows, arrived)
@@ -339,10 +349,17 @@
         total = rank_refs[0][...]
         for r in rank_refs[1:]:
             total = total + r[...]
-        spread = jnp.concatenate([total] * (batches * rank // HD), axis=1)
-        spread = jnp.where(batch_mask(rows, forks, batches, rank), spread, 0.0)
-        high = spread.astype(BF16)
-        low = (spread - high.astype(F32)).astype(BF16)
+        total = total.T
+        copies = each_rank(batches, rank).astype(BF16)
+        mask = batch_mask(rows, forks, batches, rank)
+
+        def spread(term):
+            wide = jnp.dot(term, copies, preferred_element_type=F32)
+            return jnp.where(mask, wide, 0.0).astype(BF16)
+
+        first = total.astype(BF16)
+        high = spread(first)
+        low = spread((total - first.astype(F32)).astype(BF16))
         columns = up_ref[...].reshape(batches * rank, tile)
         out = jnp.dot(high, columns, preferred_element_type=F32)
         out = out + jnp.dot(low, columns, preferred_element_type=F32)

time: 105 us -> 103 us (0.981)
  waiting for transfers between devices: 42.7 us -> 39.6 us
  Pallas kernels: 38.2 us -> 39.4 us
    ppermute x3, waiting for transfers between devices: 3.09 us -> 0.01 us  [body(): lax.ppermute(rank_part, 'tensor', [(t, t ^ e) for t in range(2 * chips)])]
  transfers between devices with their start and end apart: 10 -> 10, of which waited for: 6 -> 4; matrix products, arithmetic and copies ran while one was open for 5% -> 6% of each run, Pallas kernels for 27% -> 28%
where the time goes in v4:
time: 103 us
  waiting for transfers between devices  39.6 us (38%)
  Pallas kernels  39.4 us (38%)
  starting transfers between devices  14.5 us (14%)
  local copies, waits for them, and re-layouts  5.7 us (6%)
  other arithmetic  3.69 us (4%)
    ppermute x1, waiting for transfers between devices, body(): sums.append(lax.ppermute(part, 'tensor', along(e)))  23.7 us
    pallas_call x1, Pallas kernels, attention(): pl.pallas_call(functools.partial(attention_kernel, unit_heads, key_block)...  20.3 us
    all_to_all x1, waiting for transfers between devices, body(): arrived = lax.all_to_all(packed, 'replica', 0, 0)  11.4 us
    ppermute x3, starting transfers between devices, body(): lax.ppermute(own_rows, 'replica', [(z, z ^ d) for z in range(replicas)])  5.76 us
    all_to_all x1, starting transfers between devices, body(): arrived = lax.all_to_all(packed, 'replica', 0, 0)  4.8 us
    pallas_call x1, Pallas kernels, project(): pl.pallas_call(kernel, out_shape=jax.ShapeDtypeStruct((rows, width), dtyp...  4.53 us
    pallas_call x1, Pallas kernels, pack(): pl.pallas_call(kernel, out_shape=jax.ShapeDtypeStruct((replicas, capacity...  4.27 us
    pallas_call x1, Pallas kernels, chosen(): pl.pallas_call(kernel, out_shape=jax.ShapeDtypeStruct((batches, rank, wid...  4.04 us
  transfers between devices with their start and end apart: 10, of which 4 were waited for; matrix products, arithmetic and copies ran while one was open for 6% of the time, Pallas kernels for 28%

profile of v4, /device:TPU:0, one launch (start us, length us, event | category | flops | bytes accessed | tf_op | source)
XLA Modules:
  0.0 103.1 jit_solution(16147358030161230135)
XLA Ops:
  0.0 0.9 select_reduce_fusion.rows_ref
  0.9 0.0 copy-start.6
  0.9 5.1 %collective-permute-start.2 = (s32[16]{0:T(128)S(1)}, s32[16]{0:T(128)S(1)}, u32[]{:S(2)}, u32[]{:S(2)}) collective-permute-start(s32[16]{0:T(128)S(1)} %select_reduce_fusion.rows_ref), channel_id=1, source_target_pairs={{0,12},{4,8},{8,4},{12,0},{1,13},{5,9},{9,5},{13,1},{2,14},{6,10},... | collective-permute-start | bytes 200 | tf_op jit(solution)/shard_map/ppermute | solution.py:420
  6.0 0.0 collective-permute-start.1
  6.0 0.6 collective-permute-start
  6.6 1.7 %copy_bitcast_fusion.1 = (bf16[2,128,256]{2,1,0:T(8,128)(2,1)}, bf16[2,128,256]{2,1,0:T(8,128)(2,1)}) fusion(bf16[128,2,256]{2,1,0:T(2,128)(2,1)} %param.12, bf16[128,2,256]{2,1,0:T(2,128)(2,1)} %param.11), kind=kLoop, calls=%fused_computation.2 | loop fusion | bytes 524288 | tf_op jit(solution)/shard_map/transpose | solution.py:435
  8.3 0.0 collective-permute-done.2
  8.3 2.1 %collective-permute-done.1 = s32[16]{0:T(128)S(1)} collective-permute-done((s32[16]{0:T(128)S(1)}, s32[16]{0:T(128)S(1)}, u32[]{:S(2)}, u32[]{:S(2)}) %collective-permute-start.1) | collective-permute-done | bytes 96 | tf_op jit(solution)/shard_map/ppermute | solution.py:420
  10.4 0.0 collective-permute-done
  10.4 0.6 pad_add_fusion.rows_ref
  11.0 4.3 %pack.1 = bf16[4,8,16,3072]{3,2,1,0:T(8,128)(2,1)} custom-call(s32[4,16]{1,0:T(4,128)} %pad_add_fusion.rows_ref, s32[1]{0:T(128)} %bitcast.8.place_ref, bf16[16,16,2048]{2,1,0:T(8,128)(2,1)} %refs_0_.1, bf16[16,16,1024]{2,1,0:T(8,128)(2,1)} %refs_1_.1), custom_call_target="tpu_custom_call" | custom-call | tf_op jit(solution)/shard_map/pack/pallas_call | solution.py:229
  15.3 0.0 copy-start.7
  15.3 0.0 copy-start.5
  15.3 0.0 copy-done.6
  15.3 4.8 %all-to-all-start = ((bf16[4,8,16,3072]{3,2,1,0:T(8,128)(2,1)}), bf16[4,8,16,3072]{3,2,1,0:T(8,128)(2,1)}, u32[]{:S(2)}, u32[]{:S(2)}) async-start(bf16[4,8,16,3072]{3,2,1,0:T(8,128)(2,1)} %pack.1), calls=%async_computation | async-start | bytes 6291456 | tf_op jit(solution)/shard_map/all_to_all | solution.py:425
  20.1 0.0 copy-done.7
  20.1 0.0 copy-done.5
  20.2 0.9 copy.25
  21.1 0.8 copy.21.lens_ref
  21.9 0.6 pad_add_fusion.2.groups_ref
  22.5 20.3 %attention.1 = (bf16[256,1024]{1,0:T(8,128)(2,1)}, bf16[256,2048]{1,0:T(8,128)(2,1)}, bf16[256,2048]{1,0:T(8,128)(2,1)}, bf16[256,2048]{1,0:T(8,128)(2,1)}) custom-call(s32[3]{0:T(128)} %pad_add_fusion.2.groups_ref, bf16[2,128,1024]{2,1,0:T(8,128)(2,1)} %bitcast.17, bf16[2,128,256]{2,1,0:T(8,128)(2,1)} %get-tuple-element.20.rk_ref, ...), custom_call_target="tpu_custom_call" | custom-call | flops 20000000000 | bytes 6291456 | tf_op jit(solution)/shard_map/attention/pallas_call | solution.py:147
  42.8 0.1 collective-permute-start.3
  42.9 0.5 collective-permute-start.4
  43.4 2.4 %collective-permute-done.3 = bf16[256,2048]{1,0:T(8,128)(2,1)S(1)} collective-permute-done((bf16[256,2048]{1,0:T(8,128)(2,1)}, bf16[256,2048]{1,0:T(8,128)(2,1)S(1)}, u32[]{:S(2)}, u32[]{:S(2)}) %collective-permute-start.3) | collective-permute-done | bytes 1048608 | tf_op jit(solution)/shard_map/ppermute | solution.py:447
  45.7 1.6 %add_convert_fusion = bf16[256,2048]{1,0:T(8,128)(2,1)S(1)} fusion(bf16[256,2048]{1,0:T(8,128)(2,1)S(1)} %collective-permute-done.3, bf16[256,2048]{1,0:T(8,128)(2,1)} %get-tuple-element.14), kind=kLoop, calls=%fused_computation | loop fusion | flops 2097152 | bytes 3145728 | tf_op jit(solution)/shard_map/convert_element_type | solution.py:455
  47.4 1.6 %collective-permute-start.5 = (bf16[256,2048]{1,0:T(8,128)(2,1)S(1)}, bf16[256,2048]{1,0:T(8,128)(2,1)S(1)}, u32[]{:S(2)}, u32[]{:S(2)}) collective-permute-start(bf16[256,2048]{1,0:T(8,128)(2,1)S(1)} %add_convert_fusion), channel_id=1, source_target_pairs={{0,2},{1,3},{2,0},{3,1},{4,6},{5,7},{6,4},{7,5},{8,10},{9,11},{10,... | collective-permute-start | bytes 3145736 | tf_op jit(solution)/shard_map/ppermute | solution.py:456
  48.9 0.0 collective-permute-done.4.rest_0_
  48.9 0.0 copy-start.3
  48.9 23.7 %collective-permute-done.5.rest_1_ = bf16[256,2048]{1,0:T(8,128)(2,1)S(1)} collective-permute-done((bf16[256,2048]{1,0:T(8,128)(2,1)S(1)}, bf16[256,2048]{1,0:T(8,128)(2,1)S(1)}, u32[]{:S(2)}, u32[]{:S(2)}) %collective-permute-start.5) | collective-permute-done | bytes 1048608 | tf_op jit(solution)/shard_map/ppermute | solution.py:456
  72.7 0.0 copy-start.4
  72.7 0.0 copy-done.3
  72.7 1.0 copy-done.4
  73.7 4.5 %project.1.base_ref = bf16[256,2048]{1,0:T(8,128)(2,1)} custom-call(s32[1]{0:T(128)} %bitcast.group_ref, bf16[256,1024]{1,0:T(8,128)(2,1)} %get-tuple-element.18.a_ref, bf16[1024,8192]{1,0:T(8,128)(2,1)} %w_ref.3, bf16[256,2048]{1,0:T(8,128)(2,1)} %copy-done.3, bf16[256,2048]{1,0:T(8,128)(2,1)} %copy-done.4), custom_call_target="tpu_custom_call" | custom-call | flops 1073741824 | bytes 4194304 | tf_op jit(solution)/shard_map/project/pallas_call | solution.py:188
  78.2 0.0 copy-start
  78.2 11.4 %all-to-all-done.arrived_ref = bf16[4,8,16,3072]{3,2,1,0:T(8,128)(2,1)} async-done(((bf16[4,8,16,3072]{3,2,1,0:T(8,128)(2,1)}), bf16[4,8,16,3072]{3,2,1,0:T(8,128)(2,1)}, u32[]{:S(2)}, u32[]{:S(2)}) %all-to-all-start) | async-done | bytes 3145760 | tf_op jit(solution)/shard_map/all_to_all | solution.py:425
  89.7 3.8 %low_rank.1.rest_0_ = f32[16,256]{1,0:T(8,128)} custom-call(s32[16]{0:T(128)} %copy-done.6, bf16[256,1024]{1,0:T(8,128)(2,1)} %get-tuple-element.18.a_ref, bf16[4,8,16,3072]{3,2,1,0:T(8,128)(2,1)} %all-to-all-done.arrived_ref), custom_call_target="tpu_custom_call" | custom-call | tf_op jit(solution)/shard_map/low_rank/pallas_call | solution.py:310
  93.5 0.0 collective-permute-start.6
  93.5 1.5 %collective-permute-start.7 = (f32[16,256]{1,0:T(8,128)}, f32[16,256]{1,0:T(8,128)S(1)}, u32[]{:S(2)}, u32[]{:S(2)}) collective-permute-start(f32[16,256]{1,0:T(8,128)} %low_rank.1.rest_0_), channel_id=1, source_target_pairs={{0,2},{1,3},{2,0},{3,1},{4,6},{5,7},{6,4},{7,5},{8,10},{9,11},{10,... | collective-permute-start | bytes 49160 | tf_op jit(solution)/shard_map/ppermute | solution.py:463
  95.0 0.4 collective-permute-start.8
  95.4 4.0 %chosen.1.up_ref = bf16[16,16,2048]{2,1,0:T(8,128)(2,1)} custom-call(s32[16]{0:T(128)} %copy-done.6, bf16[4,8,16,3072]{3,2,1,0:T(8,128)(2,1)} %all-to-all-done.arrived_ref), custom_call_target="tpu_custom_call" | custom-call | tf_op jit(solution)/shard_map/chosen/pallas_call | solution.py:330
  99.4 0.0 collective-permute-done.6.rest_1_
  99.4 0.0 collective-permute-done.7.rest_2_
  99.4 0.0 collective-permute-done.8.rest_3_
  99.4 0.0 copy-done
  99.4 0.0 copy-done.2
  99.4 0.0 copy-start.1
  99.5 1.2 %copy-done.1 = bf16[16,16,2048]{2,1,0:T(8,128)(2,1)S(1)} copy-done((bf16[16,16,2048]{2,1,0:T(8,128)(2,1)S(1)}, bf16[16,16,2048]{2,1,0:T(8,128)(2,1)}, u32[]{:S(2)}) %copy-start.1) | copy-done | bytes 1048600
  100.7 2.5 %finish.1 = bf16[128,2,2048]{2,1,0:T(2,128)(2,1)} custom-call(bf16[256,2048]{1,0:T(8,128)(2,1)S(1)} %copy-done, bf16[16,16,2048]{2,1,0:T(8,128)(2,1)S(1)} %copy-done.1, f32[16,256]{1,0:T(8,128)S(1)} %copy-done.2, f32[16,256]{1,0:T(8,128)S(1)} %collective-permute-done.6.rest_1_, f32[16,256]{1,0:T(8,128)S(1)} %collective-permute-done.7.rest_2_, ...), custom_call_target="tpu_custom_call" | custom-call | tf_op jit(solution)/shard_map/finish/pallas_call | solution.py:370
  (2 shorter events, 0.0 us)
Async XLA Ops:
  0.9 14.4 %copy-start.6 = (s32[16]{0:T(128)}, s32[16]{0:T(128)S(1)}, u32[]{:S(2)}) copy-start(s32[16]{0:T(128)S(1)} %select_reduce_fusion.rows_ref) | copy-start | bytes 196
  0.9 7.5 %collective-permute-start.2 = (s32[16]{0:T(128)S(1)}, s32[16]{0:T(128)S(1)}, u32[]{:S(2)}, u32[]{:S(2)}) collective-permute-start(s32[16]{0:T(128)S(1)} %select_reduce_fusion.rows_ref), channel_id=1, source_target_pairs={{0,12},{4,8},{8,4},{12,0},{1,13},{5,9},{9,5},{13,1},{2,14},{6,10},... | collective-permute-start | bytes 200 | tf_op jit(solution)/shard_map/ppermute | solution.py:420
  6.0 4.4 %collective-permute-start.1 = (s32[16]{0:T(128)S(1)}, s32[16]{0:T(128)S(1)}, u32[]{:S(2)}, u32[]{:S(2)}) collective-permute-start(s32[16]{0:T(128)S(1)} %select_reduce_fusion.rows_ref), channel_id=1, source_target_pairs={{0,8},{4,12},{8,0},{12,4},{1,9},{5,13},{9,1},{13,5},{2,10},{6,14},... | collective-permute-start | bytes 200 | tf_op jit(solution)/shard_map/ppermute | solution.py:420
  6.0 4.4 %collective-permute-start = (s32[16]{0:T(128)S(1)}, s32[16]{0:T(128)S(1)}, u32[]{:S(2)}, u32[]{:S(2)}) collective-permute-start(s32[16]{0:T(128)S(1)} %select_reduce_fusion.rows_ref), channel_id=1, source_target_pairs={{0,4},{4,0},{8,12},{12,8},{1,5},{5,1},{9,13},{13,9},{2,6},{6,2},{1... | collective-permute-start | bytes 200 | tf_op jit(solution)/shard_map/ppermute | solution.py:420
  15.3 4.8 %copy-start.7 = (s32[128]{0:T(128)S(1)}, s32[128]{0:T(128)}, u32[]{:S(2)}) copy-start(s32[128]{0:T(128)} %param.14) | copy-start | bytes 1540
  15.3 4.9 %copy-start.5 = (bf16[128,2,1024]{2,1,0:T(2,128)(2,1)S(1)}, bf16[128,2,1024]{2,1,0:T(2,128)(2,1)}, u32[]{:S(2)}) copy-start(bf16[128,2,1024]{2,1,0:T(2,128)(2,1)} %param.10) | copy-start | bytes 1572868
  15.3 74.4 %all-to-all-start = ((bf16[4,8,16,3072]{3,2,1,0:T(8,128)(2,1)}), bf16[4,8,16,3072]{3,2,1,0:T(8,128)(2,1)}, u32[]{:S(2)}, u32[]{:S(2)}) async-start(bf16[4,8,16,3072]{3,2,1,0:T(8,128)(2,1)} %pack.1), calls=%async_computation | async-start | bytes 6291456 | tf_op jit(solution)/shard_map/all_to_all | solution.py:425
  42.8 2.9 %collective-permute-start.3 = (bf16[256,2048]{1,0:T(8,128)(2,1)}, bf16[256,2048]{1,0:T(8,128)(2,1)S(1)}, u32[]{:S(2)}, u32[]{:S(2)}) collective-permute-start(bf16[256,2048]{1,0:T(8,128)(2,1)} %get-tuple-element.15), channel_id=1, source_target_pairs={{0,1},{1,0},{2,3},{3,2},{4,5},{5,4},{6,7},{7,6},{8,9},{9,8},{10,11... | collective-permute-start | bytes 3145736 | tf_op jit(solution)/shard_map/ppermute | solution.py:447
  42.9 6.0 %collective-permute-start.4 = (bf16[256,2048]{1,0:T(8,128)(2,1)}, bf16[256,2048]{1,0:T(8,128)(2,1)S(1)}, u32[]{:S(2)}, u32[]{:S(2)}) collective-permute-start(bf16[256,2048]{1,0:T(8,128)(2,1)} %get-tuple-element.17), channel_id=1, source_target_pairs={{0,1},{1,0},{2,3},{3,2},{4,5},{5,4},{6,7},{7,6},{8,9},{9,8},{10,11... | collective-permute-start | bytes 3145736 | tf_op jit(solution)/shard_map/ppermute | solution.py:447
  47.4 25.3 %collective-permute-start.5 = (bf16[256,2048]{1,0:T(8,128)(2,1)S(1)}, bf16[256,2048]{1,0:T(8,128)(2,1)S(1)}, u32[]{:S(2)}, u32[]{:S(2)}) collective-permute-start(bf16[256,2048]{1,0:T(8,128)(2,1)S(1)} %add_convert_fusion), channel_id=1, source_target_pairs={{0,2},{1,3},{2,0},{3,1},{4,6},{5,7},{6,4},{7,5},{8,10},{9,11},{10,... | collective-permute-start | bytes 3145736 | tf_op jit(solution)/shard_map/ppermute | solution.py:456
  48.9 23.7 %copy-start.3 = (bf16[256,2048]{1,0:T(8,128)(2,1)}, bf16[256,2048]{1,0:T(8,128)(2,1)S(1)}, u32[]{:S(2)}) copy-start(bf16[256,2048]{1,0:T(8,128)(2,1)S(1)} %collective-permute-done.4.rest_0_) | copy-start | bytes 3145732
  72.7 1.0 %copy-start.4 = (bf16[256,2048]{1,0:T(8,128)(2,1)}, bf16[256,2048]{1,0:T(8,128)(2,1)S(1)}, u32[]{:S(2)}) copy-start(bf16[256,2048]{1,0:T(8,128)(2,1)S(1)} %collective-permute-done.5.rest_1_) | copy-start | bytes 3145732
  78.2 21.2 %copy-start = (bf16[256,2048]{1,0:T(8,128)(2,1)S(1)}, bf16[256,2048]{1,0:T(8,128)(2,1)}, u32[]{:S(2)}) copy-start(bf16[256,2048]{1,0:T(8,128)(2,1)} %project.1.base_ref) | copy-start | bytes 3145732
  93.5 5.9 %copy-start.2 = (f32[16,256]{1,0:T(8,128)S(1)}, f32[16,256]{1,0:T(8,128)}, u32[]{:S(2)}) copy-start(f32[16,256]{1,0:T(8,128)} %low_rank.1.rest_0_) | copy-start | bytes 49156
  93.5 5.9 %collective-permute-start.6 = (f32[16,256]{1,0:T(8,128)}, f32[16,256]{1,0:T(8,128)S(1)}, u32[]{:S(2)}, u32[]{:S(2)}) collective-permute-start(f32[16,256]{1,0:T(8,128)} %low_rank.1.rest_0_), channel_id=1, source_target_pairs={{0,1},{1,0},{2,3},{3,2},{4,5},{5,4},{6,7},{7,6},{8,9},{9,8},{10,11... | collective-permute-start | bytes 49160 | tf_op jit(solution)/shard_map/ppermute | solution.py:463
  93.5 5.9 %collective-permute-start.7 = (f32[16,256]{1,0:T(8,128)}, f32[16,256]{1,0:T(8,128)S(1)}, u32[]{:S(2)}, u32[]{:S(2)}) collective-permute-start(f32[16,256]{1,0:T(8,128)} %low_rank.1.rest_0_), channel_id=1, source_target_pairs={{0,2},{1,3},{2,0},{3,1},{4,6},{5,7},{6,4},{7,5},{8,10},{9,11},{10,... | collective-permute-start | bytes 49160 | tf_op jit(solution)/shard_map/ppermute | solution.py:463
  95.0 4.4 %collective-permute-start.8 = (f32[16,256]{1,0:T(8,128)}, f32[16,256]{1,0:T(8,128)S(1)}, u32[]{:S(2)}, u32[]{:S(2)}) collective-permute-start(f32[16,256]{1,0:T(8,128)} %low_rank.1.rest_0_), channel_id=1, source_target_pairs={{0,3},{1,2},{2,1},{3,0},{4,7},{5,6},{6,5},{7,4},{8,11},{9,10},{10,... | collective-permute-start | bytes 49160 | tf_op jit(solution)/shard_map/ppermute | solution.py:463
  99.4 1.2 %copy-start.1 = (bf16[16,16,2048]{2,1,0:T(8,128)(2,1)S(1)}, bf16[16,16,2048]{2,1,0:T(8,128)(2,1)}, u32[]{:S(2)}) copy-start(bf16[16,16,2048]{2,1,0:T(8,128)(2,1)} %chosen.1.up_ref) | copy-start | bytes 3145732

commit v5 on v4

--- a/solution.py
+++ b/solution.py
@@ -237,8 +237,9 @@
     )(rows_all, place, *tables)
 
 
-def collect(rows_ref, stored, arrived_ref, selected):
-    batches = selected.shape[0]
+def collect(rows_ref, stored, arrived_ref, start, selected, sems):
+    batches, _, width = selected.shape
+    at = pl.ds(start, width)
     for owner in range(arrived_ref.shape[0]):
 
         def step(b, count):
@@ -247,25 +248,19 @@
 
             @pl.when(there)
             def _():
-                selected[b] = arrived_ref[owner, count]
+                pltpu.make_async_copy(arrived_ref.at[owner, count, :, at], selected.at[b], sems.at[b]).start()
 
             return count + there.astype(jnp.int32)
 
         lax.fori_loop(0, batches, step, jnp.int32(0))
+
+    @pl.loop(0, batches)
+    def _(b):
+        pltpu.make_async_copy(arrived_ref.at[0, 0, :, at], selected.at[b], sems.at[b]).wait()
 
 
 def whole(shape):
     return pl.BlockSpec(shape, lambda i: (0,) * len(shape))
-
-
-def columns(packed, width, block):
-    shape = packed.shape[:-1] + (width,)
-    return pl.BlockSpec(shape, lambda i: (0,) * (len(shape) - 1) + (block,))
-
-
-def columns(packed, width, block):
-    shape = packed.shape[:-1] + (width,)
-    return pl.BlockSpec(shape, lambda i: (0,) * (len(shape) - 1) + (block,))
 
 
 def batch_mask(rows, forks, batches, rank):
@@ -297,8 +292,8 @@
     batches = own_rows.shape[0]
     rank = arrived.shape[2]
 
-    def kernel(rows_ref, a_ref, arrived_ref, o_ref, selected):
-        collect(rows_ref, stored, arrived_ref, selected)
+    def kernel(rows_ref, a_ref, arrived_ref, o_ref, selected, sems):
+        collect(rows_ref, stored, arrived_ref, arrived.shape[3] - depth, selected, sems)
         every = lax.dot_general(
             a_ref[...],
             selected[...].reshape(batches * rank, depth),
@@ -310,10 +305,9 @@
     return pl.pallas_call(
         kernel,
         out_shape=jax.ShapeDtypeStruct((rank, rows), F32),
-        grid=(1,),
-        in_specs=[SMEM, whole(attended.shape), columns(arrived, depth, (arrived.shape[3] - depth) // depth)],
-        out_specs=whole((rank, rows)),
-        scratch_shapes=[pltpu.VMEM((batches, rank, depth), BF16)],
+        in_specs=[SMEM, VMEM, pl.BlockSpec(memory_space=pl.ANY)],
+        out_specs=VMEM,
+        scratch_shapes=[pltpu.VMEM((batches, rank, depth), BF16), pltpu.SemaphoreType.DMA((batches,))],
         compiler_params=PARAMS,
         name="low_rank",
     )(own_rows, attended, arrived)
@@ -322,17 +316,16 @@
 def chosen(own_rows, stored, arrived, width):
     batches = own_rows.shape[0]
     rank = arrived.shape[2]
-    tile = min(width, 1024)
-
-    def kernel(rows_ref, arrived_ref, o_ref):
-        collect(rows_ref, stored, arrived_ref, o_ref)
+
+    def kernel(rows_ref, arrived_ref, o_ref, sems):
+        collect(rows_ref, stored, arrived_ref, 0, o_ref, sems)
 
     return pl.pallas_call(
         kernel,
         out_shape=jax.ShapeDtypeStruct((batches, rank, width), BF16),
-        grid=(width // tile,),
-        in_specs=[SMEM, pl.BlockSpec(arrived.shape[:3] + (tile,), lambda i: (0, 0, 0, i))],
-        out_specs=pl.BlockSpec((batches, rank, tile), lambda i: (0, 0, i)),
+        in_specs=[SMEM, pl.BlockSpec(memory_space=pl.ANY)],
+        out_specs=VMEM,
+        scratch_shapes=[pltpu.SemaphoreType.DMA((batches,))],
         compiler_params=PARAMS,
         name="chosen",
     )(own_rows, arrived)

time: 103 us -> 103 us (level)
  transfers between devices with their start and end apart: 10 -> 10, of which waited for: 4 -> 4; matrix products, arithmetic and copies ran while one was open for 6% -> 6% of each run, Pallas kernels for 28% -> 27%
where the time goes in v5:
time: 103 us
  waiting for transfers between devices  39.6 us (38%)
  Pallas kernels  38.7 us (38%)
  starting transfers between devices  14.6 us (14%)
  local copies, waits for them, and re-layouts  5.7 us (6%)
  other arithmetic  3.69 us (4%)
    ppermute x1, waiting for transfers between devices, body(): sums.append(lax.ppermute(part, 'tensor', along(e)))  23.7 us
    pallas_call x1, Pallas kernels, attention(): pl.pallas_call(functools.partial(attention_kernel, unit_heads, key_block)...  20.3 us
    all_to_all x1, waiting for transfers between devices, body(): arrived = lax.all_to_all(packed, 'replica', 0, 0)  11.5 us
    ppermute x3, starting transfers between devices, body(): lax.ppermute(own_rows, 'replica', [(z, z ^ d) for z in range(replicas)])  5.76 us
    all_to_all x1, starting transfers between devices, body(): arrived = lax.all_to_all(packed, 'replica', 0, 0)  4.8 us
    pallas_call x1, Pallas kernels, project(): pl.pallas_call(kernel, out_shape=jax.ShapeDtypeStruct((rows, width), dtyp...  4.53 us
    pallas_call x1, Pallas kernels, pack(): pl.pallas_call(kernel, out_shape=jax.ShapeDtypeStruct((replicas, capacity...  4.27 us
    pallas_call x1, Pallas kernels, low_rank(): pl.pallas_call(kernel, out_shape=jax.ShapeDtypeStruct((rank, rows), F32),...  3.96 us
  transfers between devices with their start and end apart: 10, of which 4 were waited for; matrix products, arithmetic and copies ran while one was open for 6% of the time, Pallas kernels for 27%

profile of v5, /device:TPU:0, one launch (start us, length us, event | category | flops | bytes accessed | tf_op | source)
XLA Modules:
  0.0 102.5 jit_solution(6301951994284640644)
XLA Ops:
  0.0 0.9 select_reduce_fusion.rows_ref
  0.9 0.0 copy-start.6
  0.9 5.1 %collective-permute-start.2 = (s32[16]{0:T(128)S(1)}, s32[16]{0:T(128)S(1)}, u32[]{:S(2)}, u32[]{:S(2)}) collective-permute-start(s32[16]{0:T(128)S(1)} %select_reduce_fusion.rows_ref), channel_id=1, source_target_pairs={{0,12},{4,8},{8,4},{12,0},{1,13},{5,9},{9,5},{13,1},{2,14},{6,10},... | collective-permute-start | bytes 200 | tf_op jit(solution)/shard_map/ppermute | solution.py:413
  6.0 0.0 collective-permute-start.1
  6.0 0.6 collective-permute-start
  6.6 1.7 %copy_bitcast_fusion.1 = (bf16[2,128,256]{2,1,0:T(8,128)(2,1)}, bf16[2,128,256]{2,1,0:T(8,128)(2,1)}) fusion(bf16[128,2,256]{2,1,0:T(2,128)(2,1)} %param.12, bf16[128,2,256]{2,1,0:T(2,128)(2,1)} %param.11), kind=kLoop, calls=%fused_computation.2 | loop fusion | bytes 524288 | tf_op jit(solution)/shard_map/transpose | solution.py:428
  8.3 0.0 collective-permute-done.2
  8.3 2.1 %collective-permute-done.1 = s32[16]{0:T(128)S(1)} collective-permute-done((s32[16]{0:T(128)S(1)}, s32[16]{0:T(128)S(1)}, u32[]{:S(2)}, u32[]{:S(2)}) %collective-permute-start.1) | collective-permute-done | bytes 96 | tf_op jit(solution)/shard_map/ppermute | solution.py:413
  10.4 0.0 collective-permute-done
  10.4 0.6 pad_add_fusion.rows_ref
  11.0 4.3 %pack.1 = bf16[4,8,16,3072]{3,2,1,0:T(8,128)(2,1)} custom-call(s32[4,16]{1,0:T(4,128)} %pad_add_fusion.rows_ref, s32[1]{0:T(128)} %bitcast.8.place_ref, bf16[16,16,2048]{2,1,0:T(8,128)(2,1)} %refs_0_.1, bf16[16,16,1024]{2,1,0:T(8,128)(2,1)} %refs_1_.1), custom_call_target="tpu_custom_call" | custom-call | tf_op jit(solution)/shard_map/pack/pallas_call | solution.py:229
  15.3 0.0 copy-start.7
  15.3 0.0 copy-start.5
  15.3 0.0 copy-done.6
  15.3 4.8 %all-to-all-start = ((bf16[4,8,16,3072]{3,2,1,0:T(8,128)(2,1)}), bf16[4,8,16,3072]{3,2,1,0:T(8,128)(2,1)}, u32[]{:S(2)}, u32[]{:S(2)}) async-start(bf16[4,8,16,3072]{3,2,1,0:T(8,128)(2,1)} %pack.1), calls=%async_computation | async-start | bytes 6291456 | tf_op jit(solution)/shard_map/all_to_all | solution.py:418
  20.1 0.0 copy-done.7
  20.2 0.0 copy-done.5
  20.2 0.9 copy.25
  21.1 0.8 copy.21.lens_ref
  21.9 0.6 pad_add_fusion.2.groups_ref
  22.5 20.3 %attention.1 = (bf16[256,1024]{1,0:T(8,128)(2,1)}, bf16[256,2048]{1,0:T(8,128)(2,1)}, bf16[256,2048]{1,0:T(8,128)(2,1)}, bf16[256,2048]{1,0:T(8,128)(2,1)}) custom-call(s32[3]{0:T(128)} %pad_add_fusion.2.groups_ref, bf16[2,128,1024]{2,1,0:T(8,128)(2,1)} %bitcast.17, bf16[2,128,256]{2,1,0:T(8,128)(2,1)} %get-tuple-element.20.rk_ref, ...), custom_call_target="tpu_custom_call" | custom-call | flops 20000000000 | bytes 6291456 | tf_op jit(solution)/shard_map/attention/pallas_call | solution.py:147
  42.8 0.1 collective-permute-start.3
  42.9 0.5 collective-permute-start.4
  43.4 2.4 %collective-permute-done.3 = bf16[256,2048]{1,0:T(8,128)(2,1)S(1)} collective-permute-done((bf16[256,2048]{1,0:T(8,128)(2,1)}, bf16[256,2048]{1,0:T(8,128)(2,1)S(1)}, u32[]{:S(2)}, u32[]{:S(2)}) %collective-permute-start.3) | collective-permute-done | bytes 1048608 | tf_op jit(solution)/shard_map/ppermute | solution.py:440
  45.7 1.6 %add_convert_fusion = bf16[256,2048]{1,0:T(8,128)(2,1)S(1)} fusion(bf16[256,2048]{1,0:T(8,128)(2,1)S(1)} %collective-permute-done.3, bf16[256,2048]{1,0:T(8,128)(2,1)} %get-tuple-element.14), kind=kLoop, calls=%fused_computation | loop fusion | flops 2097152 | bytes 3145728 | tf_op jit(solution)/shard_map/convert_element_type | solution.py:448
  47.4 1.6 %collective-permute-start.5 = (bf16[256,2048]{1,0:T(8,128)(2,1)S(1)}, bf16[256,2048]{1,0:T(8,128)(2,1)S(1)}, u32[]{:S(2)}, u32[]{:S(2)}) collective-permute-start(bf16[256,2048]{1,0:T(8,128)(2,1)S(1)} %add_convert_fusion), channel_id=1, source_target_pairs={{0,2},{1,3},{2,0},{3,1},{4,6},{5,7},{6,4},{7,5},{8,10},{9,11},{10,... | collective-permute-start | bytes 3145736 | tf_op jit(solution)/shard_map/ppermute | solution.py:449
  48.9 0.0 collective-permute-done.4.rest_0_
  49.0 0.0 copy-start.3
  49.0 23.7 %collective-permute-done.5.rest_1_ = bf16[256,2048]{1,0:T(8,128)(2,1)S(1)} collective-permute-done((bf16[256,2048]{1,0:T(8,128)(2,1)S(1)}, bf16[256,2048]{1,0:T(8,128)(2,1)S(1)}, u32[]{:S(2)}, u32[]{:S(2)}) %collective-permute-start.5) | collective-permute-done | bytes 1048608 | tf_op jit(solution)/shard_map/ppermute | solution.py:449
  72.7 0.0 copy-start.4
  72.7 0.0 copy-done.3
  72.7 1.0 %copy-done.4 = bf16[256,2048]{1,0:T(8,128)(2,1)} copy-done((bf16[256,2048]{1,0:T(8,128)(2,1)}, bf16[256,2048]{1,0:T(8,128)(2,1)S(1)}, u32[]{:S(2)}) %copy-start.4) | copy-done | bytes 1048600
  73.7 4.5 %project.1.base_ref = bf16[256,2048]{1,0:T(8,128)(2,1)} custom-call(s32[1]{0:T(128)} %bitcast.group_ref, bf16[256,1024]{1,0:T(8,128)(2,1)} %get-tuple-element.18.a_ref, bf16[1024,8192]{1,0:T(8,128)(2,1)} %w_ref.3, bf16[256,2048]{1,0:T(8,128)(2,1)} %copy-done.3, bf16[256,2048]{1,0:T(8,128)(2,1)} %copy-done.4), custom_call_target="tpu_custom_call" | custom-call | flops 1073741824 | bytes 4194304 | tf_op jit(solution)/shard_map/project/pallas_call | solution.py:188
  78.2 11.5 %all-to-all-done.arrived_ref = bf16[4,8,16,3072]{3,2,1,0:T(8,128)(2,1)} async-done(((bf16[4,8,16,3072]{3,2,1,0:T(8,128)(2,1)}), bf16[4,8,16,3072]{3,2,1,0:T(8,128)(2,1)}, u32[]{:S(2)}, u32[]{:S(2)}) %all-to-all-start) | async-done | bytes 3145760 | tf_op jit(solution)/shard_map/all_to_all | solution.py:418
  89.7 4.0 %low_rank.1.rest_0_ = f32[16,256]{1,0:T(8,128)} custom-call(s32[16]{0:T(128)} %copy-done.6, bf16[256,1024]{1,0:T(8,128)(2,1)} %get-tuple-element.18.a_ref, bf16[4,8,16,3072]{3,2,1,0:T(8,128)(2,1)} %all-to-all-done.arrived_ref), custom_call_target="tpu_custom_call" | custom-call | tf_op jit(solution)/shard_map/low_rank/pallas_call | solution.py:305
  93.6 0.0 copy-start.2
  93.6 0.1 collective-permute-start.6
  93.7 1.6 %collective-permute-start.7 = (f32[16,256]{1,0:T(8,128)}, f32[16,256]{1,0:T(8,128)S(1)}, u32[]{:S(2)}, u32[]{:S(2)}) collective-permute-start(f32[16,256]{1,0:T(8,128)} %low_rank.1.rest_0_), channel_id=1, source_target_pairs={{0,2},{1,3},{2,0},{3,1},{4,6},{5,7},{6,4},{7,5},{8,10},{9,11},{10,... | collective-permute-start | bytes 49160 | tf_op jit(solution)/shard_map/ppermute | solution.py:456
  95.3 0.3 collective-permute-start.8
  95.6 3.2 %chosen.1.up_ref = bf16[16,16,2048]{2,1,0:T(8,128)(2,1)} custom-call(s32[16]{0:T(128)} %copy-done.6, bf16[4,8,16,3072]{3,2,1,0:T(8,128)(2,1)} %all-to-all-done.arrived_ref), custom_call_target="tpu_custom_call" | custom-call | tf_op jit(solution)/shard_map/chosen/pallas_call | solution.py:323
  98.8 0.0 collective-permute-done.6.rest_1_
  98.8 0.0 collective-permute-done.7.rest_2_
  98.8 0.0 collective-permute-done.8.rest_3_
  98.8 0.0 copy-done
  98.9 0.0 copy-done.2
  98.9 0.0 copy-start.1
  98.9 1.2 %copy-done.1 = bf16[16,16,2048]{2,1,0:T(8,128)(2,1)S(1)} copy-done((bf16[16,16,2048]{2,1,0:T(8,128)(2,1)S(1)}, bf16[16,16,2048]{2,1,0:T(8,128)(2,1)}, u32[]{:S(2)}) %copy-start.1) | copy-done | bytes 1048600
  100.1 2.4 %finish.1 = bf16[128,2,2048]{2,1,0:T(2,128)(2,1)} custom-call(bf16[256,2048]{1,0:T(8,128)(2,1)S(1)} %copy-done, bf16[16,16,2048]{2,1,0:T(8,128)(2,1)S(1)} %copy-done.1, f32[16,256]{1,0:T(8,128)S(1)} %copy-done.2, f32[16,256]{1,0:T(8,128)S(1)} %collective-permute-done.6.rest_1_, f32[16,256]{1,0:T(8,128)S(1)} %collective-permute-done.7.rest_2_, ...), custom_call_target="tpu_custom_call" | custom-call | tf_op jit(solution)/shard_map/finish/pallas_call | solution.py:363
  (2 shorter events, 0.0 us)
Async XLA Ops:
  0.9 14.4 %copy-start.6 = (s32[16]{0:T(128)}, s32[16]{0:T(128)S(1)}, u32[]{:S(2)}) copy-start(s32[16]{0:T(128)S(1)} %select_reduce_fusion.rows_ref) | copy-start | bytes 196
  0.9 7.5 %collective-permute-start.2 = (s32[16]{0:T(128)S(1)}, s32[16]{0:T(128)S(1)}, u32[]{:S(2)}, u32[]{:S(2)}) collective-permute-start(s32[16]{0:T(128)S(1)} %select_reduce_fusion.rows_ref), channel_id=1, source_target_pairs={{0,12},{4,8},{8,4},{12,0},{1,13},{5,9},{9,5},{13,1},{2,14},{6,10},... | collective-permute-start | bytes 200 | tf_op jit(solution)/shard_map/ppermute | solution.py:413
  6.0 4.4 %collective-permute-start.1 = (s32[16]{0:T(128)S(1)}, s32[16]{0:T(128)S(1)}, u32[]{:S(2)}, u32[]{:S(2)}) collective-permute-start(s32[16]{0:T(128)S(1)} %select_reduce_fusion.rows_ref), channel_id=1, source_target_pairs={{0,8},{4,12},{8,0},{12,4},{1,9},{5,13},{9,1},{13,5},{2,10},{6,14},... | collective-permute-start | bytes 200 | tf_op jit(solution)/shard_map/ppermute | solution.py:413
  6.0 4.4 %collective-permute-start = (s32[16]{0:T(128)S(1)}, s32[16]{0:T(128)S(1)}, u32[]{:S(2)}, u32[]{:S(2)}) collective-permute-start(s32[16]{0:T(128)S(1)} %select_reduce_fusion.rows_ref), channel_id=1, source_target_pairs={{0,4},{4,0},{8,12},{12,8},{1,5},{5,1},{9,13},{13,9},{2,6},{6,2},{1... | collective-permute-start | bytes 200 | tf_op jit(solution)/shard_map/ppermute | solution.py:413
  15.3 4.8 %copy-start.7 = (s32[128]{0:T(128)S(1)}, s32[128]{0:T(128)}, u32[]{:S(2)}) copy-start(s32[128]{0:T(128)} %param.14) | copy-start | bytes 1540
  15.3 4.9 %copy-start.5 = (bf16[128,2,1024]{2,1,0:T(2,128)(2,1)S(1)}, bf16[128,2,1024]{2,1,0:T(2,128)(2,1)}, u32[]{:S(2)}) copy-start(bf16[128,2,1024]{2,1,0:T(2,128)(2,1)} %param.10) | copy-start | bytes 1572868
  15.3 74.4 %all-to-all-start = ((bf16[4,8,16,3072]{3,2,1,0:T(8,128)(2,1)}), bf16[4,8,16,3072]{3,2,1,0:T(8,128)(2,1)}, u32[]{:S(2)}, u32[]{:S(2)}) async-start(bf16[4,8,16,3072]{3,2,1,0:T(8,128)(2,1)} %pack.1), calls=%async_computation | async-start | bytes 6291456 | tf_op jit(solution)/shard_map/all_to_all | solution.py:418
  42.8 2.9 %collective-permute-start.3 = (bf16[256,2048]{1,0:T(8,128)(2,1)}, bf16[256,2048]{1,0:T(8,128)(2,1)S(1)}, u32[]{:S(2)}, u32[]{:S(2)}) collective-permute-start(bf16[256,2048]{1,0:T(8,128)(2,1)} %get-tuple-element.15), channel_id=1, source_target_pairs={{0,1},{1,0},{2,3},{3,2},{4,5},{5,4},{6,7},{7,6},{8,9},{9,8},{10,11... | collective-permute-start | bytes 3145736 | tf_op jit(solution)/shard_map/ppermute | solution.py:440
  42.9 6.1 %collective-permute-start.4 = (bf16[256,2048]{1,0:T(8,128)(2,1)}, bf16[256,2048]{1,0:T(8,128)(2,1)S(1)}, u32[]{:S(2)}, u32[]{:S(2)}) collective-permute-start(bf16[256,2048]{1,0:T(8,128)(2,1)} %get-tuple-element.17), channel_id=1, source_target_pairs={{0,1},{1,0},{2,3},{3,2},{4,5},{5,4},{6,7},{7,6},{8,9},{9,8},{10,11... | collective-permute-start | bytes 3145736 | tf_op jit(solution)/shard_map/ppermute | solution.py:440
  47.4 25.3 %collective-permute-start.5 = (bf16[256,2048]{1,0:T(8,128)(2,1)S(1)}, bf16[256,2048]{1,0:T(8,128)(2,1)S(1)}, u32[]{:S(2)}, u32[]{:S(2)}) collective-permute-start(bf16[256,2048]{1,0:T(8,128)(2,1)S(1)} %add_convert_fusion), channel_id=1, source_target_pairs={{0,2},{1,3},{2,0},{3,1},{4,6},{5,7},{6,4},{7,5},{8,10},{9,11},{10,... | collective-permute-start | bytes 3145736 | tf_op jit(solution)/shard_map/ppermute | solution.py:449
  49.0 23.7 %copy-start.3 = (bf16[256,2048]{1,0:T(8,128)(2,1)}, bf16[256,2048]{1,0:T(8,128)(2,1)S(1)}, u32[]{:S(2)}) copy-start(bf16[256,2048]{1,0:T(8,128)(2,1)S(1)} %collective-permute-done.4.rest_0_) | copy-start | bytes 3145732
  72.7 1.0 %copy-start.4 = (bf16[256,2048]{1,0:T(8,128)(2,1)}, bf16[256,2048]{1,0:T(8,128)(2,1)S(1)}, u32[]{:S(2)}) copy-start(bf16[256,2048]{1,0:T(8,128)(2,1)S(1)} %collective-permute-done.5.rest_1_) | copy-start | bytes 3145732
  78.2 20.6 %copy-start = (bf16[256,2048]{1,0:T(8,128)(2,1)S(1)}, bf16[256,2048]{1,0:T(8,128)(2,1)}, u32[]{:S(2)}) copy-start(bf16[256,2048]{1,0:T(8,128)(2,1)} %project.1.base_ref) | copy-start | bytes 3145732
  93.6 5.2 %copy-start.2 = (f32[16,256]{1,0:T(8,128)S(1)}, f32[16,256]{1,0:T(8,128)}, u32[]{:S(2)}) copy-start(f32[16,256]{1,0:T(8,128)} %low_rank.1.rest_0_) | copy-start | bytes 49156
  93.6 5.2 %collective-permute-start.6 = (f32[16,256]{1,0:T(8,128)}, f32[16,256]{1,0:T(8,128)S(1)}, u32[]{:S(2)}, u32[]{:S(2)}) collective-permute-start(f32[16,256]{1,0:T(8,128)} %low_rank.1.rest_0_), channel_id=1, source_target_pairs={{0,1},{1,0},{2,3},{3,2},{4,5},{5,4},{6,7},{7,6},{8,9},{9,8},{10,11... | collective-permute-start | bytes 49160 | tf_op jit(solution)/shard_map/ppermute | solution.py:456
  93.7 5.1 %collective-permute-start.7 = (f32[16,256]{1,0:T(8,128)}, f32[16,256]{1,0:T(8,128)S(1)}, u32[]{:S(2)}, u32[]{:S(2)}) collective-permute-start(f32[16,256]{1,0:T(8,128)} %low_rank.1.rest_0_), channel_id=1, source_target_pairs={{0,2},{1,3},{2,0},{3,1},{4,6},{5,7},{6,4},{7,5},{8,10},{9,11},{10,... | collective-permute-start | bytes 49160 | tf_op jit(solution)/shard_map/ppermute | solution.py:456
  95.3 3.6 %collective-permute-start.8 = (f32[16,256]{1,0:T(8,128)}, f32[16,256]{1,0:T(8,128)S(1)}, u32[]{:S(2)}, u32[]{:S(2)}) collective-permute-start(f32[16,256]{1,0:T(8,128)} %low_rank.1.rest_0_), channel_id=1, source_target_pairs={{0,3},{1,2},{2,1},{3,0},{4,7},{5,6},{6,5},{7,4},{8,11},{9,10},{10,... | collective-permute-start | bytes 49160 | tf_op jit(solution)/shard_map/ppermute | solution.py:456
  98.9 1.2 %copy-start.1 = (bf16[16,16,2048]{2,1,0:T(8,128)(2,1)S(1)}, bf16[16,16,2048]{2,1,0:T(8,128)(2,1)}, u32[]{:S(2)}) copy-start(bf16[16,16,2048]{2,1,0:T(8,128)(2,1)} %chosen.1.up_ref) | copy-start | bytes 3145732

commit v6 on v5

--- a/solution.py
+++ b/solution.py
@@ -308,7 +308,7 @@
         in_specs=[SMEM, VMEM, pl.BlockSpec(memory_space=pl.ANY)],
         out_specs=VMEM,
         scratch_shapes=[pltpu.VMEM((batches, rank, depth), BF16), pltpu.SemaphoreType.DMA((batches,))],
-        compiler_params=PARAMS,
+        compiler_params=SMALL_PARAMS,
         name="low_rank",
     )(own_rows, attended, arrived)
 
@@ -326,7 +326,7 @@
         in_specs=[SMEM, pl.BlockSpec(memory_space=pl.ANY)],
         out_specs=VMEM,
         scratch_shapes=[pltpu.SemaphoreType.DMA((batches,))],
-        compiler_params=PARAMS,
+        compiler_params=SMALL_PARAMS,
         name="chosen",
     )(own_rows, arrived)
 

time: 103 us -> 100 us (0.971)
  waiting for transfers between devices: 39.6 us -> 38.1 us
    all_to_all x1, waiting for transfers between devices: 11.5 us -> 8.5 us  [body(): arrived = lax.all_to_all(packed, 'replica', 0, 0)]
    pallas_call x1, Pallas kernels: 20.3 us -> 21.3 us  [attention(): pl.pallas_call(functools.partial(attention_kernel, unit_heads, key_block)...]
    unnamed x17 -> x7, local copies, waits for them, and re-layouts: 3.2 us -> 3.05 us
  transfers between devices with their start and end apart: 10 -> 10, of which waited for: 4 -> 5; matrix products, arithmetic and copies ran while one was open for 6% -> 8% of each run, Pallas kernels for 27% -> 28%
where the time goes in v6:
time: 100 us; the launch traced here: 99.8 us
  waiting for transfers between devices  38.1 us (38%)
  Pallas kernels  37.9 us (38%)
  starting transfers between devices  13.6 us (14%)
  local copies, waits for them, and re-layouts  5.55 us (6%)
  other arithmetic  4.58 us (5%)
    ppermute x1, waiting for transfers between devices, body(): sums.append(lax.ppermute(part, 'tensor', along(e)))  24 us
    pallas_call x1, Pallas kernels, attention(): pl.pallas_call(functools.partial(attention_kernel, unit_heads, key_block)...  21.3 us
    all_to_all x1, waiting for transfers between devices, body(): arrived = lax.all_to_all(packed, 'replica', 0, 0)  8.5 us
    ppermute x3, starting transfers between devices, body(): lax.ppermute(own_rows, 'replica', [(z, z ^ d) for z in range(replicas)])  5.75 us
    pallas_call x1, Pallas kernels, project(): pl.pallas_call(kernel, out_shape=jax.ShapeDtypeStruct((rows, width), dtyp...  4.49 us
    pallas_call x1, Pallas kernels, pack(): pl.pallas_call(kernel, out_shape=jax.ShapeDtypeStruct((replicas, capacity...  4.26 us
    all_to_all x1, starting transfers between devices, body(): arrived = lax.all_to_all(packed, 'replica', 0, 0)  3.83 us
    ppermute x2, waiting for transfers between devices, body(): swapped = [lax.ppermute(p, 'tensor', swap) for p in (parts[0], parts[2])]  3.08 us
  transfers between devices with their start and end apart: 10, of which 5 were waited for; matrix products, arithmetic and copies ran while one was open for 8% of the time, Pallas kernels for 28%

profile of v6, /device:TPU:0, one launch (start us, length us, event | category | flops | bytes accessed | tf_op | source)
XLA Modules:
  0.0 99.8 jit_solution(11080346957543514767)
XLA Ops:
  0.0 0.9 select_reduce_fusion.rows_ref
  0.9 5.1 %collective-permute-start.2 = (s32[16]{0:T(128)S(1)}, s32[16]{0:T(128)S(1)}, u32[]{:S(2)}, u32[]{:S(2)}) collective-permute-start(s32[16]{0:T(128)S(1)} %select_reduce_fusion.rows_ref), channel_id=1, source_target_pairs={{0,12},{4,8},{8,4},{12,0},{1,13},{5,9},{9,5},{13,1},{2,14},{6,10},... | collective-permute-start | bytes 200 | tf_op jit(solution)/shard_map/ppermute | solution.py:413
  6.0 0.0 collective-permute-start.1
  6.0 0.6 collective-permute-start
  6.6 1.7 %copy_bitcast_fusion.1 = (bf16[2,128,256]{2,1,0:T(8,128)(2,1)}, bf16[2,128,256]{2,1,0:T(8,128)(2,1)}) fusion(bf16[128,2,256]{2,1,0:T(2,128)(2,1)} %param.12, bf16[128,2,256]{2,1,0:T(2,128)(2,1)} %param.11), kind=kLoop, calls=%fused_computation.2 | loop fusion | bytes 524288 | tf_op jit(solution)/shard_map/transpose | solution.py:428
  8.3 0.0 collective-permute-done.2
  8.3 2.1 %collective-permute-done.1 = s32[16]{0:T(128)S(1)} collective-permute-done((s32[16]{0:T(128)S(1)}, s32[16]{0:T(128)S(1)}, u32[]{:S(2)}, u32[]{:S(2)}) %collective-permute-start.1) | collective-permute-done | bytes 96 | tf_op jit(solution)/shard_map/ppermute | solution.py:413
  10.4 0.0 collective-permute-done
  10.4 0.6 pad_add_fusion.rows_ref
  11.0 4.3 %pack.1 = bf16[4,8,16,3072]{3,2,1,0:T(8,128)(2,1)} custom-call(s32[4,16]{1,0:T(4,128)} %pad_add_fusion.rows_ref, s32[1]{0:T(128)} %bitcast.8.place_ref, bf16[16,16,2048]{2,1,0:T(8,128)(2,1)} %refs_0_.1, bf16[16,16,1024]{2,1,0:T(8,128)(2,1)} %refs_1_.1), custom_call_target="tpu_custom_call" | custom-call | tf_op jit(solution)/shard_map/pack/pallas_call | solution.py:229
  15.3 0.0 copy-start.2
  15.3 3.8 %all-to-all-start = ((bf16[4,8,16,3072]{3,2,1,0:T(8,128)(2,1)}), bf16[4,8,16,3072]{3,2,1,0:T(8,128)(2,1)S(1)}, u32[]{:S(2)}, u32[]{:S(2)}) async-start(bf16[4,8,16,3072]{3,2,1,0:T(8,128)(2,1)} %pack.1), calls=%async_computation | async-start | bytes 6291456 | tf_op jit(solution)/shard_map/all_to_all | solution.py:418
  19.1 0.0 copy-done.2
  19.2 2.0 %copy.25 = bf16[128,2,1024]{2,0,1:T(8,128)(2,1)} copy(bf16[128,2,1024]{2,1,0:T(2,128)(2,1)} %param.10) | data formatting | bytes 1048576 | tf_op args[0]
  21.2 0.8 copy.21.lens_ref
  21.9 0.6 pad_add_fusion.2.groups_ref
  22.6 21.3 %attention.1 = (bf16[256,1024]{1,0:T(8,128)(2,1)}, bf16[256,2048]{1,0:T(8,128)(2,1)}, bf16[256,2048]{1,0:T(8,128)(2,1)}, bf16[256,2048]{1,0:T(8,128)(2,1)}) custom-call(s32[3]{0:T(128)} %pad_add_fusion.2.groups_ref, bf16[2,128,1024]{2,1,0:T(8,128)(2,1)} %bitcast.18, bf16[2,128,256]{2,1,0:T(8,128)(2,1)} %get-tuple-element.20.rk_ref, ...), custom_call_target="tpu_custom_call" | custom-call | flops 20000000000 | bytes 6291456 | tf_op jit(solution)/shard_map/attention/pallas_call | solution.py:147
  43.9 0.1 collective-permute-start.3
  44.0 0.5 collective-permute-start.4
  44.5 3.1 %collective-permute-done.3 = bf16[256,2048]{1,0:T(8,128)(2,1)S(1)} collective-permute-done((bf16[256,2048]{1,0:T(8,128)(2,1)}, bf16[256,2048]{1,0:T(8,128)(2,1)S(1)}, u32[]{:S(2)}, u32[]{:S(2)}) %collective-permute-start.3) | collective-permute-done | bytes 1048608 | tf_op jit(solution)/shard_map/ppermute | solution.py:440
  47.6 2.5 %add_convert_fusion = bf16[256,2048]{1,0:T(8,128)(2,1)} fusion(bf16[256,2048]{1,0:T(8,128)(2,1)S(1)} %collective-permute-done.3, bf16[256,2048]{1,0:T(8,128)(2,1)} %get-tuple-element.14), kind=kLoop, calls=%fused_computation | loop fusion | flops 2097152 | bytes 3145728 | tf_op jit(solution)/shard_map/convert_element_type | solution.py:448
  50.1 1.5 %collective-permute-start.5 = (bf16[256,2048]{1,0:T(8,128)(2,1)}, bf16[256,2048]{1,0:T(8,128)(2,1)}, u32[]{:S(2)}, u32[]{:S(2)}) collective-permute-start(bf16[256,2048]{1,0:T(8,128)(2,1)} %add_convert_fusion), channel_id=1, source_target_pairs={{0,2},{1,3},{2,0},{3,1},{4,6},{5,7},{6,4},{7,5},{8,10},{9,11},{10,... | collective-permute-start | bytes 3145736 | tf_op jit(solution)/shard_map/ppermute | solution.py:449
  51.6 0.0 collective-permute-done.4.rest_0_
  51.6 24.0 %collective-permute-done.5.rest_1_ = bf16[256,2048]{1,0:T(8,128)(2,1)} collective-permute-done((bf16[256,2048]{1,0:T(8,128)(2,1)}, bf16[256,2048]{1,0:T(8,128)(2,1)}, u32[]{:S(2)}, u32[]{:S(2)}) %collective-permute-start.5) | collective-permute-done | bytes 1048608 | tf_op jit(solution)/shard_map/ppermute | solution.py:449
  75.6 4.5 %project.1.base_ref = bf16[256,2048]{1,0:T(8,128)(2,1)} custom-call(s32[1]{0:T(128)} %bitcast.group_ref, bf16[256,1024]{1,0:T(8,128)(2,1)} %get-tuple-element.18.a_ref, bf16[1024,8192]{1,0:T(8,128)(2,1)} %w_ref.3, bf16[256,2048]{1,0:T(8,128)(2,1)} %collective-permute-done.4.rest_0_, bf16[256,2048]{1,0:T(8,128)(2,1)} %collective-permute-done.5.rest_1_), custom_call_target="tpu_custom_call" | custom-call | flops 1073741824 | bytes 4194304 | tf_op jit(solution)/shard_map/project/pallas_call | solution.py:188
  80.1 8.5 %all-to-all-done.arrived_ref = bf16[4,8,16,3072]{3,2,1,0:T(8,128)(2,1)S(1)} async-done(((bf16[4,8,16,3072]{3,2,1,0:T(8,128)(2,1)}), bf16[4,8,16,3072]{3,2,1,0:T(8,128)(2,1)S(1)}, u32[]{:S(2)}, u32[]{:S(2)}) %all-to-all-start) | async-done | bytes 3145760 | tf_op jit(solution)/shard_map/all_to_all | solution.py:418
  88.6 0.0 copy-start.1
  88.6 1.0 %copy-done.1 = bf16[256,1024]{1,0:T(8,128)(2,1)S(1)} copy-done((bf16[256,1024]{1,0:T(8,128)(2,1)S(1)}, bf16[256,1024]{1,0:T(8,128)(2,1)}, u32[]{:S(2)}) %copy-start.1) | copy-done | bytes 524312
  89.6 0.0 copy-start
  89.6 2.9 %low_rank.1.rest_0_ = f32[16,256]{1,0:T(8,128)S(1)} custom-call(s32[16]{0:T(128)S(1)} %select_reduce_fusion.rows_ref, bf16[256,1024]{1,0:T(8,128)(2,1)S(1)} %copy-done.1, bf16[4,8,16,3072]{3,2,1,0:T(8,128)(2,1)S(1)} %all-to-all-done.arrived_ref), custom_call_target="tpu_custom_call" | custom-call | tf_op jit(solution)/shard_map/low_rank/pallas_call | solution.py:305
  92.6 0.1 collective-permute-start.6
  92.7 1.6 %collective-permute-start.7 = (f32[16,256]{1,0:T(8,128)S(1)}, f32[16,256]{1,0:T(8,128)S(1)}, u32[]{:S(2)}, u32[]{:S(2)}) collective-permute-start(f32[16,256]{1,0:T(8,128)S(1)} %low_rank.1.rest_0_), channel_id=1, source_target_pairs={{0,2},{1,3},{2,0},{3,1},{4,6},{5,7},{6,4},{7,5},{8,10},{9,11},{10,... | collective-permute-start | bytes 49160 | tf_op jit(solution)/shard_map/ppermute | solution.py:456
  94.2 0.3 collective-permute-start.8
  94.5 2.4 %chosen.1.up_ref = bf16[16,16,2048]{2,1,0:T(8,128)(2,1)S(1)} custom-call(s32[16]{0:T(128)S(1)} %select_reduce_fusion.rows_ref, bf16[4,8,16,3072]{3,2,1,0:T(8,128)(2,1)S(1)} %all-to-all-done.arrived_ref), custom_call_target="tpu_custom_call" | custom-call | tf_op jit(solution)/shard_map/chosen/pallas_call | solution.py:323
  97.0 0.0 collective-permute-done.6.rest_1_
  97.0 0.0 collective-permute-done.7.rest_2_
  97.0 0.4 collective-permute-done.8.rest_3_
  97.4 0.0 copy-done
  97.4 2.5 %finish.1 = bf16[128,2,2048]{2,1,0:T(2,128)(2,1)} custom-call(bf16[256,2048]{1,0:T(8,128)(2,1)S(1)} %copy-done, bf16[16,16,2048]{2,1,0:T(8,128)(2,1)S(1)} %chosen.1.up_ref, f32[16,256]{1,0:T(8,128)S(1)} %low_rank.1.rest_0_, f32[16,256]{1,0:T(8,128)S(1)} %collective-permute-done.6.rest_1_, f32[16,256]{1,0:T(8,128)S(1)} %collective-permute-done.7.rest_2_, ...), custom_call_target="tpu_custom_call" | custom-call | tf_op jit(solution)/shard_map/finish/pallas_call | solution.py:363
  (1 shorter events, 0.0 us)
Async XLA Ops:
  0.9 7.5 %collective-permute-start.2 = (s32[16]{0:T(128)S(1)}, s32[16]{0:T(128)S(1)}, u32[]{:S(2)}, u32[]{:S(2)}) collective-permute-start(s32[16]{0:T(128)S(1)} %select_reduce_fusion.rows_ref), channel_id=1, source_target_pairs={{0,12},{4,8},{8,4},{12,0},{1,13},{5,9},{9,5},{13,1},{2,14},{6,10},... | collective-permute-start | bytes 200 | tf_op jit(solution)/shard_map/ppermute | solution.py:413
  6.0 4.4 %collective-permute-start.1 = (s32[16]{0:T(128)S(1)}, s32[16]{0:T(128)S(1)}, u32[]{:S(2)}, u32[]{:S(2)}) collective-permute-start(s32[16]{0:T(128)S(1)} %select_reduce_fusion.rows_ref), channel_id=1, source_target_pairs={{0,8},{4,12},{8,0},{12,4},{1,9},{5,13},{9,1},{13,5},{2,10},{6,14},... | collective-permute-start | bytes 200 | tf_op jit(solution)/shard_map/ppermute | solution.py:413
  6.0 4.4 %collective-permute-start = (s32[16]{0:T(128)S(1)}, s32[16]{0:T(128)S(1)}, u32[]{:S(2)}, u32[]{:S(2)}) collective-permute-start(s32[16]{0:T(128)S(1)} %select_reduce_fusion.rows_ref), channel_id=1, source_target_pairs={{0,4},{4,0},{8,12},{12,8},{1,5},{5,1},{9,13},{13,9},{2,6},{6,2},{1... | collective-permute-start | bytes 200 | tf_op jit(solution)/shard_map/ppermute | solution.py:413
  15.3 3.8 %copy-start.2 = (s32[128]{0:T(128)S(1)}, s32[128]{0:T(128)}, u32[]{:S(2)}) copy-start(s32[128]{0:T(128)} %param.14) | copy-start | bytes 1540
  15.3 73.3 %all-to-all-start = ((bf16[4,8,16,3072]{3,2,1,0:T(8,128)(2,1)}), bf16[4,8,16,3072]{3,2,1,0:T(8,128)(2,1)S(1)}, u32[]{:S(2)}, u32[]{:S(2)}) async-start(bf16[4,8,16,3072]{3,2,1,0:T(8,128)(2,1)} %pack.1), calls=%async_computation | async-start | bytes 6291456 | tf_op jit(solution)/shard_map/all_to_all | solution.py:418
  43.9 3.7 %collective-permute-start.3 = (bf16[256,2048]{1,0:T(8,128)(2,1)}, bf16[256,2048]{1,0:T(8,128)(2,1)S(1)}, u32[]{:S(2)}, u32[]{:S(2)}) collective-permute-start(bf16[256,2048]{1,0:T(8,128)(2,1)} %get-tuple-element.15), channel_id=1, source_target_pairs={{0,1},{1,0},{2,3},{3,2},{4,5},{5,4},{6,7},{7,6},{8,9},{9,8},{10,11... | collective-permute-start | bytes 3145736 | tf_op jit(solution)/shard_map/ppermute | solution.py:440
  44.0 7.5 %collective-permute-start.4 = (bf16[256,2048]{1,0:T(8,128)(2,1)}, bf16[256,2048]{1,0:T(8,128)(2,1)}, u32[]{:S(2)}, u32[]{:S(2)}) collective-permute-start(bf16[256,2048]{1,0:T(8,128)(2,1)} %get-tuple-element.17), channel_id=1, source_target_pairs={{0,1},{1,0},{2,3},{3,2},{4,5},{5,4},{6,7},{7,6},{8,9},{9,8},{10,11... | collective-permute-start | bytes 3145736 | tf_op jit(solution)/shard_map/ppermute | solution.py:440
  50.1 25.5 %collective-permute-start.5 = (bf16[256,2048]{1,0:T(8,128)(2,1)}, bf16[256,2048]{1,0:T(8,128)(2,1)}, u32[]{:S(2)}, u32[]{:S(2)}) collective-permute-start(bf16[256,2048]{1,0:T(8,128)(2,1)} %add_convert_fusion), channel_id=1, source_target_pairs={{0,2},{1,3},{2,0},{3,1},{4,6},{5,7},{6,4},{7,5},{8,10},{9,11},{10,... | collective-permute-start | bytes 3145736 | tf_op jit(solution)/shard_map/ppermute | solution.py:449
  88.6 1.0 %copy-start.1 = (bf16[256,1024]{1,0:T(8,128)(2,1)S(1)}, bf16[256,1024]{1,0:T(8,128)(2,1)}, u32[]{:S(2)}) copy-start(bf16[256,1024]{1,0:T(8,128)(2,1)} %get-tuple-element.18.a_ref) | copy-start | bytes 1572868
  89.6 7.8 %copy-start = (bf16[256,2048]{1,0:T(8,128)(2,1)S(1)}, bf16[256,2048]{1,0:T(8,128)(2,1)}, u32[]{:S(2)}) copy-start(bf16[256,2048]{1,0:T(8,128)(2,1)} %project.1.base_ref) | copy-start | bytes 3145732
  92.6 4.4 %collective-permute-start.6 = (f32[16,256]{1,0:T(8,128)S(1)}, f32[16,256]{1,0:T(8,128)S(1)}, u32[]{:S(2)}, u32[]{:S(2)}) collective-permute-start(f32[16,256]{1,0:T(8,128)S(1)} %low_rank.1.rest_0_), channel_id=1, source_target_pairs={{0,1},{1,0},{2,3},{3,2},{4,5},{5,4},{6,7},{7,6},{8,9},{9,8},{10,11... | collective-permute-start | bytes 49160 | tf_op jit(solution)/shard_map/ppermute | solution.py:456
  92.7 4.3 %collective-permute-start.7 = (f32[16,256]{1,0:T(8,128)S(1)}, f32[16,256]{1,0:T(8,128)S(1)}, u32[]{:S(2)}, u32[]{:S(2)}) collective-permute-start(f32[16,256]{1,0:T(8,128)S(1)} %low_rank.1.rest_0_), channel_id=1, source_target_pairs={{0,2},{1,3},{2,0},{3,1},{4,6},{5,7},{6,4},{7,5},{8,10},{9,11},{10,... | collective-permute-start | bytes 49160 | tf_op jit(solution)/shard_map/ppermute | solution.py:456
  94.2 3.2 %collective-permute-start.8 = (f32[16,256]{1,0:T(8,128)S(1)}, f32[16,256]{1,0:T(8,128)S(1)}, u32[]{:S(2)}, u32[]{:S(2)}) collective-permute-start(f32[16,256]{1,0:T(8,128)S(1)} %low_rank.1.rest_0_), channel_id=1, source_target_pairs={{0,3},{1,2},{2,1},{3,0},{4,7},{5,6},{6,5},{7,4},{8,11},{9,10},{10,... | collective-permute-start | bytes 49160 | tf_op jit(solution)/shard_map/ppermute | solution.py:456
